TPU v7x, 32 devices: a whole 2x2x4 slice. The times are simulated.
32 devices in a mesh: dp: 8 (over y, x, core), tensor: 4 (over z).
Axes of the slice: x: 2, y: 2, z: 4, core: 2. Of those that a mesh axis runs over, the one named last changes fastest.
Arguments:
- tokens: bfloat16 [64, 256, 768], P('dp'), may hold values from -6 to 6
- lengths: int32 [64], P('dp'), may hold values from 64 to 256, as said below
- adapter_mask: int32 [64], P('dp'), may hold values from 1 to 65535, as said below
- cotangent: bfloat16 [64, 256, 768], P(('dp', 'tensor')), may hold values from -6 to 6
- att_query: bfloat16 [768, 768], P(None, 'tensor'), may hold values from -0.3125 to 0.3125
- att_key: bfloat16 [768, 768], P(None, 'tensor'), may hold values from -0.3125 to 0.3125
- att_value: bfloat16 [768, 768], P(None, 'tensor'), may hold values from -0.21875 to 0.21875
- att_out: bfloat16 [768, 768], P('tensor'), may hold values from -0.875 to 0.875
- norm1_gain: float32 [768], replicated, may hold values from 0.5 to 1.5
- norm1_bias: float32 [768], replicated, may hold values from -1.25 to 1.25
- ffn_in: bfloat16 [768, 3072], P(None, 'tensor'), may hold values from -0.21875 to 0.21875
- ffn_bias: float32 [3072], replicated, may hold values from -1.75 to 1.75
- ffn_out: bfloat16 [3072, 768], P('tensor'), may hold values from -0.109375 to 0.109375
- adapt_down: bfloat16 [768, 768], replicated, may hold values from -0.21875 to 0.21875
- adapt_up: bfloat16 [16, 48, 768], replicated, may hold values from -1.5 to 1.5
- norm2_gain: float32 [768], replicated, may hold values from 0.5 to 1.5
- norm2_bias: float32 [768], replicated, may hold values from -1.25 to 1.25
- joining_query: bfloat16 [768, 768], P(('dp', 'tensor')), may hold values from -0.4375 to 0.4375
- joining_key: bfloat16 [768, 768], P(('dp', 'tensor')), may hold values from -0.4375 to 0.4375
- joining_value: bfloat16 [768, 768], P(('dp', 'tensor')), may hold values from -0.21875 to 0.21875
- joining_qbias: bfloat16 [768], P(('dp', 'tensor')), may hold values from -1.75 to 1.75
- joining_vbias: bfloat16 [768], P(('dp', 'tensor')), may hold values from -1.75 to 1.75
Outputs:
- layer_out: bfloat16 [64, 256, 768], P(('dp', 'tensor'))
- input_grad: bfloat16 [64, 256, 768], P(('dp', 'tensor'))
- grad_joining_query: float32 [768, 768], P(('dp', 'tensor'))
- grad_joining_key: float32 [768, 768], P(('dp', 'tensor'))
- grad_joining_value: float32 [768, 768], P(('dp', 'tensor'))
- grad_joining_qbias: float32 [768], P(('dp', 'tensor'))
- grad_joining_vbias: float32 [768], P(('dp', 'tensor'))
Inputs may be any that keep to these rules, and one draw needn't show every extreme that they name: Padding lengths; some sequence is full and some has exactly 64 tokens. `adapter_mask`: bit m (m below 16) tells whether adapter m is available to the sequence; every sequence has one available adapter or more, some sequence all of them, some only adapter 0.
All inputs are finite; a program needn't handle non-finite values.
Results may differ from a plain program's by a relative error of at most 0.039.
Values may be sent and summed in bfloat16 or wider, within the bound.
No kernel may reach another device: no remote copies, remote signals or barrier semaphores. Data moves between devices by JAX's collectives and lax.ppermute only.
A program may use at most 256 MiB of HBM per device.

v0:
```python
from functools import partial
import math

import jax
import jax.numpy as jnp
from jax import lax
from jax.experimental import pallas as pl
from jax.experimental.pallas import tpu as pltpu
from jax.sharding import PartitionSpec as P

HEADS = 12
EPS = 1e-05
MASKED = -1e30
ALL = ("dp", "tensor")
BF = jnp.bfloat16
F32 = jnp.float32


def mm(left, right):
    return jnp.dot(left, right, preferred_element_type=F32)


def mm_t(left, right):
    return lax.dot_general(left, right, (((1,), (1,)), ((), ())), preferred_element_type=F32)


def t_mm(left, right):
    return lax.dot_general(left, right, (((0,), (0,)), ((), ())), preferred_element_type=F32)


def norm_parts(values):
    average = jnp.mean(values, axis=-1, keepdims=True)
    centered = values - average
    variance = jnp.mean(centered * centered, axis=-1, keepdims=True)
    rstd = lax.rsqrt(variance + EPS)
    return centered * rstd, rstd


def norm_back(grad, gain, xhat, rstd):
    scaled = grad * gain
    return rstd * (
        scaled
        - jnp.mean(scaled, axis=-1, keepdims=True)
        - xhat * jnp.mean(scaled * xhat, axis=-1, keepdims=True)
    )


def gelu_parts(pre):
    cdf = 0.5 * (1.0 + lax.erf(pre * (1.0 / math.sqrt(2.0))))
    pdf = jnp.exp(-0.5 * pre * pre) * (1.0 / math.sqrt(2.0 * math.pi))
    return pre * cdf, cdf + pre * pdf


def limit(mebibytes):
    return pltpu.CompilerParams(vmem_limit_bytes=mebibytes * 2**20)


VMEM = pl.BlockSpec(memory_space=pltpu.VMEM)
SMEM = pl.BlockSpec(memory_space=pltpu.SMEM)
LITTLE = limit(24)
FAR_XY = [(i, i ^ 6) for i in range(8)]
CORE = [(i, i ^ 1) for i in range(8)]
ALONG_X = [(i, i ^ 2) for i in range(8)]
ALONG_Y = [(i, i ^ 4) for i in range(8)]
SPLIT_XY = [(i, i ^ (4 if i & 1 else 2)) for i in range(8)]
CROSS_XY = [(i, i ^ (3 if i & 1 else 5)) for i in range(8)]


def send(array, pairs):
    return lax.ppermute(array, "dp", pairs)


def shift(array, by, groups):
    return lax.ppermute(array, "tensor", [(i, (i + by) % groups) for i in range(groups)])


def scoped(name, step, *args):
    with jax.named_scope(name):
        return step(*args)


def tie(array, *others):
    return lax.optimization_barrier((array,) + others)[0]


def fetch_blocks(spots_ref, sources, stage_ref, sem):
    if len(sources) == 1:
        pltpu.make_async_copy(sources[0], stage_ref, sem).start()
        return
    planes = planes_in_order(spots_ref)
    for k, (ref, first) in enumerate(views(sources)):
        for i, plane in enumerate(planes[1:] + planes[:1]):
            pltpu.make_async_copy(ref.at[first + i], stage_ref.at[spots_ref[k] * len(planes) + plane], sem).start()


def order_rows(stage_ref, join_ref, biases_ref):
    blocks = stage_ref.shape[0]
    rows = join_ref.shape[1] // blocks
    total = 0.0
    for b in range(0, blocks, 2):
        pair = [stage_ref[b + i].astype(F32) for i in range(2)]
        for m in range(3):
            both = jnp.concatenate([block[m * rows : (m + 1) * rows] for block in pair], axis=0)
            join_ref[m, b * rows : (b + 2) * rows, :] = both.astype(BF)
        total = total + pair[0][3 * rows :] + pair[1][3 * rows :]
    biases_ref[...] = total


def fetch(spots_ref, sources, out_ref, sems, which, side_by_side=False):
    planes = planes_in_order(spots_ref)
    dim = sources[-1].shape[-1]
    rows = sources[-1].shape[-2]

    def copy(source, r, at):
        if side_by_side:
            target = out_ref.at[at, pl.ds(r * dim, dim)]
        else:
            target = out_ref.at[pl.ds(r * rows + at.start, at.size)]
        pltpu.make_async_copy(source, target, sems.at[r]).start()

    for r in which:
        if len(sources) == 1:
            copy(sources[0].at[planes[r]], r, pl.ds(0, rows))
        elif r == 0:
            copy(sources[-1], r, pl.ds(0, rows))
        else:
            for k, (ref, first) in enumerate(views(sources[:-1])):
                part = ref.shape[1]
                copy(ref.at[first + r - 1], r, pl.ds(pl.multiple_of(spots_ref[k] * part, part), part))


def arrive(out_ref, sems, r, side_by_side=False):
    dim = out_ref.shape[0] if side_by_side else out_ref.shape[1]
    block = out_ref.at[:, pl.ds(r * dim, dim)] if side_by_side else out_ref.at[pl.ds(r * out_ref.shape[0] // 4, out_ref.shape[0] // 4)]
    pltpu.make_async_copy(block, block, sems.at[r]).wait()


def fetch_stacked(spots_ref, sources, out_ref, sems, last):
    groups, dim = out_ref.shape[0], out_ref.shape[1]
    chosen = range(groups - 1, groups) if last else range(groups - 1)
    if len(sources) == 1:
        for m in chosen:
            pltpu.make_async_copy(sources[0].at[m], out_ref.at[m], sems.at[m]).start()
        return
    own = sources[-groups:]
    pieces = views(sources[:-groups])
    width, rows = dim // groups, pieces[0][0].shape[1]
    per = width // rows
    my_z = spots_ref[8]
    for m in chosen:
        at = pl.ds(pl.multiple_of(my_z * width, width), width)
        pltpu.make_async_copy(own[m], out_ref.at[m, at], sems.at[m]).start()
    for k, (ref, first) in enumerate(pieces):
        e = spots_ref[k]
        m = lax.div(e, per)

        @pl.when((m == groups - 1) == last)
        def _():
            for i, plane in enumerate(planes_in_order(spots_ref)[1:]):
                at = pl.ds(pl.multiple_of(plane * width + lax.rem(e, per) * rows, rows), rows)
                pltpu.make_async_copy(ref.at[first + i], out_ref.at[m, at], sems.at[m]).start()


def arrive_stacked(out_ref, sems, m):
    pltpu.make_async_copy(out_ref.at[m], out_ref.at[m], sems.at[m]).wait()


def views(sources):
    if len(sources) == 8:
        return [(source, 0) for source in sources]
    both, near, far, swapped, swapped_far = sources
    count = far.shape[0]
    return [(both, 0), (both, count), (near, 0), (near, count), (far, 0), (swapped, 0), (swapped, count), (swapped_far, 0)]


def cut_kernel(spots_ref, *refs):
    count = (len(refs) - 1) // 3
    shards, outs, sems = refs[:count], refs[count:-1], refs[-1]
    pairs = []
    for i, shard in enumerate(shards):
        rows = outs[2 * i].shape[0]
        at = pl.ds(pl.multiple_of(lax.div(spots_ref[0], 2) * rows, rows), rows)
        pairs.append((shard.at[at], outs[2 * i]))
        at = pl.ds(pl.multiple_of(spots_ref[0] * (rows // 2), rows // 2), rows // 2)
        pairs.append((shard.at[at], outs[2 * i + 1]))
    for copy in begin(pairs, sems):
        copy.wait()


def cut(spots, shards):
    outs = []
    for shard in shards:
        rows, dim = shard.shape
        outs += [jax.ShapeDtypeStruct((rows // 4, dim), BF), jax.ShapeDtypeStruct((rows // 8, dim), BF)]
    return pl.pallas_call(
        cut_kernel,
        out_shape=outs,
        in_specs=[SMEM] + [ANY] * len(shards),
        out_specs=[VMEM] * len(outs),
        scratch_shapes=[pltpu.SemaphoreType.DMA((len(outs),))],
        compiler_params=limit(60),
    )(spots, *shards)


def merge_kernel(spots_ref, *refs, count):
    beside, across, beside2, across2, *own = refs[:count]
    outs = refs[count:]
    core = lax.rem(spots_ref[0], 2)
    rows = across.shape[0]
    blocks = 3 + len(own) // 2
    sides = [outs[0], outs[1]] if len(outs) == 2 else [outs[0].at[pl.ds(i * blocks, blocks)] for i in range(2)]
    parts = [pl.ds(pl.multiple_of(at * rows, rows), rows) for at in (core, 1 - core)]
    for side, at, last, mine in zip(sides, parts, (across, across2), own or (None, None)):
        side[core] = beside[at, :]
        side[1 - core] = beside2[at, :]
        side[2] = last[...]
        if mine is not None:
            side[3] = mine[...]


def merge(spots, arrays, split):
    rows, dim = arrays[1].shape
    blocks = 3 + (len(arrays) - 4) // 2
    outs = [blocks, blocks] if split else [2 * blocks]
    return pl.pallas_call(
        partial(merge_kernel, count=len(arrays)),
        out_shape=[jax.ShapeDtypeStruct((out, rows, dim), BF) for out in outs],
        in_specs=[SMEM] + [VMEM] * len(arrays),
        out_specs=[VMEM] * len(outs),
        compiler_params=limit(8),
    )(spots, *arrays)


def planes_in_order(spots_ref, groups=4):
    return [lax.rem(spots_ref[8] + step, groups) for step in (0, 1, groups - 1, 2)]


def begin(pairs, sems):
    copies = [pltpu.make_async_copy(source, target, sems.at[i]) for i, (source, target) in enumerate(pairs)]
    for one in copies:
        one.start()
    return copies


WEIGHT_SEMS = pltpu.SemaphoreType.DMA((4,))
ANY = pl.BlockSpec(memory_space=pltpu.HBM)


class Gather:
    def __init__(self, dp_size, groups, my_d, my_z, seqs):
        self.dp_size, self.groups, self.my_d, self.my_z = dp_size, groups, my_d, my_z
        self.paired = dp_size == 8 and groups == 4 and seqs == 2
        core = lax.rem(my_d, 2)
        even = [0, 1, 2, 3, 7, 5, 4, 6]
        odd = [0, 1, 4, 5, 7, 3, 2, 6]
        flips = jnp.where(core == 0, jnp.array(even, jnp.int32), jnp.array(odd, jnp.int32))
        self.spots = jnp.concatenate([jnp.bitwise_xor(my_d, flips), my_z[None]]).astype(jnp.int32)

    def all_parts(self, part):
        whole = lax.all_gather(part, ("dp", "tensor"), axis=0)
        return whole.reshape((self.dp_size, self.groups) + part.shape).transpose(1, 0, 2, 3)

    def part_of(self, shard):
        rows = shard.shape[0] // self.dp_size
        return lax.dynamic_slice_in_dim(shard, self.my_d * rows, rows, 0)

    def all_rounds(self, parts, early, steps):
        count = len(parts)
        gathered, spread = [], []
        ahead, done = self.planes(parts[0], 0), [rows for part in parts[1:] for rows in part[:2]] + early
        for r in range(count + 2):
            with jax.named_scope("round%d" % r):
                ready = list(lax.optimization_barrier((*ahead, *done)))
                ahead = ready[: len(ahead)]
                if r >= 1:
                    at = len(ahead)
                    if r <= count:
                        last = spread[r - 1]
                        last[1] = ready[at : at + len(last[1])]
                        at += len(last[1])
                    if 2 <= r <= count:
                        spread[r - 2][2] = ready[at]
                done = []
                if 1 <= r < count:
                    near_half = last[1][0] if len(last[1]) == 2 else last[1][0][: last[1][0].shape[0] // 2]
                    last.append(scoped("far", send, near_half, CROSS_XY))
                if r < count:
                    beside, across = ahead
                    ahead = []
                    if r + 1 < count:
                        ahead = self.planes([tie(rows, beside) for rows in parts[r + 1]], r + 1)
                    others = [scoped("others", send, beside, CORE), scoped("others", send, across, CORE)]
                    both = merge(self.spots, [beside, across, *others, *parts[r][2:]], r == count - 1)
                    near = [scoped("near", send, side, SPLIT_XY) for side in both]
                    spread.append([both, near])
                    done += near
                else:
                    ahead = []
                if 1 <= r <= count:
                    late = last[2:] if r == count else []
                    last.append([scoped("swap", send, array, CORE) for array in last[1][:-1]])
                    last[3].append(scoped("swap", send, tie(last[1][-1], *late), CORE))
                    done += (last[2:3] if r < count else []) + last[3]
                if r >= 2:
                    whole = spread[r - 2]
                    gathered.append([*whole[0], *whole[1], whole[2], *whole[3], scoped("swapfar", send, whole[2], CORE)])
                done += steps[r](gathered)
                if r == count - 1:
                    spread[r].append(scoped("far", send, tie(near[0], *done[len(near) :]), CROSS_XY))
        return gathered

    def planes(self, part, r):
        with jax.named_scope("planes%d" % r):
            groups = self.groups
            pairs = [
                (d * groups + z, d * groups + (z + (1 if d & 1 else groups - 1)) % groups)
                for d in range(self.dp_size)
                for z in range(groups)
            ]
            beside = scoped("beside", lax.ppermute, part[1], ("dp", "tensor"), pairs)
            return beside, scoped("across", shift, part[0], 2, groups)

    def half_of(self, quarter):
        rows = quarter.shape[0] // 2
        return jnp.where(lax.rem(self.my_d, 2) == 0, quarter[:rows], quarter[rows:])

    def quarter_of(self, shard):
        rows = 2 * shard.shape[0] // self.dp_size
        return lax.dynamic_slice_in_dim(shard, self.my_d // 2 * rows, rows, 0)

    def whole(self, part, stacked=False):
        whole = self.all_parts(part)
        dim = part.shape[1]
        if stacked:
            whole = whole.reshape(self.groups, 4, -1, dim).transpose(1, 0, 2, 3)
        return [whole.reshape(4, -1, dim)]


def reduce_grads(gather, grads, own_rows, between, at_last):
    groups, spots = gather.groups, gather.spots
    if not gather.paired:
        mats, bias = grads
        mats = lax.psum_scatter(mats, ("dp", "tensor"), scatter_dimension=1, tiled=True)
        middle = between(None)
        return (mats[0], mats[1], mats[2], lax.psum(bias, ("dp", "tensor"))), at_last(None)
    keep, away = grads
    rows, dim = keep.shape[1:]
    low = jax.ShapeDtypeStruct((rows, dim), BF)
    come = scoped("cores", send, away, CORE)
    to_x, to_y, to_far = pl.pallas_call(
        add_cores_kernel,
        out_shape=[low, low, low],
        in_specs=[SMEM, ANY, ANY],
        out_specs=[ANY] * 3,
        scratch_shapes=[pltpu.VMEM((3, rows, dim), BF)] * 3 + [pltpu.SemaphoreType.DMA((6,)), pltpu.SemaphoreType.DMA((3,))],
        compiler_params=limit(60),
    )(spots, keep, come)
    from_far = scoped("far", send, to_far, FAR_XY)
    from_x = scoped("x", send, to_x, ALONG_X)
    from_y = scoped("y", send, to_y, ALONG_Y)
    block = jax.ShapeDtypeStruct((3 * own_rows + 8, dim), BF)
    middle = between(to_far)
    mine, *goes = pl.pallas_call(
        add_plane_kernel,
        out_shape=[jax.ShapeDtypeStruct((3 * own_rows + 8, dim), F32)] + [block] * (groups - 1),
        in_specs=[SMEM] + [ANY] * 5,
        out_specs=[VMEM] * groups,
        scratch_shapes=[pltpu.VMEM((rows - 16, dim), F32), pltpu.VMEM((5, rows, dim), BF), pltpu.SemaphoreType.DMA((5,))],
        compiler_params=limit(60),
    )(spots, from_x, from_y, from_far, tie(keep, middle), come)
    after = at_last(mine)
    comes = [scoped("stack%d" % i, shift, go, i + 1, groups) for i, go in enumerate(goes)]
    part = jax.ShapeDtypeStruct((own_rows, dim), F32)
    sums = pl.pallas_call(
        add_stack_kernel,
        out_shape=[part, part, part, jax.ShapeDtypeStruct((8, dim), F32)],
        in_specs=[VMEM] * groups,
        out_specs=[VMEM] * 4,
        compiler_params=LITTLE,
    )(mine, *comes)
    return sums, after


def cost(flops, moved, exps=0):
    return pl.CostEstimate(flops=int(flops), bytes_accessed=int(moved), transcendentals=int(exps))


def head_masks():
    lane = lax.broadcasted_iota(jnp.int32, (1, 128), 1)
    first = (lane < 64).astype(F32)
    return [first.astype(BF), (1.0 - first).astype(BF)], lane < 64


def attention_kernel(spots_ref, len_ref, x_ref, norms_ref, *refs):
    *sources, q_hbm, k_hbm, v_hbm, p_hbm, low_ref, xhat_hbm, rstd_ref, w_ref, ctx_ref, q_ref, k_ref, v_ref, p_ref, xhat_ref, sems, store_sems = refs
    fetch_stacked(spots_ref, sources, w_ref, sems, False)
    fetch_stacked(spots_ref, sources, w_ref, sems, True)
    rows, dim = x_ref.shape
    for m in range(4):
        arrive_stacked(w_ref, sems, m)
    seq_len = p_ref.shape[1]
    x = x_ref[...]
    q_ref[...] = (mm_t(x, w_ref[0]).astype(BF).astype(F32) * (1.0 / math.sqrt(dim // HEADS))).astype(BF)
    k_ref[...] = mm_t(x, w_ref[1]).astype(BF)
    v_ref[...] = mm_t(x, w_ref[2]).astype(BF)
    stores = begin(((q_ref, q_hbm), (k_ref, k_hbm), (v_ref, v_hbm)), store_sems)
    masks, first = head_masks()
    key_at = lax.broadcasted_iota(jnp.int32, (seq_len, 1), 0)

    for s in range(rows // seq_len):
        at = slice(s * seq_len, (s + 1) * seq_len)
        valid = key_at < len_ref[s]
        for j in range(HEADS // 2):
            cols = slice(128 * j, 128 * (j + 1))
            q, k, v = q_ref[at, cols], k_ref[at, cols], v_ref[at, cols]
            parts = []
            for h in range(2):
                scores = jnp.where(valid, mm_t(k, q * masks[h]), MASKED)
                exps = jnp.exp(scores - jnp.max(scores, axis=0, keepdims=True))
                probs = (exps * (1.0 / jnp.sum(exps, axis=0, keepdims=True))).astype(BF)
                p_ref[s * HEADS + 2 * j + h] = probs
                parts.append(t_mm(probs, v))
            ctx_ref[at, cols] = jnp.where(first, parts[0], parts[1]).astype(BF)
        heads = pl.ds(s * HEADS, HEADS)
        stores += begin(((p_ref.at[heads], p_hbm.at[heads]),), store_sems.at[pl.ds(3 + s, 1)])
    xhat, rstd = norm_parts(x.astype(F32) + mm(ctx_ref[...], w_ref[3]))
    xhat_ref[...] = xhat
    stores += begin(((xhat_ref, xhat_hbm),), store_sems.at[pl.ds(3 + rows // seq_len, 1)])
    rstd_ref[...] = rstd
    low_ref[...] = (xhat * norms_ref[0:1, :] + norms_ref[1:2, :]).astype(BF)
    for store in stores:
        store.wait()


def attention_forward(spots, lengths, x, sources, norms, seq_len):
    rows, dim = x.shape
    seqs = rows // seq_len
    low = jax.ShapeDtypeStruct((rows, dim), BF)
    return pl.pallas_call(
        attention_kernel,
        out_shape=[low, low, low,
                   jax.ShapeDtypeStruct((seqs * HEADS, seq_len, seq_len), BF), low,
                   jax.ShapeDtypeStruct((rows, dim), F32), jax.ShapeDtypeStruct((rows, 1), F32)],
        in_specs=[SMEM] * 2 + [VMEM] * 2 + [ANY] * len(sources),
        out_specs=[ANY] * 4 + [VMEM, ANY, VMEM],
        scratch_shapes=[pltpu.VMEM((4, dim, dim), BF)] + [pltpu.VMEM((rows, dim), BF)] * 4 + [
            pltpu.VMEM((seqs * HEADS, seq_len, seq_len), BF), pltpu.VMEM((rows, dim), F32),
            WEIGHT_SEMS, pltpu.SemaphoreType.DMA((4 + seqs,)),
        ],
        compiler_params=limit(60),
        cost_estimate=cost(2 * rows * dim * (4 * dim + 2 * seq_len), 2 * (4 * dim * dim + 8 * rows * dim), rows * seq_len * HEADS),
    )(spots, lengths, x, norms, *sources)


def by_rows(rows, step, work, unroll=1):
    work(slice(0, rows))


def ffn_in_kernel(spots_ref, x_ref, bias_ref, *refs):
    *sources, act_hbm, slope_hbm, act_ref, slope_ref, w_ref, pre_ref, sems, store_sems = refs
    units = pre_ref.shape[1]
    order = planes_in_order(spots_ref)
    stores = []
    fetch(spots_ref, sources, w_ref, sems, [0, 1])
    for r in range(4):
        fetch(spots_ref, sources, w_ref, sems, [r + 2] if r < 2 else [])
        arrive(w_ref, sems, r)
        pre_ref[...] = mm(x_ref[...], w_ref[r * x_ref.shape[1] : (r + 1) * x_ref.shape[1], :])
        cols = slice(r * units, (r + 1) * units)
        act, slope = gelu_parts(pre_ref[...] + bias_ref[order[r]])
        act_ref[:, cols] = act.astype(BF)
        slope_ref[:, cols] = slope.astype(BF)
        pairs = [(act_ref, act_hbm), (slope_ref, slope_hbm)]
        stores += begin([(ref.at[:, cols], hbm.at[:, cols]) for ref, hbm in pairs], store_sems.at[pl.ds(2 * r, 2)])
    for store in stores:
        store.wait()


def ffn_forward(spots, x, sources, bias, units):
    rows, dim = x.shape
    planes = bias.shape[0] // units
    out = jax.ShapeDtypeStruct((rows, planes * units), BF)
    return pl.pallas_call(
        ffn_in_kernel,
        out_shape=[out, out],
        in_specs=[SMEM] + [VMEM] * 2 + [ANY] * len(sources),
        out_specs=[ANY] * 2,
        scratch_shapes=[
            pltpu.VMEM((rows, planes * units), BF), pltpu.VMEM((rows, planes * units), BF),
            pltpu.VMEM((planes * dim, units), BF), pltpu.VMEM((rows, units), F32), WEIGHT_SEMS, pltpu.SemaphoreType.DMA((8,)),
        ],
        compiler_params=limit(60),
        cost_estimate=cost(2 * rows * dim * units * planes, 2 * planes * units * (dim + 2 * rows), 2 * rows * units * planes),
    )(spots, x, bias.reshape(planes, 1, units), *sources)


def two_pass(values, table):
    high = values.astype(BF)
    return mm(high, table) + mm((values - high.astype(F32)).astype(BF), table)


def put_rows(ref, mats, bias):
    at = 0
    for mat in mats:
        ref[at : at + mat.shape[0], :] = mat.astype(BF)
        at += mat.shape[0]
    high = bias.astype(BF).astype(F32)
    ref[at : at + 16, :] = jnp.concatenate([high, bias - high], axis=0).astype(BF)


def sum_rows(arrays):
    total = arrays[0].astype(F32)
    for array in arrays[1:]:
        total = total + array.astype(F32)
    rows = total.shape[0] - 16
    return total[:rows], total[rows : rows + 8] + total[rows + 8 :]


def add_cores_kernel(spots_ref, keep_hbm, come_hbm, *refs):
    hbm, (sums_ref, keep_ref, come_ref, sems, store_sems) = refs[:3], refs[3:]
    quarter = lax.div(spots_ref[0], 2)
    pairs = []
    for i in range(3):
        q = jnp.bitwise_xor(quarter, i + 1)
        pairs += [(keep_hbm.at[q], keep_ref.at[i]), (come_hbm.at[q], come_ref.at[i])]
    copies = begin(pairs, sems)
    stores = []
    for i in range(3):
        copies[2 * i].wait()
        copies[2 * i + 1].wait()
        mats, bias = sum_rows([keep_ref[i], come_ref[i]])
        put_rows(sums_ref.at[i], [mats], bias)
        stores += begin(((sums_ref.at[i], hbm[i]),), store_sems.at[pl.ds(i, 1)])
    for store in stores:
        store.wait()


def fold_bias(bias):
    high = bias.astype(BF).astype(F32)
    row = lax.broadcasted_iota(jnp.int32, (8, 1), 0)
    return jnp.where(row < 4, high, pltpu.roll(bias - high, 4, 0))


def add_plane_kernel(spots_ref, *refs):
    parts, refs = refs[:3], refs[3:]
    keep_hbm, come_hbm, mine_ref, *go_refs, total_ref, arrays_ref, sems = refs
    quarter = lax.div(spots_ref[0], 2)
    sources = (keep_hbm.at[quarter], come_hbm.at[quarter], *parts)
    for copy in begin([(source, arrays_ref.at[i]) for i, source in enumerate(sources)], sems):
        copy.wait()
    total_ref[...], bias = sum_rows([arrays_ref[i] for i in range(5)])
    groups = len(go_refs) + 1
    width = total_ref.shape[0] // 3
    rows = width // groups

    def block(plane):
        at = [pl.multiple_of(i * width + plane * rows, 8) for i in range(3)]
        return jnp.concatenate([total_ref[pl.ds(a, rows), :] for a in at], axis=0)

    my_z = spots_ref[8]
    mine_ref[...] = jnp.concatenate([block(my_z), bias], axis=0)
    folded = fold_bias(bias)
    for i, ref in enumerate(go_refs):
        ref[...] = jnp.concatenate([block(lax.rem(my_z + i + 1, groups)), folded], axis=0).astype(BF)


def add_stack_kernel(mine_ref, *refs):
    come_refs, (q_ref, k_ref, v_ref, bias_ref) = refs[:-4], refs[-4:]
    total = mine_ref[...]
    rows = q_ref.shape[0]
    for ref in come_refs:
        come = ref[...].astype(F32)
        bias = come[3 * rows :]
        total = total + jnp.concatenate([come[: 3 * rows], bias + pltpu.roll(bias, 4, 0)], axis=0)
    q_ref[...], k_ref[...], v_ref[...] = (total[i * rows : (i + 1) * rows] for i in range(3))
    bias_ref[...] = total[3 * rows :]


def joining_kernel(
    spots_ref, member_ref, member_t_ref, avail_ref, norms_ref, act_hbm, xhat1_hbm, cot_hbm, *refs, halves, count
):
    gain1, bias1, gain2, bias2 = (norms_ref[i : i + 1, :] for i in range(4))
    down_hbm, up_hbm, *refs = refs
    join_sources, sources, refs = refs[:count], refs[count:-38], refs[-38:]
    stage_ref, biases_ref, stage_sem, refs = refs[-3], refs[-2], refs[-1], refs[:-3]
    out_hbm, g2_hbm, g_ffn_ref, grad_hbm0, grad_hbm1 = refs[:5]
    act_ref, w_out_ref, down_ref, up_ref, join_ref, xhat1_ref, cot_ref, act_sems, out_sems, sems, store_sems = refs[5:16]
    ffn_ref, u_ref, w_ref, big_u_ref, big_w_ref, p_wide_ref, sums_ref = refs[16:23]
    x_ref, act2_ref, slope_ref, q_ref, gq_ref, low_ref, mixed_ref, t_ref = refs[23:31]
    out_ref, g2_ref, bias_rows_ref, bias_ref = refs[31:35]
    rows, dim = out_ref.shape
    units = w_out_ref.shape[0] // 4
    seqs = avail_ref.shape[0]
    per = rows // seqs
    everyone = [slice(i * per, (i + 1) * per) for i in range(seqs)]
    fscale = 1.0 / math.sqrt(dim)
    member, member_t = member_ref[...], member_t_ref[...]
    loads = []

    def issue(r):
        if r < 4:
            fetch(spots_ref, sources, w_out_ref, out_sems, [r])
            cols = pl.ds(r * units, units)
            loads.extend(begin(((act_hbm.at[:, cols], act_ref.at[:, cols]),), act_sems.at[pl.ds(r, 1)]))
        elif r == 4:
            fetch_blocks(spots_ref, join_sources, stage_ref, stage_sem)
        elif r == 5:
            pairs = ((down_hbm, down_ref), (up_hbm, up_ref), (xhat1_hbm, xhat1_ref), (cot_hbm, cot_ref))
            loads.extend(begin(pairs, sems))

    issue(0)
    issue(1)
    for r in range(4):
        issue(r + 2)
        loads[r].wait()
        arrive(w_out_ref, out_sems, r)
        if r % 2 == 1:
            both = slice((r - 1) * units, (r + 1) * units)
            for at in everyone:
                term = mm(act_ref[at, both], w_out_ref[both, :])
                ffn_ref[at, :] = term if r == 1 else ffn_ref[at, :] + term
    loads = loads[4:]
    for at in everyone:
        x_ref[at, :] = ffn_ref[at, :].astype(BF)
    pltpu.make_async_copy(stage_ref, stage_ref, stage_sem).wait()
    order_rows(stage_ref, join_ref, biases_ref)
    qb, vb = biases_ref[0:1, :], biases_ref[1:2, :]
    for load in loads:
        load.wait()
    up = up_ref[...]
    halves_of = {}

    def narrow(i, name, value=None):
        if value is not None:
            halves_of[i, name] = value
        return halves_of[i, name]

    def per_adapter(values):
        high = values.astype(BF)
        return mm(high, member) + mm((values - high.astype(F32)).astype(BF), member)

    def to_q(i, at):
        q_ref[at, :] = (mm(x_ref[at, :], join_ref[0]) + qb).astype(BF)

    def down(i, at):
        act, slope = gelu_parts(mm(x_ref[at, :], down_ref[...]))
        act2_ref[at, :] = act.astype(BF)
        slope_ref[at, :] = slope.astype(BF)

    def to_u(i, at):
        u = mm_t(q_ref[at, :], join_ref[1])
        u_ref[at, :] = u
        narrow(i, "dot", jnp.sum(ffn_ref[at, :] * u, axis=-1, keepdims=True))

    def scores(i, at):
        big_u = mm_t(u_ref[at, :].astype(BF), up)
        big_u_ref[at, :] = big_u
        fscores = (per_adapter(act2_ref[at, :].astype(F32) * big_u) + narrow(i, "dot")) * fscale
        fscores = jnp.where(avail_ref[i] > 0, fscores, MASKED)
        fexp = jnp.exp(fscores - jnp.max(fscores, axis=-1, keepdims=True))
        narrow(i, "probs", fexp / jnp.sum(fexp, axis=-1, keepdims=True))

    def mix(i, at):
        p_wide = two_pass(narrow(i, "probs"), member_t)
        p_wide_ref[at, :] = p_wide
        weighed = (p_wide * act2_ref[at, :].astype(F32)).astype(BF)
        mixed_ref[at, :] = (ffn_ref[at, :] + mm(weighed, up)).astype(BF)

    def norm(i, at):
        normed1 = xhat1_ref[at, :] * gain1 + bias1
        xhat2, rstd2 = norm_parts(normed1 + mm(mixed_ref[at, :], join_ref[2]) + vb)
        out_ref[at, :] = (xhat2 * gain2 + bias2).astype(BF)
        g2 = norm_back(cot_ref[at, :].astype(F32), gain2, xhat2, rstd2)
        g2_ref[at, :] = g2
        low_ref[at, :] = g2.astype(BF)
        narrow(i, "dot2", jnp.sum(g2 * vb, axis=-1, keepdims=True))
        narrow(i, "d_vb", jnp.sum(g2.reshape(-1, 8, dim), axis=0))

    def to_w(i, at):
        w = mm_t(low_ref[at, :], join_ref[2])
        w_ref[at, :] = w
        narrow(i, "dot2", narrow(i, "dot2") + jnp.sum(ffn_ref[at, :] * w, axis=-1, keepdims=True))

    def score_grads(i, at):
        big_w = mm_t(w_ref[at, :].astype(BF), up)
        big_w_ref[at, :] = big_w
        gvals = per_adapter(act2_ref[at, :].astype(F32) * big_w) + narrow(i, "dot2")
        fprobs = narrow(i, "probs")
        gs = fprobs * (gvals - jnp.sum(gvals * fprobs, axis=-1, keepdims=True)) * fscale
        narrow(i, "gs", gs)
        narrow(i, "gs_sum", jnp.sum(gs, axis=-1, keepdims=True))

    def to_t(i, at):
        wide = two_pass(narrow(i, "gs"), member_t)
        weighed = (wide * act2_ref[at, :].astype(F32)).astype(BF)
        grad = wide * big_u_ref[at, :] + p_wide_ref[at, :] * big_w_ref[at, :]
        slope_ref[at, :] = (grad * slope_ref[at, :].astype(F32)).astype(BF)
        t_ref[at, :] = (mm(weighed, up) + narrow(i, "gs_sum") * ffn_ref[at, :]).astype(BF)

    def to_gq(i, at):
        gq = mm(t_ref[at, :], join_ref[1]).astype(BF)
        gq_ref[at, :] = gq
        narrow(i, "d_qb", jnp.sum(gq.astype(F32).reshape(-1, 8, dim), axis=0))

    def all_halves(*steps):
        for step in steps:
            for i, at in enumerate(everyone):
                step(i, at)

    all_halves(to_q, down, to_u, scores, mix, norm)
    stores = begin(((out_ref, out_hbm), (g2_ref, g2_hbm)), store_sems)
    all_halves(to_w, score_grads)
    sums_ref[2] = t_mm(mixed_ref[...], low_ref[...]).astype(sums_ref.dtype)
    all_halves(to_t)
    sums_ref[1] = t_mm(t_ref[...], q_ref[...]).astype(sums_ref.dtype)
    all_halves(to_gq)
    sums_ref[0] = t_mm(x_ref[...], gq_ref[...]).astype(sums_ref.dtype)
    row = lax.broadcasted_iota(jnp.int32, (8, 1), 0)
    d_qb, d_vb = (
        jnp.sum(sum(narrow(i, name) for i in range(seqs)), axis=0, keepdims=True) for name in ("d_qb", "d_vb")
    )
    bias_ref[...] = jnp.where(row == 0, d_qb, jnp.where(row == 1, d_vb, 0.0))
    if halves:
        core = lax.rem(spots_ref[0], 2)
        part = dim // 8
        put_rows(bias_rows_ref, [], bias_ref[...])
        for hbm, side, sem in ((grad_hbm1, 1 - core, store_sems.at[2]), (grad_hbm0, core, store_sems.at[3])):
            for q in range(4):
                at = pl.ds(pl.multiple_of((2 * q + side) * part, part), part)
                for i in range(3):
                    pltpu.make_async_copy(sums_ref.at[i, at], hbm.at[q, pl.ds(i * part, part)], sem).start()
                pltpu.make_async_copy(bias_rows_ref, hbm.at[q, pl.ds(3 * part, 16)], sem).start()
            stores.append(pltpu.make_async_copy(hbm, hbm, sem))
    else:
        stores += begin(((sums_ref, grad_hbm0), (bias_ref, grad_hbm1)), store_sems.at[pl.ds(2, 2)])
    for i, at in enumerate(everyone):
        total = mm_t(slope_ref[at, :], down_ref[...]) + mm_t(gq_ref[at, :], join_ref[0])
        g_ffn_ref[at, :] = (narrow(i, "gs_sum") * u_ref[at, :] + w_ref[at, :] + total).astype(BF)
    for store in stores:
        store.wait()


def joining(spots, halves, act, sources, adapt_down, up, join_sources, member, member_t, avail, xhat1, norms, cot):
    rows, dim = xhat1.shape
    if halves:
        grads = [jax.ShapeDtypeStruct((4, 3 * dim // 8 + 16, dim), BF)] * 2
    else:
        grads = [jax.ShapeDtypeStruct((3, dim, dim), F32), jax.ShapeDtypeStruct((8, dim), F32)]
    wide, low = pltpu.VMEM((rows, dim), F32), pltpu.VMEM((rows, dim), BF)
    height, blocks = join_sources[-1].shape[-2:][0], 32
    stage_shape = join_sources[0].shape if len(join_sources) == 1 else (blocks, height, dim)
    return pl.pallas_call(
        partial(joining_kernel, halves=halves, count=len(join_sources)),
        out_shape=[
            jax.ShapeDtypeStruct((rows, dim), BF),
            jax.ShapeDtypeStruct((rows, dim), F32),
            jax.ShapeDtypeStruct((rows, dim), BF),
        ] + grads,
        in_specs=[SMEM] + [VMEM] * 4 + [ANY] * (len(sources) + len(join_sources) + 5),
        out_specs=[ANY, ANY, VMEM, ANY, ANY],
        scratch_shapes=[
            pltpu.VMEM(act.shape, BF),
            pltpu.VMEM((act.shape[1], dim), BF),
            pltpu.VMEM(adapt_down.shape, BF),
            pltpu.VMEM(up.shape, BF),
            pltpu.VMEM((3, dim, dim), BF),
            wide,
            low,
            WEIGHT_SEMS,
            WEIGHT_SEMS,
            pltpu.SemaphoreType.DMA((4,)),
            pltpu.SemaphoreType.DMA((4,)),
        ] + [wide] * 6 + [pltpu.VMEM((3, dim, dim), BF if halves else F32)] + [low] * 8 + [
            low,
            wide,
            pltpu.VMEM((16, dim), BF),
            pltpu.VMEM((8, dim), F32),
            pltpu.VMEM(stage_shape, BF),
            pltpu.VMEM((8, dim), F32),
            pltpu.SemaphoreType.DMA,
        ],
        compiler_params=limit(60),
        cost_estimate=cost(2 * rows * dim * (15 * dim + act.shape[1]), 2 * dim * (8 * dim + 10 * rows), 2 * rows * dim),
    )(spots, member, member_t, avail, norms, act, xhat1, cot, adapt_down, up, *join_sources, *sources)


def ffn_back_kernel(spots_ref, g_ref, rstd_ref, norms_ref, slope_hbm, g2_hbm, xhat_hbm, *refs, count):
    refs, (out_sources, in_sources) = refs[sum(count) :], (refs[: count[0]], refs[count[0] : sum(count)])
    g1_hbm, low_hbm, g1_ref, low_ref, slope_ref, g2_ref, xhat_ref, w_out_ref, w_in_ref, pre_ref, out_sems, in_sems, slope_sems, sems, store_sems = refs
    units = w_out_ref.shape[0] // 4
    rows = g_ref.shape[0]
    everyone = [slice(i * rows // 2, (i + 1) * rows // 2) for i in range(2)]
    loads = []

    def issue(r):
        if r < 4:
            fetch(spots_ref, out_sources, w_out_ref, out_sems, [r])
            cols = pl.ds(r * units, units)
            loads.extend(begin(((slope_hbm.at[:, cols], slope_ref.at[:, cols]),), slope_sems.at[pl.ds(r, 1)]))
        elif r < 8:
            fetch(spots_ref, in_sources, w_in_ref, in_sems, [r - 4], side_by_side=True)
        elif r == 8:
            loads.extend(begin(((g2_hbm, g2_ref), (xhat_hbm, xhat_ref)), sems))

    issue(0)
    issue(1)
    for r in range(4):
        issue(r + 2)
        cols = slice(r * units, (r + 1) * units)
        arrive(w_out_ref, out_sems, r)
        loads[r].wait()
        for at in everyone:
            pre_ref[at, cols] = (mm_t(g_ref[at, :], w_out_ref[cols, :]) * slope_ref[at, cols].astype(F32)).astype(BF)
    for r in range(4, 8):
        issue(r + 2)
        arrive(w_in_ref, in_sems, r - 4, side_by_side=True)
        if r == 5:
            both = slice(0, 2 * units)
            for at in everyone:
                g1_ref[at, :] = mm_t(pre_ref[at, both], w_in_ref[:, both])
    for load in loads[4:]:
        load.wait()
    both = slice(2 * units, 4 * units)
    stores = []
    for at in everyone:
        total = mm_t(pre_ref[at, both], w_in_ref[:, both]) + g1_ref[at, :] + g2_ref[at, :]
        g1 = norm_back(total, norms_ref[0:1, :], xhat_ref[at, :], rstd_ref[at, :])
        g1_ref[at, :] = g1
        low_ref[at, :] = g1.astype(BF)
        stores += begin(((g1_ref.at[at], g1_hbm.at[at]), (low_ref.at[at], low_hbm.at[at])), store_sems.at[pl.ds(len(stores), 2)])
    for store in stores:
        store.wait()


def ffn_backward(spots, g_ffn, slope, out_sources, in_sources, g2, xhat, rstd, norms):
    rows, dim = xhat.shape
    planes = 4
    units = slope.shape[1] // planes
    return pl.pallas_call(
        partial(ffn_back_kernel, count=(len(out_sources), len(in_sources))),
        out_shape=[jax.ShapeDtypeStruct((rows, dim), F32), jax.ShapeDtypeStruct((rows, dim), BF)],
        in_specs=[SMEM] + [VMEM] * 3 + [ANY] * (len(out_sources) + len(in_sources) + 3),
        out_specs=[ANY, ANY],
        scratch_shapes=[
            pltpu.VMEM((rows, dim), F32), pltpu.VMEM((rows, dim), BF),
            pltpu.VMEM(slope.shape, BF), pltpu.VMEM((rows, dim), F32), pltpu.VMEM((rows, dim), F32),
            pltpu.VMEM((planes * units, dim), BF), pltpu.VMEM((dim, planes * units), BF), pltpu.VMEM(slope.shape, BF),
            WEIGHT_SEMS, WEIGHT_SEMS, WEIGHT_SEMS, pltpu.SemaphoreType.DMA((2,)),
            pltpu.SemaphoreType.DMA((4,)),
        ],
        compiler_params=limit(60),
        cost_estimate=cost(4 * rows * dim * units * planes, 2 * planes * units * (2 * dim + rows)),
    )(spots, g_ffn, rstd, norms, slope, g2, xhat, *out_sources, *in_sources)


def attention_back_heads(s, seq_len, q_ref, k_ref, v_ref, p_ref, g_ref, dq_ref, dk_ref, dv_ref, first_seq):
    dim = q_ref.shape[1]
    scale = 1.0 / math.sqrt(dim // HEADS)
    masks, first = head_masks()
    at = slice((s - first_seq) * seq_len, (s - first_seq + 1) * seq_len)
    for j in range(HEADS // 2):
        cols = slice(128 * j, 128 * (j + 1))
        q, k, v, g = q_ref[at, cols], k_ref[at, cols], v_ref[at, cols], g_ref[at, cols]
        dq, dk, dv = [], [], []
        for h in range(2):
            probs_low = p_ref[(s - first_seq) * HEADS + 2 * j + h]
            probs = probs_low.astype(F32)
            g_probs = mm_t(v, g * masks[h])
            g_scores = (probs * (g_probs - jnp.sum(g_probs * probs, axis=0, keepdims=True))).astype(BF)
            dv.append(mm(probs_low, g))
            dk.append(mm(g_scores, q))
            dq.append(t_mm(g_scores, k))
        dq_ref[at, cols] = (jnp.where(first, dq[0], dq[1]) * scale).astype(BF)
        dk_ref[at, cols] = jnp.where(first, dk[0], dk[1]).astype(BF)
        dv_ref[at, cols] = jnp.where(first, dv[0], dv[1]).astype(BF)


def load_heads(hbm, vmem, sems, first, count):
    seq_len = hbm[3].shape[1]
    rows, heads = pl.ds(first * seq_len, count * seq_len), pl.ds(first * HEADS, count * HEADS)
    pairs = [(hbm[i].at[rows], vmem[i]) for i in range(3)] + [(hbm[3].at[heads], vmem[3])]
    return begin(pairs, sems)


def attention_back_first_kernel(spots_ref, *refs):
    *refs, ctx_hbm, dq_ref, dk_ref, dv_ref, w_ref, g1_ref, ctx_ref, q_ref, k_ref, v_ref, p_ref, w_sems, sems, g_sems = refs
    g1_hbm, *sources, q_hbm, k_hbm, v_hbm, p_hbm = refs
    seq_len = p_ref.shape[1]
    rows, dim = g1_ref.shape
    loads = begin(((g1_hbm, g1_ref),), g_sems.at[pl.ds(0, 1)])
    fetch_stacked(spots_ref, sources, w_ref, w_sems, True)
    seqs = q_ref.shape[0] // seq_len
    loads += load_heads((q_hbm, k_hbm, v_hbm, p_hbm), (q_ref, k_ref, v_ref, p_ref), sems, 0, seqs)
    loads[0].wait()
    arrive_stacked(w_ref, w_sems, 3)
    ctx_ref[...] = mm_t(g1_ref[...], w_ref[3]).astype(BF)
    later = pl.ds(seqs * seq_len, rows - seqs * seq_len)
    store = begin(((ctx_ref.at[later], ctx_hbm),), g_sems.at[pl.ds(1, 1)])[0]
    for load in loads[1:]:
        load.wait()
    for s in range(seqs):
        attention_back_heads(s, seq_len, q_ref, k_ref, v_ref, p_ref, ctx_ref, dq_ref, dk_ref, dv_ref, 0)
    store.wait()


def attention_back_last_kernel(spots_ref, *refs):
    *refs, out_ref, g1_ref, ctx_ref, dq0_ref, dk0_ref, dv0_ref, w_ref, q_ref, k_ref, v_ref, p_ref, dq_ref, dk_ref, dv_ref, w_sems, sems, late_sems = refs
    g1_hbm, ctx_hbm, dq0_hbm, dk0_hbm, dv0_hbm, *sources, q_hbm, k_hbm, v_hbm, p_hbm = refs
    rows, dim = g1_ref.shape
    seq_len = p_ref.shape[1]
    first = dq0_ref.shape[0] // seq_len
    seqs = q_ref.shape[0] // seq_len
    loads = begin(((ctx_hbm, ctx_ref),), late_sems.at[pl.ds(0, 1)])
    loads += load_heads((q_hbm, k_hbm, v_hbm, p_hbm), (q_ref, k_ref, v_ref, p_ref), sems, first, seqs)
    for load in loads:
        load.wait()
    fetch_stacked(spots_ref, sources, w_ref, w_sems, False)
    pairs = ((dq0_hbm, dq0_ref), (dk0_hbm, dk0_ref), (dv0_hbm, dv0_ref), (g1_hbm, g1_ref))
    loads = begin(pairs, late_sems.at[pl.ds(1, 4)])
    for s in range(seqs):
        attention_back_heads(s, seq_len, q_ref, k_ref, v_ref, p_ref, ctx_ref, dq_ref, dk_ref, dv_ref, 0)
    for load in loads:
        load.wait()
    for m in range(3):
        arrive_stacked(w_ref, w_sems, m)
    for at, grads in ((slice(0, first * seq_len), (dq0_ref, dk0_ref, dv0_ref)), (slice(first * seq_len, rows), (dq_ref, dk_ref, dv_ref))):
        total = g1_ref[at, :]
        for m, grad in enumerate(grads):
            total = total + mm(grad[...], w_ref[m])
        out_ref[at, :] = total.astype(BF)


def attention_backward_first(spots, g1_low, sources, q, k, v, probs):
    rows, dim = g1_low.shape
    heads, seq_len = probs.shape[0] // 2, probs.shape[1]
    half, low = jax.ShapeDtypeStruct((rows // 2, dim), BF), pltpu.VMEM((rows // 2, dim), BF)
    return pl.pallas_call(
        attention_back_first_kernel,
        out_shape=[half, half, half, half],
        in_specs=[SMEM, ANY] + [ANY] * (len(sources) + 4),
        out_specs=[ANY] + [VMEM] * 3,
        scratch_shapes=[pltpu.VMEM((4, dim, dim), BF), pltpu.VMEM((rows, dim), BF), pltpu.VMEM((rows, dim), BF), low, low, low, pltpu.VMEM((heads,) + probs.shape[1:], BF),
                        WEIGHT_SEMS, pltpu.SemaphoreType.DMA((4,)), pltpu.SemaphoreType.DMA((2,))],
        compiler_params=limit(60),
        cost_estimate=cost(2 * rows * dim * (dim + 2 * seq_len), 2 * (dim * dim + 5 * rows * dim)),
    )(spots, g1_low, *sources, q, k, v, probs)


def attention_backward_last(spots, g1, halfway, sources, q, k, v, probs):
    rows, dim = g1.shape
    heads, seq_len = probs.shape[0] // 2, probs.shape[1]
    low = pltpu.VMEM((rows // 2, dim), BF)
    return pl.pallas_call(
        attention_back_last_kernel,
        out_shape=jax.ShapeDtypeStruct((rows, dim), BF),
        in_specs=[SMEM] + [ANY] * (len(sources) + 9),
        out_specs=VMEM,
        scratch_shapes=[pltpu.VMEM((rows, dim), F32), low, low, low, low, pltpu.VMEM((4, dim, dim), BF), low, low, low, pltpu.VMEM((heads,) + probs.shape[1:], BF), low, low, low,
                        WEIGHT_SEMS, pltpu.SemaphoreType.DMA((4,)), pltpu.SemaphoreType.DMA((5,))],
        compiler_params=limit(60),
        cost_estimate=cost(2 * rows * dim * (3 * dim + 2 * seq_len), 2 * (3 * dim * dim + 5 * rows * dim)),
    )(spots, g1, *halfway, *sources, q, k, v, probs)


def shards(
    tokens, lengths, adapter_mask, cotangent, att_query, att_key, att_value, att_out,
    norm1_gain, norm1_bias, ffn_in, ffn_bias, ffn_out, adapt_down, adapt_up, norm2_gain,
    norm2_bias, joining_query, joining_key, joining_value, joining_qbias, joining_vbias,
):
    groups = lax.axis_size("tensor")
    dp_size = lax.axis_size("dp")
    my_z = lax.axis_index("tensor")
    my_d = lax.axis_index("dp")
    seq_local, seq_len, dim = tokens.shape
    mine = seq_local // groups
    rows = mine * seq_len
    adapters, neck = adapt_up.shape[0], adapt_up.shape[1]
    own_rows = joining_query.shape[0]

    gather = Gather(dp_size, groups, my_d, my_z, mine)
    spots = gather.spots
    biases = lax.dynamic_update_slice(
        jnp.zeros((8, dim), BF), jnp.stack([joining_qbias, joining_vbias]), (0, (my_d * groups + my_z) * own_rows)
    )
    att_mats = [att_query.T, att_key.T, att_value.T, att_out]
    join_part = jnp.concatenate([joining_query, joining_key, joining_value, biases], axis=0)

    def my_slice(array):
        return lax.dynamic_slice_in_dim(array, my_z * mine, mine, 0)

    x = my_slice(tokens).reshape(rows, dim)
    shifts = jnp.arange(128, dtype=jnp.int32)
    bits = jnp.right_shift(my_slice(adapter_mask)[:, None], jnp.minimum(shifts, adapters)[None, :]) % 2
    avail = jnp.where(shifts[None, :] < adapters, bits, 0)[:, None, :]
    norms = jnp.stack([norm1_gain, norm1_bias, norm2_gain, norm2_bias])
    lens = my_slice(lengths)
    owner = jnp.arange(adapters * neck, dtype=jnp.int32) // neck
    member = (owner[:, None] == shifts[None, :]).astype(BF)
    member_t = (shifts[:, None] == owner[None, :]).astype(BF)
    kept = {}

    def attend(sources):
        kept["att"] = attention_forward(spots, lens, x, sources, norms, seq_len)
        return [kept["att"][4]]

    def feed(sources):
        kept["ffn"] = ffn_forward(spots, kept["att"][4], sources, ffn_bias, ffn_in.shape[1])
        return [kept["ffn"][0]]

    if gather.paired:
        own = [att_mats, [ffn_in], None, [ffn_out]]
        steps = [
            lambda got: [],
            lambda got: [],
            lambda got: attend(got[0] + own[0]),
            lambda got: feed(got[1] + own[1]),
            lambda got: [],
            lambda got: [],
        ]
        quarter = att_mats[3]
        for i in range(3):
            quarter = jnp.where(my_d // 2 == i, att_mats[i], quarter)
        half = gather.half_of(quarter)
        rounds = [(half, tie(quarter, half))]
        shards_in, shards_out = tie(ffn_in, half), tie(ffn_out, half)
        in_quarter, in_half, out_quarter, out_half = cut(spots, [shards_in, shards_out])
        rounds += [(in_half, in_quarter), (out_half, out_quarter)]
        join_part = tie(join_part, *rounds[0])
        theirs = send(join_part, CORE)
        even = lax.rem(my_d, 2) == 0
        pair = jnp.concatenate([jnp.where(even, join_part, theirs), jnp.where(even, theirs, join_part)], axis=0)
        rounds.insert(2, (join_part, pair, join_part, theirs))
        got = gather.all_rounds(rounds, [x, norms, lens, avail, member, member_t, spots], steps)
        att_sources, in_sources, out_sources = (got[i] + own[i] for i in (0, 1, 3))
        join_sources = got[2]
    else:
        att_pack = jnp.concatenate(att_mats, axis=0)
        att_sources = gather.whole(gather.part_of(att_pack), True)
        in_sources, out_sources = (gather.whole(gather.part_of(shard)) for shard in (ffn_in, ffn_out))
        join_sources = [lax.all_gather(join_part, ("dp", "tensor"), axis=0)]
    up = adapt_up.reshape(adapters * neck, dim)
    cot = cotangent.reshape(rows, dim)

    def rest(att, ffn, avail, cot):
        q, k, v, probs, low1, xhat1, rstd1 = att
        act, slope = ffn
        layer_out, g2, g_ffn, *grads = joining(
            spots, gather.paired, act, out_sources, adapt_down, up, join_sources, member, member_t, avail, xhat1, norms, cot
        )
        done = {}

        def between(start):
            gradient = g_ffn if start is None else tie(g_ffn, start)
            done["g1"], g1_low = ffn_backward(spots, gradient, slope, out_sources, in_sources, g2, xhat1, rstd1, norms)
            done["half"] = attention_backward_first(spots, g1_low, att_sources, q, k, v, probs)
            return done["half"][1]

        def at_last(start):
            halfway = done["half"] if start is None else [tie(done["half"][0], start)] + list(done["half"][1:])
            return attention_backward_last(spots, done["g1"], halfway, att_sources, q, k, v, probs)

        return layer_out, grads, between, at_last

    if gather.paired:
        layer_out, grads, between, at_last = rest(kept["att"], kept["ffn"], avail, cot)
        (d_q, d_k, d_v, d_bias), input_grad = reduce_grads(gather, grads, own_rows, between, at_last)
    else:
        outs = []
        for first in range(0, mine, 2):
            at = slice(first * seq_len, (first + 2) * seq_len)
            att = attention_forward(spots, lens[first : first + 2], x[at], att_sources, norms, seq_len)
            ffn = ffn_forward(spots, att[4], in_sources, ffn_bias, ffn_in.shape[1])
            outs.append(rest(att, ffn, avail[first : first + 2], cot[at]))
        layer_out = jnp.concatenate([out[0] for out in outs])
        grads = [sum(out[1][i] for out in outs) for i in range(2)]
        (d_q, d_k, d_v, d_bias), input_grad = reduce_grads(
            gather, grads, own_rows, lambda start: [out[2](None) for out in outs],
            lambda start: jnp.concatenate([out[3](None) for out in outs]),
        )
    d_bias = lax.dynamic_slice_in_dim(d_bias[:2], (my_d * groups + my_z) * own_rows, own_rows, 1)
    return (
        layer_out.reshape(mine, seq_len, dim),
        input_grad.reshape(mine, seq_len, dim),
        d_q, d_k, d_v, d_bias[0], d_bias[1],
    )


def solution(mesh):
    both = P(ALL, None)
    return jax.shard_map(
        shards,
        mesh=mesh,
        in_specs=(
            P("dp", None, None), P("dp"), P("dp"), P(ALL, None, None),
            P(None, "tensor"), P(None, "tensor"), P(None, "tensor"), P("tensor", None),
            P(), P(), P(None, "tensor"), P(), P("tensor", None), P(), P(), P(), P(),
            both, both, both, P(ALL), P(ALL),
        ),
        out_specs=(P(ALL, None, None), P(ALL, None, None), both, both, both, P(ALL), P(ALL)),
        check_vma=False,
    )
```

profile of v0, /device:TPU:0, one launch (start us, length us, event | category | flops | bytes accessed | tf_op | source)
XLA Modules:
  0.0 198.9 jit_solution(5644509309529496004)
XLA Ops:
  0.8 2.1 %select_select_fusion = bf16[192,768]{1,0:T(8,128)(2,1)} fusion(bf16[192,768]{1,0:T(8,128)(2,1)} %refs_13_.1, pred[]{:T(512)S(6)} %eq.63, pred[]{:T(512)S(6)} %eq.62, pred[]{:T(512)S(6)} %eq.61, bf16[768,192]{0,1:T(8,128)(2,1)} %param.28, bf16[768,192]{0,1:T(8,128)(2,1)} %param.29, bf16[768,192]{0,1:T(8,128)(2,1)} %param.30), kind=kLoop, calls=%fused_computation.4 | loop fusion | flops 442368 | bytes 1474563 | tf_op jit(solution)/shard_map/jit(_where)/select_n | solution.py:1022
  2.8 1.7 slice_select_fusion
  4.5 4.0 %collective-permute-start.1 = (bf16[96,768]{1,0:T(8,128)(2,1)}, bf16[96,768]{1,0:T(8,128)(2,1)S(1)}, u32[]{:S(2)}, u32[]{:S(2)}) collective-permute-start(bf16[96,768]{1,0:T(8,128)(2,1)} %slice_select_fusion), channel_id=1, source_target_pairs={{0,2},{1,3},{2,0},{3,1},{4,6},{5,7},{6,4},{7,5},{8,10},{9,11},{10,... | collective-permute-start | bytes 442376 | tf_op jit(solution)/shard_map/planes0/across/ppermute | solution.py:74
  17.6 2.8 %shard_map.279 = (bf16[192,768]{1,0:T(8,128)(2,1)}, bf16[96,768]{1,0:T(8,128)(2,1)}, bf16[192,768]{1,0:T(8,128)(2,1)}, bf16[96,768]{1,0:T(8,128)(2,1)}) custom-call(s32[9]{0:T(128)} %pad_add_fusion.spots_ref, bf16[768,768]{1,0:T(8,128)(2,1)} %refs_14_.1, bf16[768,768]{1,0:T(8,128)(2,1)} %refs_8_.3), custom_call_target="tpu_custom_call" | custom-call | tf_op jit(solution)/shard_map/pallas_call | solution.py:195
  26.0 1.8 collective-permute-start.7
  27.8 1.6 collective-permute-start.5
  30.0 14.2 %collective-permute-done.6.refs_1_ = bf16[96,768]{1,0:T(8,128)(2,1)S(1)} collective-permute-done((bf16[96,768]{1,0:T(8,128)(2,1)S(1)}, bf16[96,768]{1,0:T(8,128)(2,1)S(1)}, u32[]{:S(2)}, u32[]{:S(2)}) %collective-permute-start.6) | collective-permute-done | bytes 147488 | tf_op jit(solution)/shard_map/round0/planes1/across/ppermute | solution.py:74
  48.3 1.6 collective-permute-start.8
  49.9 11.0 %collective-permute-done.9.refs_1_ = bf16[80,768]{1,0:T(8,128)(2,1)S(1)} collective-permute-done((bf16[80,768]{1,0:T(8,128)(2,1)S(1)}, bf16[80,768]{1,0:T(8,128)(2,1)S(1)}, u32[]{:S(2)}, u32[]{:S(2)}) %collective-permute-start.9) | collective-permute-done | bytes 122912 | tf_op jit(solution)/shard_map/round1/planes2/across/ppermute | solution.py:74
  60.9 3.6 %collective-permute-done.12.refs_1_.refs_10_ = bf16[6,96,768]{2,1,0:T(8,128)(2,1)} collective-permute-done((bf16[6,96,768]{2,1,0:T(8,128)(2,1)S(1)}, bf16[6,96,768]{2,1,0:T(8,128)(2,1)}, u32[]{:S(2)}, u32[]{:S(2)}) %collective-permute-start.12) | collective-permute-done | bytes 884768 | tf_op jit(solution)/shard_map/round1/near/ppermute | solution.py:70
  68.8 1.8 slice.27
  74.0 12.2 %round2.2 = (bf16[512,768]{1,0:T(8,128)(2,1)}, bf16[512,768]{1,0:T(8,128)(2,1)}, bf16[512,768]{1,0:T(8,128)(2,1)}, bf16[24,256,256]{2,1,0:T(8,128)(2,1)}, bf16[5...) custom-call(s32[9]{0:T(128)} %pad_add_fusion.spots_ref, s32[2]{0:T(128)} %dynamic_slice.13.len_ref, ...), custom_call_target="tpu_custom_call" | custom-call | flops 2818572288 | bytes 11010048 | tf_op jit(solution)/shard_map/round2/pallas_call | solution.py:439
  88.0 1.8 slice.28
  94.5 8.6 %round3.2 = (bf16[512,3072]{1,0:T(8,128)(2,1)}, bf16[512,3072]{1,0:T(8,128)(2,1)}) custom-call(s32[9]{0:T(128)} %pad_add_fusion.spots_ref, bf16[512,768]{1,0:T(8,128)(2,1)} %get-tuple-element.93.x_ref, f32[4,1,768]{2,1,0:T(1,128)} %bitcast.32, bf16[6,96,768]{2,1,0:T(8,128)(2,1)} %copy-done.2, bf16[6,96,768]{2,1,0:T(8,128)(2,1)} %collective-permute-done.12.refs_1_.refs_10_, ...), custom_call_target="tpu_custom_call" | custom-call | flops 2415919104 | bytes 11010048 | tf_op jit(solution)/shard_map/round3/pallas_call | solution.py:483
  104.5 5.3 %collective-permute-done.27.refs_10_.refs_3_ = bf16[3,96,768]{2,1,0:T(8,128)(2,1)} collective-permute-done((bf16[3,96,768]{2,1,0:T(8,128)(2,1)}, bf16[3,96,768]{2,1,0:T(8,128)(2,1)}, u32[]{:S(2)}, u32[]{:S(2)}) %collective-permute-start.27) | collective-permute-done | bytes 442400 | tf_op jit(solution)/shard_map/round3/near/ppermute | solution.py:70
  110.3 2.5 %collective-permute-done.31.refs_11_.refs_4_ = bf16[3,96,768]{2,1,0:T(8,128)(2,1)S(1)} collective-permute-done((bf16[3,96,768]{2,1,0:T(8,128)(2,1)S(1)}, bf16[3,96,768]{2,1,0:T(8,128)(2,1)S(1)}, u32[]{:S(2)}, u32[]{:S(2)}) %collective-permute-start.31) | collective-permute-done | bytes 442400 | tf_op jit(solution)/shard_map/round3/far/ppermute | solution.py:70
  116.0 30.7 %shard_map.280 = (bf16[512,768]{1,0:T(8,128)(2,1)}, f32[512,768]{1,0:T(8,128)}, bf16[512,768]{1,0:T(8,128)(2,1)}, bf16[4,304,768]{2,1,0:T(8,128)(2,1)}, bf16[4,304,768]{2,1,0:T(8,128)(2,1)}) custom-call(s32[9]{0:T(128)} %pad_add_fusion.spots_ref, bf16[768,128]{1,0:T(8,128)(2,1)} %fusion.member_ref, bf16[128,768]{1,0:T(8,128)(2,1)} %fusion.1.member_t_ref, ...), custom_call_target="tpu_custom_call" | custom-call | flops 11475615744 | bytes 17301504 | tf_op jit(solution)/shard_map/pallas_call | solution.py:752
  146.9 4.0 %collective-permute-done.35.come_hbm.refs_4_ = bf16[4,304,768]{2,1,0:T(8,128)(2,1)} collective-permute-done((bf16[4,304,768]{2,1,0:T(8,128)(2,1)}, bf16[4,304,768]{2,1,0:T(8,128)(2,1)}, u32[]{:S(2)}, u32[]{:S(2)}) %collective-permute-start.35) | collective-permute-done | bytes 1867808 | tf_op jit(solution)/shard_map/cores/ppermute | solution.py:70
  150.9 3.4 %shard_map.281 = (bf16[304,768]{1,0:T(8,128)(2,1)}, bf16[304,768]{1,0:T(8,128)(2,1)}, bf16[304,768]{1,0:T(8,128)(2,1)}) custom-call(s32[9]{0:T(128)} %pad_add_fusion.spots_ref, bf16[4,304,768]{2,1,0:T(8,128)(2,1)} %get-tuple-element.131.keep_hbm.refs_3_, bf16[4,304,768]{2,1,0:T(8,128)(2,1)} %collective-permute-done.35.come_hbm.refs_4_), custom_call_target="tpu_custom_call" | custom-call | tf_op jit(solution)/shard_map/pallas_call | solution.py:350
  157.8 11.8 %shard_map.282 = (f32[512,768]{1,0:T(8,128)}, bf16[512,768]{1,0:T(8,128)(2,1)}) custom-call(s32[9]{0:T(128)} %pad_add_fusion.spots_ref, bf16[512,768]{1,0:T(8,128)(2,1)} %get-tuple-element.117.g_ref, f32[512,1]{1,0:T(8,128)} %get-tuple-element.118.rstd_ref, f32[4,768]{1,0:T(4,128)} %pad_maximum_fusion.2.norms_ref, ...), custom_call_target="tpu_custom_call" | custom-call | flops 4831838208 | bytes 12582912 | tf_op jit(solution)/shard_map/pallas_call | solution.py:839
  169.6 8.4 %shard_map.283 = (bf16[256,768]{1,0:T(8,128)(2,1)}, bf16[256,768]{1,0:T(8,128)(2,1)}, bf16[256,768]{1,0:T(8,128)(2,1)}, bf16[256,768]{1,0:T(8,128)(2,1)}) custom-call(s32[9]{0:T(128)} %pad_add_fusion.spots_ref, bf16[512,768]{1,0:T(8,128)(2,1)} %get-tuple-element.122.refs_0_, bf16[6,96,768]{2,1,0:T(8,128)(2,1)} %copy-done.1, bf16[6,96,768]{2,1,0:T(8,128)(2,1)} %copy-done.6, ...), custom_call_target="tpu_custom_call" | custom-call | flops 1006632960 | bytes 5111808 | tf_op jit(solution)/shard_map/pallas_call | solution.py:937
  179.1 3.8 %shard_map.284 = (f32[80,768]{1,0:T(8,128)}, bf16[80,768]{1,0:T(8,128)(2,1)}, bf16[80,768]{1,0:T(8,128)(2,1)}, bf16[80,768]{1,0:T(8,128)(2,1)}) custom-call(s32[9]{0:T(128)} %pad_add_fusion.spots_ref, bf16[304,768]{1,0:T(8,128)(2,1)} %collective-permute-done.36.refs_0_, bf16[304,768]{1,0:T(8,128)(2,1)} %collective-permute-done.37.refs_1_, ...), custom_call_target="tpu_custom_call" | custom-call | tf_op jit(solution)/shard_map/pallas_call | solution.py:363
  185.3 2.1 %collective-permute-start.41 = (bf16[80,768]{1,0:T(8,128)(2,1)}, bf16[80,768]{1,0:T(8,128)(2,1)S(1)}, u32[]{:S(2)}, u32[]{:S(2)}) collective-permute-start(bf16[80,768]{1,0:T(8,128)(2,1)} %get-tuple-element.138), channel_id=1, source_target_pairs={{0,3},{1,0},{2,1},{3,2},{4,7},{5,4},{6,5},{7,6},{8,11},{9,8},{10,9... | collective-permute-start | bytes 368648 | tf_op jit(solution)/shard_map/stack2/ppermute | solution.py:74
  187.5 9.9 %shard_map.285 = bf16[512,768]{1,0:T(8,128)(2,1)} custom-call(s32[9]{0:T(128)} %pad_add_fusion.spots_ref, f32[512,768]{1,0:T(8,128)} %get-tuple-element.121.refs_0_, bf16[256,768]{1,0:T(8,128)(2,1)} %get-tuple-element.133.refs_1_, bf16[256,768]{1,0:T(8,128)(2,1)} %get-tuple-element.130.refs_2_, bf16[256,768]{1,0:T(8,128)(2,1)} %get-tuple-element.134.refs_3_, ...), custom_call_target="tpu_custom_call" | custom-call | flops 2214592512 | bytes 7471104 | tf_op jit(solution)/shard_map/pallas_call | solution.py:953
  (164 shorter events, 46.8 us)
Async XLA Ops:
  4.5 17.5 %collective-permute-start.1 = (bf16[96,768]{1,0:T(8,128)(2,1)}, bf16[96,768]{1,0:T(8,128)(2,1)S(1)}, u32[]{:S(2)}, u32[]{:S(2)}) collective-permute-start(bf16[96,768]{1,0:T(8,128)(2,1)} %slice_select_fusion), channel_id=1, source_target_pairs={{0,2},{1,3},{2,0},{3,1},{4,6},{5,7},{6,4},{7,5},{8,10},{9,11},{10,... | collective-permute-start | bytes 442376 | tf_op jit(solution)/shard_map/planes0/across/ppermute | solution.py:74
  8.5 13.5 %collective-permute-start = (bf16[192,768]{1,0:T(8,128)(2,1)}, bf16[192,768]{1,0:T(8,128)(2,1)}, u32[]{:S(2)}, u32[]{:S(2)}) collective-permute-start(bf16[192,768]{1,0:T(8,128)(2,1)} %select_select_fusion), channel_id=1, source_target_pairs={{0,3},{1,0},{2,1},{3,2},{4,5},{5,6},{6,7},{7,4},{8,11},{9,8},{10,9... | collective-permute-start | bytes 884744 | tf_op jit(solution)/shard_map/planes0/beside/ppermute | solution.py:79
  10.3 11.7 %collective-permute-start.2 = (bf16[80,768]{1,0:T(8,128)(2,1)S(1)}, bf16[80,768]{1,0:T(8,128)(2,1)S(1)}, u32[]{:S(2)}, u32[]{:S(2)}) collective-permute-start(bf16[80,768]{1,0:T(8,128)(2,1)S(1)} %pad_maximum_fusion.1.refs_4_), channel_id=1, source_target_pairs={{0,4},{4,0},{8,12},{12,8},{16,20},{20,16},{24,28},{28,24},{1,5},{5... | collective-permute-start | bytes 368648 | tf_op jit(solution)/shard_map/ppermute | solution.py:70
  26.0 18.1 %collective-permute-start.7 = (bf16[6,96,768]{2,1,0:T(8,128)(2,1)S(1)}, bf16[6,96,768]{2,1,0:T(8,128)(2,1)S(1)}, u32[]{:S(2)}, u32[]{:S(2)}) collective-permute-start(bf16[6,96,768]{2,1,0:T(8,128)(2,1)S(1)} %round0.1.refs_0_.refs_1_.refs_5_), channel_id=1, source_target_pairs={{0,8},{4,20},{8,0},{12,28},{16,24},{20,4},{24,16},{28,12},{1,9},{5... | collective-permute-start | bytes 2654216 | tf_op jit(solution)/shard_map/round0/near/ppermute | solution.py:70
  27.8 16.3 %collective-permute-start.5 = (bf16[192,768]{1,0:T(8,128)(2,1)S(1)}, bf16[192,768]{1,0:T(8,128)(2,1)S(1)}, u32[]{:S(2)}, u32[]{:S(2)}) collective-permute-start(bf16[192,768]{1,0:T(8,128)(2,1)S(1)} %copy-done.25), channel_id=1, source_target_pairs={{0,3},{1,0},{2,1},{3,2},{4,5},{5,6},{6,7},{7,4},{8,11},{9,8},{10,9... | collective-permute-start | bytes 884744 | tf_op jit(solution)/shard_map/round0/planes1/beside/ppermute | solution.py:79
  29.5 14.7 %collective-permute-start.6 = (bf16[96,768]{1,0:T(8,128)(2,1)S(1)}, bf16[96,768]{1,0:T(8,128)(2,1)S(1)}, u32[]{:S(2)}, u32[]{:S(2)}) collective-permute-start(bf16[96,768]{1,0:T(8,128)(2,1)S(1)} %copy-done.27), channel_id=1, source_target_pairs={{0,2},{1,3},{2,0},{3,1},{4,6},{5,7},{6,4},{7,5},{8,10},{9,11},{10,... | collective-permute-start | bytes 442376 | tf_op jit(solution)/shard_map/round0/planes1/across/ppermute | solution.py:74
  44.7 16.2 %collective-permute-start.14 = (bf16[6,96,768]{2,1,0:T(8,128)(2,1)S(1)}, bf16[6,96,768]{2,1,0:T(8,128)(2,1)S(1)}, u32[]{:S(2)}, u32[]{:S(2)}) collective-permute-start(bf16[6,96,768]{2,1,0:T(8,128)(2,1)S(1)} %collective-permute-done.7.refs_1_.refs_2_.refs_6_), channel_id=1, source_target_pairs={{0,4},{4,0},{8,12},{12,8},{16,20},{20,16},{24,28},{28,24},{1,5},{5... | collective-permute-start | bytes 2654216 | tf_op jit(solution)/shard_map/round1/swap/ppermute | solution.py:70
  46.6 17.9 %collective-permute-start.12 = (bf16[6,96,768]{2,1,0:T(8,128)(2,1)S(1)}, bf16[6,96,768]{2,1,0:T(8,128)(2,1)}, u32[]{:S(2)}, u32[]{:S(2)}) collective-permute-start(bf16[6,96,768]{2,1,0:T(8,128)(2,1)S(1)} %round1.1.refs_0_.refs_9_), channel_id=1, source_target_pairs={{0,8},{4,20},{8,0},{12,28},{16,24},{20,4},{24,16},{28,12},{1,9},{5... | collective-permute-start | bytes 2654216 | tf_op jit(solution)/shard_map/round1/near/ppermute | solution.py:70
  47.2 13.7 %collective-permute-start.13 = (bf16[3,96,768]{2,1,0:T(8,128)(2,1)S(1)}, bf16[3,96,768]{2,1,0:T(8,128)(2,1)S(1)}, u32[]{:S(2)}, u32[]{:S(2)}) collective-permute-start(bf16[3,96,768]{2,1,0:T(8,128)(2,1)S(1)} %slice.26), channel_id=1, source_target_pairs={{0,20},{4,8},{8,28},{12,0},{16,4},{20,24},{24,12},{28,16},{1,21},{... | collective-permute-start | bytes 1327112 | tf_op jit(solution)/shard_map/round1/far/ppermute | solution.py:70
  48.3 12.6 %collective-permute-start.8 = (bf16[160,768]{1,0:T(8,128)(2,1)S(1)}, bf16[160,768]{1,0:T(8,128)(2,1)S(1)}, u32[]{:S(2)}, u32[]{:S(2)}) collective-permute-start(bf16[160,768]{1,0:T(8,128)(2,1)S(1)} %pad_maximum_fusion), channel_id=1, source_target_pairs={{0,3},{1,0},{2,1},{3,2},{4,5},{5,6},{6,7},{7,4},{8,11},{9,8},{10,9... | collective-permute-start | bytes 737288 | tf_op jit(solution)/shard_map/round1/planes2/beside/ppermute | solution.py:79
  67.8 19.2 %collective-permute-start.20 = (bf16[8,80,768]{2,1,0:T(8,128)(2,1)}, bf16[8,80,768]{2,1,0:T(8,128)(2,1)}, u32[]{:S(2)}, u32[]{:S(2)}) collective-permute-start(bf16[8,80,768]{2,1,0:T(8,128)(2,1)} %round2.3.refs_2_), channel_id=1, source_target_pairs={{0,8},{4,20},{8,0},{12,28},{16,24},{20,4},{24,16},{28,12},{1,9},{5... | collective-permute-start | bytes 2949128 | tf_op jit(solution)/shard_map/round2/near/ppermute | solution.py:70
  68.3 18.3 %collective-permute-start.22 = (bf16[6,96,768]{2,1,0:T(8,128)(2,1)}, bf16[6,96,768]{2,1,0:T(8,128)(2,1)}, u32[]{:S(2)}, u32[]{:S(2)}) collective-permute-start(bf16[6,96,768]{2,1,0:T(8,128)(2,1)} %collective-permute-done.12.refs_1_.refs_10_), channel_id=1, source_target_pairs={{0,4},{4,0},{8,12},{12,8},{16,20},{20,16},{24,28},{28,24},{1,5},{5... | collective-permute-start | bytes 2654216 | tf_op jit(solution)/shard_map/round2/swap/ppermute | solution.py:70
  70.6 16.0 %collective-permute-start.21 = (bf16[3,96,768]{2,1,0:T(8,128)(2,1)}, bf16[3,96,768]{2,1,0:T(8,128)(2,1)}, u32[]{:S(2)}, u32[]{:S(2)}) collective-permute-start(bf16[3,96,768]{2,1,0:T(8,128)(2,1)} %slice.27), channel_id=1, source_target_pairs={{0,20},{4,8},{8,28},{12,0},{16,4},{20,24},{24,12},{28,16},{1,21},{... | collective-permute-start | bytes 1327112 | tf_op jit(solution)/shard_map/round2/far/ppermute | solution.py:70
  71.9 14.8 %collective-permute-start.16 = (bf16[192,768]{1,0:T(8,128)(2,1)}, bf16[192,768]{1,0:T(8,128)(2,1)S(1)}, u32[]{:S(2)}, u32[]{:S(2)}) collective-permute-start(bf16[192,768]{1,0:T(8,128)(2,1)} %get-tuple-element.96), channel_id=1, source_target_pairs={{0,3},{1,0},{2,1},{3,2},{4,5},{5,6},{6,7},{7,4},{8,11},{9,8},{10,9... | collective-permute-start | bytes 884744 | tf_op jit(solution)/shard_map/round2/planes3/beside/ppermute | solution.py:79
  73.2 13.4 %collective-permute-start.17 = (bf16[96,768]{1,0:T(8,128)(2,1)S(1)}, bf16[96,768]{1,0:T(8,128)(2,1)S(1)}, u32[]{:S(2)}, u32[]{:S(2)}) collective-permute-start(bf16[96,768]{1,0:T(8,128)(2,1)S(1)} %copy-done.26), channel_id=1, source_target_pairs={{0,2},{1,3},{2,0},{3,1},{4,6},{5,7},{6,4},{7,5},{8,10},{9,11},{10,... | collective-permute-start | bytes 442376 | tf_op jit(solution)/shard_map/round2/planes3/across/ppermute | solution.py:74
  87.0 16.3 %collective-permute-start.29 = (bf16[8,80,768]{2,1,0:T(8,128)(2,1)}, bf16[8,80,768]{2,1,0:T(8,128)(2,1)}, u32[]{:S(2)}, u32[]{:S(2)}) collective-permute-start(bf16[8,80,768]{2,1,0:T(8,128)(2,1)} %collective-permute-done.20.refs_3_), channel_id=1, source_target_pairs={{0,4},{4,0},{8,12},{12,8},{16,20},{20,16},{24,28},{28,24},{1,5},{5... | collective-permute-start | bytes 2949128 | tf_op jit(solution)/shard_map/round3/swap/ppermute | solution.py:70
  89.8 13.2 %collective-permute-start.28 = (bf16[4,80,768]{2,1,0:T(8,128)(2,1)}, bf16[4,80,768]{2,1,0:T(8,128)(2,1)S(1)}, u32[]{:S(2)}, u32[]{:S(2)}) collective-permute-start(bf16[4,80,768]{2,1,0:T(8,128)(2,1)} %slice.28), channel_id=1, source_target_pairs={{0,20},{4,8},{8,28},{12,0},{16,4},{20,24},{24,12},{28,16},{1,21},{... | collective-permute-start | bytes 1474568 | tf_op jit(solution)/shard_map/round3/far/ppermute | solution.py:70
  93.3 16.5 %collective-permute-start.27 = (bf16[3,96,768]{2,1,0:T(8,128)(2,1)}, bf16[3,96,768]{2,1,0:T(8,128)(2,1)}, u32[]{:S(2)}, u32[]{:S(2)}) collective-permute-start(bf16[3,96,768]{2,1,0:T(8,128)(2,1)} %get-tuple-element.106.refs_8_.refs_1_), channel_id=1, source_target_pairs={{0,8},{4,20},{8,0},{12,28},{16,24},{20,4},{24,16},{28,12},{1,9},{5... | collective-permute-start | bytes 1327112 | tf_op jit(solution)/shard_map/round3/near/ppermute | solution.py:70
  154.3 24.0 %collective-permute-start.38 = (bf16[304,768]{1,0:T(8,128)(2,1)}, bf16[304,768]{1,0:T(8,128)(2,1)S(1)}, u32[]{:S(2)}, u32[]{:S(2)}) collective-permute-start(bf16[304,768]{1,0:T(8,128)(2,1)} %get-tuple-element.116), channel_id=1, source_target_pairs={{0,24},{4,28},{8,16},{12,20},{16,8},{20,12},{24,0},{28,4},{1,25},{... | collective-permute-start | bytes 1400840 | tf_op jit(solution)/shard_map/far/ppermute | solution.py:70
  155.9 22.2 %collective-permute-start.36 = (bf16[304,768]{1,0:T(8,128)(2,1)}, bf16[304,768]{1,0:T(8,128)(2,1)}, u32[]{:S(2)}, u32[]{:S(2)}) collective-permute-start(bf16[304,768]{1,0:T(8,128)(2,1)} %get-tuple-element.128), channel_id=1, source_target_pairs={{0,8},{4,12},{8,0},{12,4},{16,24},{20,28},{24,16},{28,20},{1,9},{5... | collective-permute-start | bytes 1400840 | tf_op jit(solution)/shard_map/x/ppermute | solution.py:70
  156.9 21.4 %collective-permute-start.37 = (bf16[304,768]{1,0:T(8,128)(2,1)}, bf16[304,768]{1,0:T(8,128)(2,1)}, u32[]{:S(2)}, u32[]{:S(2)}) collective-permute-start(bf16[304,768]{1,0:T(8,128)(2,1)} %get-tuple-element.129), channel_id=1, source_target_pairs={{0,16},{4,20},{8,24},{12,28},{16,0},{20,4},{24,8},{28,12},{1,17},{... | collective-permute-start | bytes 1400840 | tf_op jit(solution)/shard_map/y/ppermute | solution.py:70
  182.9 14.5 %collective-permute-start.39 = (bf16[80,768]{1,0:T(8,128)(2,1)}, bf16[80,768]{1,0:T(8,128)(2,1)S(1)}, u32[]{:S(2)}, u32[]{:S(2)}) collective-permute-start(bf16[80,768]{1,0:T(8,128)(2,1)} %get-tuple-element.136), channel_id=1, source_target_pairs={{0,1},{1,2},{2,3},{3,0},{4,5},{5,6},{6,7},{7,4},{8,9},{9,10},{10,1... | collective-permute-start | bytes 368648 | tf_op jit(solution)/shard_map/stack0/ppermute | solution.py:74
  184.3 13.0 %collective-permute-start.40 = (bf16[80,768]{1,0:T(8,128)(2,1)}, bf16[80,768]{1,0:T(8,128)(2,1)S(1)}, u32[]{:S(2)}, u32[]{:S(2)}) collective-permute-start(bf16[80,768]{1,0:T(8,128)(2,1)} %get-tuple-element.137), channel_id=1, source_target_pairs={{0,2},{1,3},{2,0},{3,1},{4,6},{5,7},{6,4},{7,5},{8,10},{9,11},{10,... | collective-permute-start | bytes 368648 | tf_op jit(solution)/shard_map/stack1/ppermute | solution.py:74
  185.3 12.1 %collective-permute-start.41 = (bf16[80,768]{1,0:T(8,128)(2,1)}, bf16[80,768]{1,0:T(8,128)(2,1)S(1)}, u32[]{:S(2)}, u32[]{:S(2)}) collective-permute-start(bf16[80,768]{1,0:T(8,128)(2,1)} %get-tuple-element.138), channel_id=1, source_target_pairs={{0,3},{1,0},{2,1},{3,2},{4,7},{5,4},{6,5},{7,6},{8,11},{9,8},{10,9... | collective-permute-start | bytes 368648 | tf_op jit(solution)/shard_map/stack2/ppermute | solution.py:74
  (48 other events, 379.8 us)
where the time goes:
time: 203 us; the launch traced here: 199 us
  Pallas kernels  97 us (48%)
  waiting for transfers between devices  46.6 us (23%)
  starting transfers between devices  32.7 us (16%)
  local copies, waits for them, and re-layouts  11.6 us (6%)
  other arithmetic  9.57 us (5%)
    pallas_call x1, Pallas kernels, joining(): pl.pallas_call(partial(joining_kernel, halves=halves, count=len(join_sour...  30.7 us
    ppermute x7, waiting for transfers between devices, shift(): lax.ppermute(array, 'tensor', [(i, (i + by) % groups) for i in range(grou...  25.6 us
    ppermute x31, waiting for transfers between devices, send(): return lax.ppermute(array, 'dp', pairs)  21 us
    ppermute x31, starting transfers between devices, send(): return lax.ppermute(array, 'dp', pairs)  17.6 us
    pallas_call x1, Pallas kernels, attention_forward(): pl.pallas_call(attention_kernel, out_shape=[low, low, low, jax.ShapeDtype...  12.2 us
    pallas_call x1, Pallas kernels, ffn_backward(): pl.pallas_call(partial(ffn_back_kernel, count=(len(out_sources), len(in_s...  11.8 us
    pallas_call x1, Pallas kernels, attention_backward_last(): pl.pallas_call(attention_back_last_kernel, out_shape=jax.ShapeDtypeStruct...  9.87 us
    ppermute x7, starting transfers between devices, shift(): lax.ppermute(array, 'tensor', [(i, (i + by) % groups) for i in range(grou...  9.21 us
  transfers between devices with their start and end apart: 42, of which 15 were waited for; matrix products, arithmetic and copies ran while one was open for 6% of the time, Pallas kernels for 28%

commit v1 on v0

--- a/solution.py
+++ b/solution.py
@@ -270,7 +270,7 @@
         ahead, done = self.planes(parts[0], 0), [rows for part in parts[1:] for rows in part[:2]] + early
         for r in range(count + 2):
             with jax.named_scope("round%d" % r):
-                ready = list(lax.optimization_barrier((*ahead, *done)))
+                ready = list(lax.optimization_barrier((*ahead, *done))) if r < count else list(done)
                 ahead = ready[: len(ahead)]
                 if r >= 1:
                     at = len(ahead)
@@ -297,7 +297,7 @@
                 else:
                     ahead = []
                 if 1 <= r <= count:
-                    late = last[2:] if r == count else []
+                    late = []
                     last.append([scoped("swap", send, array, CORE) for array in last[1][:-1]])
                     last[3].append(scoped("swap", send, tie(last[1][-1], *late), CORE))
                     done += (last[2:3] if r < count else []) + last[3]
@@ -856,23 +856,21 @@
 def attention_back_heads(s, seq_len, q_ref, k_ref, v_ref, p_ref, g_ref, dq_ref, dk_ref, dv_ref, first_seq):
     dim = q_ref.shape[1]
     scale = 1.0 / math.sqrt(dim // HEADS)
-    masks, first = head_masks()
+    masks = head_masks()[0]
     at = slice((s - first_seq) * seq_len, (s - first_seq + 1) * seq_len)
     for j in range(HEADS // 2):
         cols = slice(128 * j, 128 * (j + 1))
         q, k, v, g = q_ref[at, cols], k_ref[at, cols], v_ref[at, cols], g_ref[at, cols]
-        dq, dk, dv = [], [], []
+        split = [jnp.concatenate([array * mask for mask in masks], axis=0) for array in (q, k, g)]
+        probs_low = [p_ref[(s - first_seq) * HEADS + 2 * j + h] for h in range(2)]
+        g_scores = []
         for h in range(2):
-            probs_low = p_ref[(s - first_seq) * HEADS + 2 * j + h]
-            probs = probs_low.astype(F32)
-            g_probs = mm_t(v, g * masks[h])
-            g_scores = (probs * (g_probs - jnp.sum(g_probs * probs, axis=0, keepdims=True))).astype(BF)
-            dv.append(mm(probs_low, g))
-            dk.append(mm(g_scores, q))
-            dq.append(t_mm(g_scores, k))
-        dq_ref[at, cols] = (jnp.where(first, dq[0], dq[1]) * scale).astype(BF)
-        dk_ref[at, cols] = jnp.where(first, dk[0], dk[1]).astype(BF)
-        dv_ref[at, cols] = jnp.where(first, dv[0], dv[1]).astype(BF)
+            probs = probs_low[h].astype(F32)
+            g_probs = mm_t(v, split[2][h * seq_len : (h + 1) * seq_len])
+            g_scores.append((probs * (g_probs - jnp.sum(g_probs * probs, axis=0, keepdims=True))).astype(BF))
+        dq_ref[at, cols] = (t_mm(jnp.concatenate(g_scores, axis=0), split[1]) * scale).astype(BF)
+        dk_ref[at, cols] = mm(jnp.concatenate(g_scores, axis=1), split[0]).astype(BF)
+        dv_ref[at, cols] = mm(jnp.concatenate(probs_low, axis=1), split[2]).astype(BF)
 
 
 def load_heads(hbm, vmem, sems, first, count):

time: 203 us -> 202 us (level)
  no operation moved by 1% of the time
where the time goes in v1:
time: 202 us; the launch traced here: 198 us
  Pallas kernels  96.4 us (48%)
  waiting for transfers between devices  46.9 us (23%)
  starting transfers between devices  32.5 us (16%)
  local copies, waits for them, and re-layouts  11.6 us (6%)
  other arithmetic  9.57 us (5%)
    pallas_call x1, Pallas kernels, joining(): pl.pallas_call(partial(joining_kernel, halves=halves, count=len(join_sour...  30.7 us
    ppermute x7, waiting for transfers between devices, shift(): lax.ppermute(array, 'tensor', [(i, (i + by) % groups) for i in range(grou...  25.6 us
    ppermute x31, waiting for transfers between devices, send(): return lax.ppermute(array, 'dp', pairs)  21.3 us
    ppermute x31, starting transfers between devices, send(): return lax.ppermute(array, 'dp', pairs)  17.4 us
    pallas_call x1, Pallas kernels, attention_forward(): pl.pallas_call(attention_kernel, out_shape=[low, low, low, jax.ShapeDtype...  12.2 us
    pallas_call x1, Pallas kernels, ffn_backward(): pl.pallas_call(partial(ffn_back_kernel, count=(len(out_sources), len(in_s...  11.8 us
    pallas_call x1, Pallas kernels, attention_backward_last(): pl.pallas_call(attention_back_last_kernel, out_shape=jax.ShapeDtypeStruct...  9.6 us
    ppermute x7, starting transfers between devices, shift(): lax.ppermute(array, 'tensor', [(i, (i + by) % groups) for i in range(grou...  9.21 us
  transfers between devices with their start and end apart: 42, of which 15 were waited for; matrix products, arithmetic and copies ran while one was open for 6% of the time, Pallas kernels for 28%

profile of v1, /device:TPU:0, one launch (start us, length us, event | category | flops | bytes accessed | tf_op | source)
XLA Modules:
  0.0 198.4 jit_solution(4442527793019247491)
XLA Ops:
  0.8 2.1 %select_select_fusion = bf16[192,768]{1,0:T(8,128)(2,1)} fusion(bf16[192,768]{1,0:T(8,128)(2,1)} %refs_13_.1, pred[]{:T(512)S(6)} %eq.63, pred[]{:T(512)S(6)} %eq.62, pred[]{:T(512)S(6)} %eq.61, bf16[768,192]{0,1:T(8,128)(2,1)} %param.28, bf16[768,192]{0,1:T(8,128)(2,1)} %param.29, bf16[768,192]{0,1:T(8,128)(2,1)} %param.30), kind=kLoop, calls=%fused_computation.4 | loop fusion | flops 442368 | bytes 1474563 | tf_op jit(solution)/shard_map/jit(_where)/select_n | solution.py:1020
  2.8 1.7 slice_select_fusion
  4.5 4.0 %collective-permute-start.1 = (bf16[96,768]{1,0:T(8,128)(2,1)}, bf16[96,768]{1,0:T(8,128)(2,1)S(1)}, u32[]{:S(2)}, u32[]{:S(2)}) collective-permute-start(bf16[96,768]{1,0:T(8,128)(2,1)} %slice_select_fusion), channel_id=1, source_target_pairs={{0,2},{1,3},{2,0},{3,1},{4,6},{5,7},{6,4},{7,5},{8,10},{9,11},{10,... | collective-permute-start | bytes 442376 | tf_op jit(solution)/shard_map/planes0/across/ppermute | solution.py:74
  17.6 2.8 %shard_map.279 = (bf16[192,768]{1,0:T(8,128)(2,1)}, bf16[96,768]{1,0:T(8,128)(2,1)}, bf16[192,768]{1,0:T(8,128)(2,1)}, bf16[96,768]{1,0:T(8,128)(2,1)}) custom-call(s32[9]{0:T(128)} %pad_add_fusion.spots_ref, bf16[768,768]{1,0:T(8,128)(2,1)} %refs_14_.1, bf16[768,768]{1,0:T(8,128)(2,1)} %refs_8_.3), custom_call_target="tpu_custom_call" | custom-call | tf_op jit(solution)/shard_map/pallas_call | solution.py:195
  26.0 1.8 collective-permute-start.7
  27.8 1.6 collective-permute-start.5
  30.0 14.2 %collective-permute-done.6.refs_1_ = bf16[96,768]{1,0:T(8,128)(2,1)S(1)} collective-permute-done((bf16[96,768]{1,0:T(8,128)(2,1)S(1)}, bf16[96,768]{1,0:T(8,128)(2,1)S(1)}, u32[]{:S(2)}, u32[]{:S(2)}) %collective-permute-start.6) | collective-permute-done | bytes 147488 | tf_op jit(solution)/shard_map/round0/planes1/across/ppermute | solution.py:74
  48.3 1.6 collective-permute-start.8
  49.9 11.0 %collective-permute-done.9.refs_1_ = bf16[80,768]{1,0:T(8,128)(2,1)S(1)} collective-permute-done((bf16[80,768]{1,0:T(8,128)(2,1)S(1)}, bf16[80,768]{1,0:T(8,128)(2,1)S(1)}, u32[]{:S(2)}, u32[]{:S(2)}) %collective-permute-start.9) | collective-permute-done | bytes 122912 | tf_op jit(solution)/shard_map/round1/planes2/across/ppermute | solution.py:74
  60.9 3.6 %collective-permute-done.12.refs_1_.refs_10_ = bf16[6,96,768]{2,1,0:T(8,128)(2,1)} collective-permute-done((bf16[6,96,768]{2,1,0:T(8,128)(2,1)S(1)}, bf16[6,96,768]{2,1,0:T(8,128)(2,1)}, u32[]{:S(2)}, u32[]{:S(2)}) %collective-permute-start.12) | collective-permute-done | bytes 884768 | tf_op jit(solution)/shard_map/round1/near/ppermute | solution.py:70
  68.8 1.8 slice.27
  74.0 12.2 %round2.2 = (bf16[512,768]{1,0:T(8,128)(2,1)}, bf16[512,768]{1,0:T(8,128)(2,1)}, bf16[512,768]{1,0:T(8,128)(2,1)}, bf16[24,256,256]{2,1,0:T(8,128)(2,1)}, bf16[5...) custom-call(s32[9]{0:T(128)} %pad_add_fusion.spots_ref, s32[2]{0:T(128)} %dynamic_slice.13.len_ref, ...), custom_call_target="tpu_custom_call" | custom-call | flops 2818572288 | bytes 11010048 | tf_op jit(solution)/shard_map/round2/pallas_call | solution.py:439
  88.0 1.8 slice.28
  94.5 8.6 %round3.2 = (bf16[512,3072]{1,0:T(8,128)(2,1)}, bf16[512,3072]{1,0:T(8,128)(2,1)}) custom-call(s32[9]{0:T(128)} %pad_add_fusion.spots_ref, bf16[512,768]{1,0:T(8,128)(2,1)} %get-tuple-element.89.x_ref, f32[4,1,768]{2,1,0:T(1,128)} %bitcast.32, bf16[6,96,768]{2,1,0:T(8,128)(2,1)} %copy-done.2, bf16[6,96,768]{2,1,0:T(8,128)(2,1)} %collective-permute-done.12.refs_1_.refs_10_, ...), custom_call_target="tpu_custom_call" | custom-call | flops 2415919104 | bytes 11010048 | tf_op jit(solution)/shard_map/round3/pallas_call | solution.py:483
  104.5 5.3 %collective-permute-done.30.refs_10_.refs_3_ = bf16[3,96,768]{2,1,0:T(8,128)(2,1)} collective-permute-done((bf16[3,96,768]{2,1,0:T(8,128)(2,1)}, bf16[3,96,768]{2,1,0:T(8,128)(2,1)}, u32[]{:S(2)}, u32[]{:S(2)}) %collective-permute-start.30) | collective-permute-done | bytes 442400 | tf_op jit(solution)/shard_map/round3/near/ppermute | solution.py:70
  110.3 2.5 %collective-permute-done.31.refs_11_.refs_4_ = bf16[3,96,768]{2,1,0:T(8,128)(2,1)S(1)} collective-permute-done((bf16[3,96,768]{2,1,0:T(8,128)(2,1)S(1)}, bf16[3,96,768]{2,1,0:T(8,128)(2,1)S(1)}, u32[]{:S(2)}, u32[]{:S(2)}) %collective-permute-start.31) | collective-permute-done | bytes 442400 | tf_op jit(solution)/shard_map/round3/far/ppermute | solution.py:70
  115.3 30.7 %shard_map.280 = (bf16[512,768]{1,0:T(8,128)(2,1)}, f32[512,768]{1,0:T(8,128)}, bf16[512,768]{1,0:T(8,128)(2,1)}, bf16[4,304,768]{2,1,0:T(8,128)(2,1)}, bf16[4,304,768]{2,1,0:T(8,128)(2,1)}) custom-call(s32[9]{0:T(128)} %pad_add_fusion.spots_ref, bf16[768,128]{1,0:T(8,128)(2,1)} %fusion.member_ref, bf16[128,768]{1,0:T(8,128)(2,1)} %fusion.1.member_t_ref, ...), custom_call_target="tpu_custom_call" | custom-call | flops 11475615744 | bytes 17301504 | tf_op jit(solution)/shard_map/pallas_call | solution.py:752
  146.4 3.9 %collective-permute-done.35.come_hbm.refs_4_ = bf16[4,304,768]{2,1,0:T(8,128)(2,1)} collective-permute-done((bf16[4,304,768]{2,1,0:T(8,128)(2,1)}, bf16[4,304,768]{2,1,0:T(8,128)(2,1)}, u32[]{:S(2)}, u32[]{:S(2)}) %collective-permute-start.35) | collective-permute-done | bytes 1867808 | tf_op jit(solution)/shard_map/cores/ppermute | solution.py:70
  150.3 3.4 %shard_map.281 = (bf16[304,768]{1,0:T(8,128)(2,1)}, bf16[304,768]{1,0:T(8,128)(2,1)}, bf16[304,768]{1,0:T(8,128)(2,1)}) custom-call(s32[9]{0:T(128)} %pad_add_fusion.spots_ref, bf16[4,304,768]{2,1,0:T(8,128)(2,1)} %get-tuple-element.123.keep_hbm.refs_3_, bf16[4,304,768]{2,1,0:T(8,128)(2,1)} %collective-permute-done.35.come_hbm.refs_4_), custom_call_target="tpu_custom_call" | custom-call | tf_op jit(solution)/shard_map/pallas_call | solution.py:350
  157.2 11.8 %shard_map.282 = (f32[512,768]{1,0:T(8,128)}, bf16[512,768]{1,0:T(8,128)(2,1)}) custom-call(s32[9]{0:T(128)} %pad_add_fusion.spots_ref, bf16[512,768]{1,0:T(8,128)(2,1)} %get-tuple-element.109.g_ref, f32[512,1]{1,0:T(8,128)} %get-tuple-element.110.rstd_ref, f32[4,768]{1,0:T(4,128)} %pad_maximum_fusion.2.norms_ref, ...), custom_call_target="tpu_custom_call" | custom-call | flops 4831838208 | bytes 12582912 | tf_op jit(solution)/shard_map/pallas_call | solution.py:839
  169.0 7.9 %shard_map.283 = (bf16[256,768]{1,0:T(8,128)(2,1)}, bf16[256,768]{1,0:T(8,128)(2,1)}, bf16[256,768]{1,0:T(8,128)(2,1)}, bf16[256,768]{1,0:T(8,128)(2,1)}) custom-call(s32[9]{0:T(128)} %pad_add_fusion.spots_ref, bf16[512,768]{1,0:T(8,128)(2,1)} %get-tuple-element.114.refs_0_, bf16[6,96,768]{2,1,0:T(8,128)(2,1)} %copy-done.1, bf16[6,96,768]{2,1,0:T(8,128)(2,1)} %copy-done.6, ...), custom_call_target="tpu_custom_call" | custom-call | flops 1006632960 | bytes 5111808 | tf_op jit(solution)/shard_map/pallas_call | solution.py:935
  178.6 4.0 %shard_map.284 = (f32[80,768]{1,0:T(8,128)}, bf16[80,768]{1,0:T(8,128)(2,1)}, bf16[80,768]{1,0:T(8,128)(2,1)}, bf16[80,768]{1,0:T(8,128)(2,1)}) custom-call(s32[9]{0:T(128)} %pad_add_fusion.spots_ref, bf16[304,768]{1,0:T(8,128)(2,1)} %collective-permute-done.36.refs_0_, bf16[304,768]{1,0:T(8,128)(2,1)} %collective-permute-done.37.refs_1_, ...), custom_call_target="tpu_custom_call" | custom-call | tf_op jit(solution)/shard_map/pallas_call | solution.py:363
  184.9 2.3 %collective-permute-start.41 = (bf16[80,768]{1,0:T(8,128)(2,1)}, bf16[80,768]{1,0:T(8,128)(2,1)S(1)}, u32[]{:S(2)}, u32[]{:S(2)}) collective-permute-start(bf16[80,768]{1,0:T(8,128)(2,1)} %get-tuple-element.130), channel_id=1, source_target_pairs={{0,3},{1,0},{2,1},{3,2},{4,7},{5,4},{6,5},{7,6},{8,11},{9,8},{10,9... | collective-permute-start | bytes 368648 | tf_op jit(solution)/shard_map/stack2/ppermute | solution.py:74
  187.2 9.6 %shard_map.285 = bf16[512,768]{1,0:T(8,128)(2,1)} custom-call(s32[9]{0:T(128)} %pad_add_fusion.spots_ref, f32[512,768]{1,0:T(8,128)} %get-tuple-element.113.refs_0_, bf16[256,768]{1,0:T(8,128)(2,1)} %get-tuple-element.125.refs_1_, bf16[256,768]{1,0:T(8,128)(2,1)} %get-tuple-element.122.refs_2_, bf16[256,768]{1,0:T(8,128)(2,1)} %get-tuple-element.126.refs_3_, ...), custom_call_target="tpu_custom_call" | custom-call | flops 2214592512 | bytes 7471104 | tf_op jit(solution)/shard_map/pallas_call | solution.py:951
  (164 shorter events, 46.9 us)
Async XLA Ops:
  4.5 17.5 %collective-permute-start.1 = (bf16[96,768]{1,0:T(8,128)(2,1)}, bf16[96,768]{1,0:T(8,128)(2,1)S(1)}, u32[]{:S(2)}, u32[]{:S(2)}) collective-permute-start(bf16[96,768]{1,0:T(8,128)(2,1)} %slice_select_fusion), channel_id=1, source_target_pairs={{0,2},{1,3},{2,0},{3,1},{4,6},{5,7},{6,4},{7,5},{8,10},{9,11},{10,... | collective-permute-start | bytes 442376 | tf_op jit(solution)/shard_map/planes0/across/ppermute | solution.py:74
  8.5 13.5 %collective-permute-start = (bf16[192,768]{1,0:T(8,128)(2,1)}, bf16[192,768]{1,0:T(8,128)(2,1)}, u32[]{:S(2)}, u32[]{:S(2)}) collective-permute-start(bf16[192,768]{1,0:T(8,128)(2,1)} %select_select_fusion), channel_id=1, source_target_pairs={{0,3},{1,0},{2,1},{3,2},{4,5},{5,6},{6,7},{7,4},{8,11},{9,8},{10,9... | collective-permute-start | bytes 884744 | tf_op jit(solution)/shard_map/planes0/beside/ppermute | solution.py:79
  10.3 11.7 %collective-permute-start.2 = (bf16[80,768]{1,0:T(8,128)(2,1)S(1)}, bf16[80,768]{1,0:T(8,128)(2,1)S(1)}, u32[]{:S(2)}, u32[]{:S(2)}) collective-permute-start(bf16[80,768]{1,0:T(8,128)(2,1)S(1)} %pad_maximum_fusion.1.refs_4_), channel_id=1, source_target_pairs={{0,4},{4,0},{8,12},{12,8},{16,20},{20,16},{24,28},{28,24},{1,5},{5... | collective-permute-start | bytes 368648 | tf_op jit(solution)/shard_map/ppermute | solution.py:70
  26.0 18.1 %collective-permute-start.7 = (bf16[6,96,768]{2,1,0:T(8,128)(2,1)S(1)}, bf16[6,96,768]{2,1,0:T(8,128)(2,1)S(1)}, u32[]{:S(2)}, u32[]{:S(2)}) collective-permute-start(bf16[6,96,768]{2,1,0:T(8,128)(2,1)S(1)} %round0.1.refs_0_.refs_1_.refs_5_), channel_id=1, source_target_pairs={{0,8},{4,20},{8,0},{12,28},{16,24},{20,4},{24,16},{28,12},{1,9},{5... | collective-permute-start | bytes 2654216 | tf_op jit(solution)/shard_map/round0/near/ppermute | solution.py:70
  27.8 16.3 %collective-permute-start.5 = (bf16[192,768]{1,0:T(8,128)(2,1)S(1)}, bf16[192,768]{1,0:T(8,128)(2,1)S(1)}, u32[]{:S(2)}, u32[]{:S(2)}) collective-permute-start(bf16[192,768]{1,0:T(8,128)(2,1)S(1)} %copy-done.25), channel_id=1, source_target_pairs={{0,3},{1,0},{2,1},{3,2},{4,5},{5,6},{6,7},{7,4},{8,11},{9,8},{10,9... | collective-permute-start | bytes 884744 | tf_op jit(solution)/shard_map/round0/planes1/beside/ppermute | solution.py:79
  29.5 14.7 %collective-permute-start.6 = (bf16[96,768]{1,0:T(8,128)(2,1)S(1)}, bf16[96,768]{1,0:T(8,128)(2,1)S(1)}, u32[]{:S(2)}, u32[]{:S(2)}) collective-permute-start(bf16[96,768]{1,0:T(8,128)(2,1)S(1)} %copy-done.27), channel_id=1, source_target_pairs={{0,2},{1,3},{2,0},{3,1},{4,6},{5,7},{6,4},{7,5},{8,10},{9,11},{10,... | collective-permute-start | bytes 442376 | tf_op jit(solution)/shard_map/round0/planes1/across/ppermute | solution.py:74
  44.7 16.2 %collective-permute-start.14 = (bf16[6,96,768]{2,1,0:T(8,128)(2,1)S(1)}, bf16[6,96,768]{2,1,0:T(8,128)(2,1)S(1)}, u32[]{:S(2)}, u32[]{:S(2)}) collective-permute-start(bf16[6,96,768]{2,1,0:T(8,128)(2,1)S(1)} %collective-permute-done.7.refs_1_.refs_2_.refs_6_), channel_id=1, source_target_pairs={{0,4},{4,0},{8,12},{12,8},{16,20},{20,16},{24,28},{28,24},{1,5},{5... | collective-permute-start | bytes 2654216 | tf_op jit(solution)/shard_map/round1/swap/ppermute | solution.py:70
  46.6 17.9 %collective-permute-start.12 = (bf16[6,96,768]{2,1,0:T(8,128)(2,1)S(1)}, bf16[6,96,768]{2,1,0:T(8,128)(2,1)}, u32[]{:S(2)}, u32[]{:S(2)}) collective-permute-start(bf16[6,96,768]{2,1,0:T(8,128)(2,1)S(1)} %round1.1.refs_0_.refs_9_), channel_id=1, source_target_pairs={{0,8},{4,20},{8,0},{12,28},{16,24},{20,4},{24,16},{28,12},{1,9},{5... | collective-permute-start | bytes 2654216 | tf_op jit(solution)/shard_map/round1/near/ppermute | solution.py:70
  47.2 13.7 %collective-permute-start.13 = (bf16[3,96,768]{2,1,0:T(8,128)(2,1)S(1)}, bf16[3,96,768]{2,1,0:T(8,128)(2,1)S(1)}, u32[]{:S(2)}, u32[]{:S(2)}) collective-permute-start(bf16[3,96,768]{2,1,0:T(8,128)(2,1)S(1)} %slice.26), channel_id=1, source_target_pairs={{0,20},{4,8},{8,28},{12,0},{16,4},{20,24},{24,12},{28,16},{1,21},{... | collective-permute-start | bytes 1327112 | tf_op jit(solution)/shard_map/round1/far/ppermute | solution.py:70
  48.3 12.6 %collective-permute-start.8 = (bf16[160,768]{1,0:T(8,128)(2,1)S(1)}, bf16[160,768]{1,0:T(8,128)(2,1)S(1)}, u32[]{:S(2)}, u32[]{:S(2)}) collective-permute-start(bf16[160,768]{1,0:T(8,128)(2,1)S(1)} %pad_maximum_fusion), channel_id=1, source_target_pairs={{0,3},{1,0},{2,1},{3,2},{4,5},{5,6},{6,7},{7,4},{8,11},{9,8},{10,9... | collective-permute-start | bytes 737288 | tf_op jit(solution)/shard_map/round1/planes2/beside/ppermute | solution.py:79
  67.8 19.2 %collective-permute-start.20 = (bf16[8,80,768]{2,1,0:T(8,128)(2,1)}, bf16[8,80,768]{2,1,0:T(8,128)(2,1)}, u32[]{:S(2)}, u32[]{:S(2)}) collective-permute-start(bf16[8,80,768]{2,1,0:T(8,128)(2,1)} %round2.3.refs_2_), channel_id=1, source_target_pairs={{0,8},{4,20},{8,0},{12,28},{16,24},{20,4},{24,16},{28,12},{1,9},{5... | collective-permute-start | bytes 2949128 | tf_op jit(solution)/shard_map/round2/near/ppermute | solution.py:70
  68.3 18.3 %collective-permute-start.22 = (bf16[6,96,768]{2,1,0:T(8,128)(2,1)}, bf16[6,96,768]{2,1,0:T(8,128)(2,1)}, u32[]{:S(2)}, u32[]{:S(2)}) collective-permute-start(bf16[6,96,768]{2,1,0:T(8,128)(2,1)} %collective-permute-done.12.refs_1_.refs_10_), channel_id=1, source_target_pairs={{0,4},{4,0},{8,12},{12,8},{16,20},{20,16},{24,28},{28,24},{1,5},{5... | collective-permute-start | bytes 2654216 | tf_op jit(solution)/shard_map/round2/swap/ppermute | solution.py:70
  70.6 16.0 %collective-permute-start.21 = (bf16[3,96,768]{2,1,0:T(8,128)(2,1)}, bf16[3,96,768]{2,1,0:T(8,128)(2,1)}, u32[]{:S(2)}, u32[]{:S(2)}) collective-permute-start(bf16[3,96,768]{2,1,0:T(8,128)(2,1)} %slice.27), channel_id=1, source_target_pairs={{0,20},{4,8},{8,28},{12,0},{16,4},{20,24},{24,12},{28,16},{1,21},{... | collective-permute-start | bytes 1327112 | tf_op jit(solution)/shard_map/round2/far/ppermute | solution.py:70
  71.9 14.8 %collective-permute-start.16 = (bf16[192,768]{1,0:T(8,128)(2,1)}, bf16[192,768]{1,0:T(8,128)(2,1)S(1)}, u32[]{:S(2)}, u32[]{:S(2)}) collective-permute-start(bf16[192,768]{1,0:T(8,128)(2,1)} %get-tuple-element.92), channel_id=1, source_target_pairs={{0,3},{1,0},{2,1},{3,2},{4,5},{5,6},{6,7},{7,4},{8,11},{9,8},{10,9... | collective-permute-start | bytes 884744 | tf_op jit(solution)/shard_map/round2/planes3/beside/ppermute | solution.py:79
  73.2 13.4 %collective-permute-start.17 = (bf16[96,768]{1,0:T(8,128)(2,1)S(1)}, bf16[96,768]{1,0:T(8,128)(2,1)S(1)}, u32[]{:S(2)}, u32[]{:S(2)}) collective-permute-start(bf16[96,768]{1,0:T(8,128)(2,1)S(1)} %copy-done.26), channel_id=1, source_target_pairs={{0,2},{1,3},{2,0},{3,1},{4,6},{5,7},{6,4},{7,5},{8,10},{9,11},{10,... | collective-permute-start | bytes 442376 | tf_op jit(solution)/shard_map/round2/planes3/across/ppermute | solution.py:74
  87.0 16.3 %collective-permute-start.25 = (bf16[8,80,768]{2,1,0:T(8,128)(2,1)}, bf16[8,80,768]{2,1,0:T(8,128)(2,1)}, u32[]{:S(2)}, u32[]{:S(2)}) collective-permute-start(bf16[8,80,768]{2,1,0:T(8,128)(2,1)} %collective-permute-done.20.refs_3_), channel_id=1, source_target_pairs={{0,4},{4,0},{8,12},{12,8},{16,20},{20,16},{24,28},{28,24},{1,5},{5... | collective-permute-start | bytes 2949128 | tf_op jit(solution)/shard_map/round3/swap/ppermute | solution.py:70
  89.8 13.2 %collective-permute-start.24 = (bf16[4,80,768]{2,1,0:T(8,128)(2,1)}, bf16[4,80,768]{2,1,0:T(8,128)(2,1)S(1)}, u32[]{:S(2)}, u32[]{:S(2)}) collective-permute-start(bf16[4,80,768]{2,1,0:T(8,128)(2,1)} %slice.28), channel_id=1, source_target_pairs={{0,20},{4,8},{8,28},{12,0},{16,4},{20,24},{24,12},{28,16},{1,21},{... | collective-permute-start | bytes 1474568 | tf_op jit(solution)/shard_map/round3/far/ppermute | solution.py:70
  93.3 16.5 %collective-permute-start.30 = (bf16[3,96,768]{2,1,0:T(8,128)(2,1)}, bf16[3,96,768]{2,1,0:T(8,128)(2,1)}, u32[]{:S(2)}, u32[]{:S(2)}) collective-permute-start(bf16[3,96,768]{2,1,0:T(8,128)(2,1)} %get-tuple-element.102.refs_8_.refs_1_), channel_id=1, source_target_pairs={{0,8},{4,20},{8,0},{12,28},{16,24},{20,4},{24,16},{28,12},{1,9},{5... | collective-permute-start | bytes 1327112 | tf_op jit(solution)/shard_map/round3/near/ppermute | solution.py:70
  153.6 24.2 %collective-permute-start.38 = (bf16[304,768]{1,0:T(8,128)(2,1)}, bf16[304,768]{1,0:T(8,128)(2,1)S(1)}, u32[]{:S(2)}, u32[]{:S(2)}) collective-permute-start(bf16[304,768]{1,0:T(8,128)(2,1)} %get-tuple-element.108), channel_id=1, source_target_pairs={{0,24},{4,28},{8,16},{12,20},{16,8},{20,12},{24,0},{28,4},{1,25},{... | collective-permute-start | bytes 1400840 | tf_op jit(solution)/shard_map/far/ppermute | solution.py:70
  155.2 22.3 %collective-permute-start.36 = (bf16[304,768]{1,0:T(8,128)(2,1)}, bf16[304,768]{1,0:T(8,128)(2,1)}, u32[]{:S(2)}, u32[]{:S(2)}) collective-permute-start(bf16[304,768]{1,0:T(8,128)(2,1)} %get-tuple-element.120), channel_id=1, source_target_pairs={{0,8},{4,12},{8,0},{12,4},{16,24},{20,28},{24,16},{28,20},{1,9},{5... | collective-permute-start | bytes 1400840 | tf_op jit(solution)/shard_map/x/ppermute | solution.py:70
  156.3 21.5 %collective-permute-start.37 = (bf16[304,768]{1,0:T(8,128)(2,1)}, bf16[304,768]{1,0:T(8,128)(2,1)}, u32[]{:S(2)}, u32[]{:S(2)}) collective-permute-start(bf16[304,768]{1,0:T(8,128)(2,1)} %get-tuple-element.121), channel_id=1, source_target_pairs={{0,16},{4,20},{8,24},{12,28},{16,0},{20,4},{24,8},{28,12},{1,17},{... | collective-permute-start | bytes 1400840 | tf_op jit(solution)/shard_map/y/ppermute | solution.py:70
  182.6 14.2 %collective-permute-start.39 = (bf16[80,768]{1,0:T(8,128)(2,1)}, bf16[80,768]{1,0:T(8,128)(2,1)S(1)}, u32[]{:S(2)}, u32[]{:S(2)}) collective-permute-start(bf16[80,768]{1,0:T(8,128)(2,1)} %get-tuple-element.128), channel_id=1, source_target_pairs={{0,1},{1,2},{2,3},{3,0},{4,5},{5,6},{6,7},{7,4},{8,9},{9,10},{10,1... | collective-permute-start | bytes 368648 | tf_op jit(solution)/shard_map/stack0/ppermute | solution.py:74
  183.9 12.9 %collective-permute-start.40 = (bf16[80,768]{1,0:T(8,128)(2,1)}, bf16[80,768]{1,0:T(8,128)(2,1)S(1)}, u32[]{:S(2)}, u32[]{:S(2)}) collective-permute-start(bf16[80,768]{1,0:T(8,128)(2,1)} %get-tuple-element.129), channel_id=1, source_target_pairs={{0,2},{1,3},{2,0},{3,1},{4,6},{5,7},{6,4},{7,5},{8,10},{9,11},{10,... | collective-permute-start | bytes 368648 | tf_op jit(solution)/shard_map/stack1/ppermute | solution.py:74
  184.9 11.9 %collective-permute-start.41 = (bf16[80,768]{1,0:T(8,128)(2,1)}, bf16[80,768]{1,0:T(8,128)(2,1)S(1)}, u32[]{:S(2)}, u32[]{:S(2)}) collective-permute-start(bf16[80,768]{1,0:T(8,128)(2,1)} %get-tuple-element.130), channel_id=1, source_target_pairs={{0,3},{1,0},{2,1},{3,2},{4,7},{5,4},{6,5},{7,6},{8,11},{9,8},{10,9... | collective-permute-start | bytes 368648 | tf_op jit(solution)/shard_map/stack2/ppermute | solution.py:74
  (48 other events, 382.9 us)

commit v2 on v1

--- a/solution.py
+++ b/solution.py
@@ -880,68 +880,81 @@
     return begin(pairs, sems)
 
 
+def input_rows(g1, grads, weights):
+    total = g1
+    for grad, weight in zip(grads, weights):
+        total = total + mm(grad, weight)
+    return total.astype(BF)
+
+
 def attention_back_first_kernel(spots_ref, *refs):
-    *refs, ctx_hbm, dq_ref, dk_ref, dv_ref, w_ref, g1_ref, ctx_ref, q_ref, k_ref, v_ref, p_ref, w_sems, sems, g_sems = refs
-    g1_hbm, *sources, q_hbm, k_hbm, v_hbm, p_hbm = refs
+    *refs, ctx_hbm, out_ref, w_ref, low_ref, g1_ref, ctx_ref, q_ref, k_ref, v_ref, p_ref, dq_ref, dk_ref, dv_ref, w_sems, sems, g_sems = refs
+    low_hbm, g1_hbm, *sources, q_hbm, k_hbm, v_hbm, p_hbm = refs
     seq_len = p_ref.shape[1]
-    rows, dim = g1_ref.shape
-    loads = begin(((g1_hbm, g1_ref),), g_sems.at[pl.ds(0, 1)])
+    rows, dim = low_ref.shape
+    loads = begin(((low_hbm, low_ref),), g_sems.at[pl.ds(0, 1)])
     fetch_stacked(spots_ref, sources, w_ref, w_sems, True)
     seqs = q_ref.shape[0] // seq_len
     loads += load_heads((q_hbm, k_hbm, v_hbm, p_hbm), (q_ref, k_ref, v_ref, p_ref), sems, 0, seqs)
     loads[0].wait()
     arrive_stacked(w_ref, w_sems, 3)
-    ctx_ref[...] = mm_t(g1_ref[...], w_ref[3]).astype(BF)
-    later = pl.ds(seqs * seq_len, rows - seqs * seq_len)
+    ctx_ref[...] = mm_t(low_ref[...], w_ref[3]).astype(BF)
+    mine, later = pl.ds(0, seqs * seq_len), pl.ds(seqs * seq_len, rows - seqs * seq_len)
     store = begin(((ctx_ref.at[later], ctx_hbm),), g_sems.at[pl.ds(1, 1)])[0]
     for load in loads[1:]:
         load.wait()
+    fetch_stacked(spots_ref, sources, w_ref, w_sems, False)
+    load = begin(((g1_hbm.at[mine], g1_ref),), g_sems.at[pl.ds(2, 1)])[0]
     for s in range(seqs):
         attention_back_heads(s, seq_len, q_ref, k_ref, v_ref, p_ref, ctx_ref, dq_ref, dk_ref, dv_ref, 0)
+    load.wait()
+    for m in range(3):
+        arrive_stacked(w_ref, w_sems, m)
+    out_ref[...] = input_rows(g1_ref[...], (dq_ref[...], dk_ref[...], dv_ref[...]), (w_ref[0], w_ref[1], w_ref[2]))
     store.wait()
 
 
 def attention_back_last_kernel(spots_ref, *refs):
-    *refs, out_ref, g1_ref, ctx_ref, dq0_ref, dk0_ref, dv0_ref, w_ref, q_ref, k_ref, v_ref, p_ref, dq_ref, dk_ref, dv_ref, w_sems, sems, late_sems = refs
-    g1_hbm, ctx_hbm, dq0_hbm, dk0_hbm, dv0_hbm, *sources, q_hbm, k_hbm, v_hbm, p_hbm = refs
-    rows, dim = g1_ref.shape
+    *refs, out_ref, g1_ref, ctx_ref, first_ref, w_ref, q_ref, k_ref, v_ref, p_ref, dq_ref, dk_ref, dv_ref, w_sems, sems, late_sems = refs
+    g1_hbm, ctx_hbm, first_hbm, *sources, q_hbm, k_hbm, v_hbm, p_hbm = refs
+    rows = out_ref.shape[0]
     seq_len = p_ref.shape[1]
-    first = dq0_ref.shape[0] // seq_len
+    first = first_ref.shape[0] // seq_len
     seqs = q_ref.shape[0] // seq_len
     loads = begin(((ctx_hbm, ctx_ref),), late_sems.at[pl.ds(0, 1)])
     loads += load_heads((q_hbm, k_hbm, v_hbm, p_hbm), (q_ref, k_ref, v_ref, p_ref), sems, first, seqs)
     for load in loads:
         load.wait()
     fetch_stacked(spots_ref, sources, w_ref, w_sems, False)
-    pairs = ((dq0_hbm, dq0_ref), (dk0_hbm, dk0_ref), (dv0_hbm, dv0_ref), (g1_hbm, g1_ref))
-    loads = begin(pairs, late_sems.at[pl.ds(1, 4)])
+    later = pl.ds(first * seq_len, seqs * seq_len)
+    loads = begin(((g1_hbm.at[later], g1_ref), (first_hbm, first_ref)), late_sems.at[pl.ds(1, 2)])
     for s in range(seqs):
         attention_back_heads(s, seq_len, q_ref, k_ref, v_ref, p_ref, ctx_ref, dq_ref, dk_ref, dv_ref, 0)
     for load in loads:
         load.wait()
     for m in range(3):
         arrive_stacked(w_ref, w_sems, m)
-    for at, grads in ((slice(0, first * seq_len), (dq0_ref, dk0_ref, dv0_ref)), (slice(first * seq_len, rows), (dq_ref, dk_ref, dv_ref))):
-        total = g1_ref[at, :]
-        for m, grad in enumerate(grads):
-            total = total + mm(grad[...], w_ref[m])
-        out_ref[at, :] = total.astype(BF)
-
-
-def attention_backward_first(spots, g1_low, sources, q, k, v, probs):
-    rows, dim = g1_low.shape
+    out_ref[: first * seq_len, :] = first_ref[...]
+    out_ref[first * seq_len : rows, :] = input_rows(
+        g1_ref[...], (dq_ref[...], dk_ref[...], dv_ref[...]), (w_ref[0], w_ref[1], w_ref[2])
+    )
+
+
+def attention_backward_first(spots, g1_low, g1, sources, q, k, v, probs):
+    rows, dim = g1.shape
     heads, seq_len = probs.shape[0] // 2, probs.shape[1]
     half, low = jax.ShapeDtypeStruct((rows // 2, dim), BF), pltpu.VMEM((rows // 2, dim), BF)
     return pl.pallas_call(
         attention_back_first_kernel,
-        out_shape=[half, half, half, half],
-        in_specs=[SMEM, ANY] + [ANY] * (len(sources) + 4),
-        out_specs=[ANY] + [VMEM] * 3,
-        scratch_shapes=[pltpu.VMEM((4, dim, dim), BF), pltpu.VMEM((rows, dim), BF), pltpu.VMEM((rows, dim), BF), low, low, low, pltpu.VMEM((heads,) + probs.shape[1:], BF),
-                        WEIGHT_SEMS, pltpu.SemaphoreType.DMA((4,)), pltpu.SemaphoreType.DMA((2,))],
+        out_shape=[half, half],
+        in_specs=[SMEM] + [ANY] * (len(sources) + 6),
+        out_specs=[ANY, VMEM],
+        scratch_shapes=[pltpu.VMEM((4, dim, dim), BF), pltpu.VMEM((rows, dim), BF), pltpu.VMEM((rows // 2, dim), F32),
+                        pltpu.VMEM((rows, dim), BF), low, low, low, pltpu.VMEM((heads,) + probs.shape[1:], BF), low, low, low,
+                        WEIGHT_SEMS, pltpu.SemaphoreType.DMA((4,)), pltpu.SemaphoreType.DMA((3,))],
         compiler_params=limit(60),
-        cost_estimate=cost(2 * rows * dim * (dim + 2 * seq_len), 2 * (dim * dim + 5 * rows * dim)),
-    )(spots, g1_low, *sources, q, k, v, probs)
+        cost_estimate=cost(2 * rows * dim * (3 * dim + 2 * seq_len), 2 * (4 * dim * dim + 5 * rows * dim)),
+    )(spots, g1_low, g1, *sources, q, k, v, probs)
 
 
 def attention_backward_last(spots, g1, halfway, sources, q, k, v, probs):
@@ -951,12 +964,13 @@
     return pl.pallas_call(
         attention_back_last_kernel,
         out_shape=jax.ShapeDtypeStruct((rows, dim), BF),
-        in_specs=[SMEM] + [ANY] * (len(sources) + 9),
+        in_specs=[SMEM] + [ANY] * (len(sources) + 7),
         out_specs=VMEM,
-        scratch_shapes=[pltpu.VMEM((rows, dim), F32), low, low, low, low, pltpu.VMEM((4, dim, dim), BF), low, low, low, pltpu.VMEM((heads,) + probs.shape[1:], BF), low, low, low,
-                        WEIGHT_SEMS, pltpu.SemaphoreType.DMA((4,)), pltpu.SemaphoreType.DMA((5,))],
+        scratch_shapes=[pltpu.VMEM((rows // 2, dim), F32), low, low, pltpu.VMEM((4, dim, dim), BF), low, low, low,
+                        pltpu.VMEM((heads,) + probs.shape[1:], BF), low, low, low,
+                        WEIGHT_SEMS, pltpu.SemaphoreType.DMA((4,)), pltpu.SemaphoreType.DMA((3,))],
         compiler_params=limit(60),
-        cost_estimate=cost(2 * rows * dim * (3 * dim + 2 * seq_len), 2 * (3 * dim * dim + 5 * rows * dim)),
+        cost_estimate=cost(2 * rows * dim * (2 * dim + 2 * seq_len), 2 * (3 * dim * dim + 4 * rows * dim)),
     )(spots, g1, *halfway, *sources, q, k, v, probs)
 
 
@@ -1050,8 +1064,8 @@
         def between(start):
             gradient = g_ffn if start is None else tie(g_ffn, start)
             done["g1"], g1_low = ffn_backward(spots, gradient, slope, out_sources, in_sources, g2, xhat1, rstd1, norms)
-            done["half"] = attention_backward_first(spots, g1_low, att_sources, q, k, v, probs)
-            return done["half"][1]
+            done["half"] = attention_backward_first(spots, g1_low, done["g1"], att_sources, q, k, v, probs)
+            return done["half"][0]
 
         def at_last(start):
             halfway = done["half"] if start is None else [tie(done["half"][0], start)] + list(done["half"][1:])

time: 202 us -> 201 us (level)
  transfers between devices with their start and end apart: 42 -> 42, of which waited for: 15 -> 13; matrix products, arithmetic and copies ran while one was open for 6% -> 6% of each run, Pallas kernels for 28% -> 28%
where the time goes in v2:
time: 201 us; the launch traced here: 197 us
  Pallas kernels  96.1 us (48%)
  waiting for transfers between devices  46 us (23%)
  starting transfers between devices  32.4 us (16%)
  local copies, waits for them, and re-layouts  11.6 us (6%)
  other arithmetic  9.57 us (5%)
    pallas_call x1, Pallas kernels, joining(): pl.pallas_call(partial(joining_kernel, halves=halves, count=len(join_sour...  30.7 us
    ppermute x7, waiting for transfers between devices, shift(): lax.ppermute(array, 'tensor', [(i, (i + by) % groups) for i in range(grou...  25.6 us
    ppermute x31, waiting for transfers between devices, send(): return lax.ppermute(array, 'dp', pairs)  20.4 us
    ppermute x31, starting transfers between devices, send(): return lax.ppermute(array, 'dp', pairs)  17.4 us
    pallas_call x1, Pallas kernels, attention_forward(): pl.pallas_call(attention_kernel, out_shape=[low, low, low, jax.ShapeDtype...  12.2 us
    pallas_call x1, Pallas kernels, ffn_backward(): pl.pallas_call(partial(ffn_back_kernel, count=(len(out_sources), len(in_s...  11.8 us
    pallas_call x1, Pallas kernels, attention_backward_first(): pl.pallas_call(attention_back_first_kernel, out_shape=[half, half], in_sp...  9.16 us
    ppermute x7, starting transfers between devices, shift(): lax.ppermute(array, 'tensor', [(i, (i + by) % groups) for i in range(grou...  9.11 us
  transfers between devices with their start and end apart: 42, of which 13 were waited for; matrix products, arithmetic and copies ran while one was open for 6% of the time, Pallas kernels for 28%

profile of v2, /device:TPU:0, one launch (start us, length us, event | category | flops | bytes accessed | tf_op | source)
XLA Modules:
  0.0 197.2 jit_solution(17428273156211449413)
XLA Ops:
  0.8 2.1 %select_select_fusion = bf16[192,768]{1,0:T(8,128)(2,1)} fusion(bf16[192,768]{1,0:T(8,128)(2,1)} %refs_11_.1, pred[]{:T(512)S(6)} %eq.63, pred[]{:T(512)S(6)} %eq.62, pred[]{:T(512)S(6)} %eq.61, bf16[768,192]{0,1:T(8,128)(2,1)} %param.28, bf16[768,192]{0,1:T(8,128)(2,1)} %param.29, bf16[768,192]{0,1:T(8,128)(2,1)} %param.30), kind=kLoop, calls=%fused_computation.4 | loop fusion | flops 442368 | bytes 1474563 | tf_op jit(solution)/shard_map/jit(_where)/select_n | solution.py:1034
  2.8 1.7 slice_select_fusion
  4.5 4.0 %collective-permute-start.1 = (bf16[96,768]{1,0:T(8,128)(2,1)}, bf16[96,768]{1,0:T(8,128)(2,1)S(1)}, u32[]{:S(2)}, u32[]{:S(2)}) collective-permute-start(bf16[96,768]{1,0:T(8,128)(2,1)} %slice_select_fusion), channel_id=1, source_target_pairs={{0,2},{1,3},{2,0},{3,1},{4,6},{5,7},{6,4},{7,5},{8,10},{9,11},{10,... | collective-permute-start | bytes 442376 | tf_op jit(solution)/shard_map/planes0/across/ppermute | solution.py:74
  17.6 2.8 %shard_map.279 = (bf16[192,768]{1,0:T(8,128)(2,1)}, bf16[96,768]{1,0:T(8,128)(2,1)}, bf16[192,768]{1,0:T(8,128)(2,1)}, bf16[96,768]{1,0:T(8,128)(2,1)}) custom-call(s32[9]{0:T(128)} %pad_add_fusion.spots_ref, bf16[768,768]{1,0:T(8,128)(2,1)} %refs_14_.1, bf16[768,768]{1,0:T(8,128)(2,1)} %refs_8_.3), custom_call_target="tpu_custom_call" | custom-call | tf_op jit(solution)/shard_map/pallas_call | solution.py:195
  26.0 1.8 collective-permute-start.7
  27.8 1.6 collective-permute-start.5
  30.0 14.2 %collective-permute-done.6.refs_1_ = bf16[96,768]{1,0:T(8,128)(2,1)S(1)} collective-permute-done((bf16[96,768]{1,0:T(8,128)(2,1)S(1)}, bf16[96,768]{1,0:T(8,128)(2,1)S(1)}, u32[]{:S(2)}, u32[]{:S(2)}) %collective-permute-start.6) | collective-permute-done | bytes 147488 | tf_op jit(solution)/shard_map/round0/planes1/across/ppermute | solution.py:74
  48.3 1.6 collective-permute-start.8
  49.9 11.0 %collective-permute-done.9.refs_1_ = bf16[80,768]{1,0:T(8,128)(2,1)S(1)} collective-permute-done((bf16[80,768]{1,0:T(8,128)(2,1)S(1)}, bf16[80,768]{1,0:T(8,128)(2,1)S(1)}, u32[]{:S(2)}, u32[]{:S(2)}) %collective-permute-start.9) | collective-permute-done | bytes 122912 | tf_op jit(solution)/shard_map/round1/planes2/across/ppermute | solution.py:74
  60.9 3.6 %collective-permute-done.12.refs_1_.refs_10_ = bf16[6,96,768]{2,1,0:T(8,128)(2,1)} collective-permute-done((bf16[6,96,768]{2,1,0:T(8,128)(2,1)S(1)}, bf16[6,96,768]{2,1,0:T(8,128)(2,1)}, u32[]{:S(2)}, u32[]{:S(2)}) %collective-permute-start.12) | collective-permute-done | bytes 884768 | tf_op jit(solution)/shard_map/round1/near/ppermute | solution.py:70
  68.8 1.8 slice.27
  74.0 12.2 %round2.2 = (bf16[512,768]{1,0:T(8,128)(2,1)}, bf16[512,768]{1,0:T(8,128)(2,1)}, bf16[512,768]{1,0:T(8,128)(2,1)}, bf16[24,256,256]{2,1,0:T(8,128)(2,1)}, bf16[5...) custom-call(s32[9]{0:T(128)} %pad_add_fusion.spots_ref, s32[2]{0:T(128)} %dynamic_slice.13.len_ref, ...), custom_call_target="tpu_custom_call" | custom-call | flops 2818572288 | bytes 11010048 | tf_op jit(solution)/shard_map/round2/pallas_call | solution.py:439
  88.0 1.8 slice.28
  94.5 8.6 %round3.2 = (bf16[512,3072]{1,0:T(8,128)(2,1)}, bf16[512,3072]{1,0:T(8,128)(2,1)}) custom-call(s32[9]{0:T(128)} %pad_add_fusion.spots_ref, bf16[512,768]{1,0:T(8,128)(2,1)} %get-tuple-element.87.x_ref, f32[4,1,768]{2,1,0:T(1,128)} %bitcast.32, bf16[6,96,768]{2,1,0:T(8,128)(2,1)} %copy-done.2, bf16[6,96,768]{2,1,0:T(8,128)(2,1)} %collective-permute-done.12.refs_1_.refs_10_, ...), custom_call_target="tpu_custom_call" | custom-call | flops 2415919104 | bytes 11010048 | tf_op jit(solution)/shard_map/round3/pallas_call | solution.py:483
  104.5 5.3 %collective-permute-done.30.refs_10_.refs_3_ = bf16[3,96,768]{2,1,0:T(8,128)(2,1)} collective-permute-done((bf16[3,96,768]{2,1,0:T(8,128)(2,1)}, bf16[3,96,768]{2,1,0:T(8,128)(2,1)}, u32[]{:S(2)}, u32[]{:S(2)}) %collective-permute-start.30) | collective-permute-done | bytes 442400 | tf_op jit(solution)/shard_map/round3/near/ppermute | solution.py:70
  110.3 2.5 %collective-permute-done.31.refs_11_.refs_4_ = bf16[3,96,768]{2,1,0:T(8,128)(2,1)S(1)} collective-permute-done((bf16[3,96,768]{2,1,0:T(8,128)(2,1)S(1)}, bf16[3,96,768]{2,1,0:T(8,128)(2,1)S(1)}, u32[]{:S(2)}, u32[]{:S(2)}) %collective-permute-start.31) | collective-permute-done | bytes 442400 | tf_op jit(solution)/shard_map/round3/far/ppermute | solution.py:70
  115.3 30.7 %shard_map.280 = (bf16[512,768]{1,0:T(8,128)(2,1)}, f32[512,768]{1,0:T(8,128)}, bf16[512,768]{1,0:T(8,128)(2,1)}, bf16[4,304,768]{2,1,0:T(8,128)(2,1)}, bf16[4,304,768]{2,1,0:T(8,128)(2,1)}) custom-call(s32[9]{0:T(128)} %pad_add_fusion.spots_ref, bf16[768,128]{1,0:T(8,128)(2,1)} %fusion.member_ref, bf16[128,768]{1,0:T(8,128)(2,1)} %fusion.1.member_t_ref, ...), custom_call_target="tpu_custom_call" | custom-call | flops 11475615744 | bytes 17301504 | tf_op jit(solution)/shard_map/pallas_call | solution.py:752
  146.4 3.9 %collective-permute-done.35.come_hbm.refs_4_ = bf16[4,304,768]{2,1,0:T(8,128)(2,1)} collective-permute-done((bf16[4,304,768]{2,1,0:T(8,128)(2,1)}, bf16[4,304,768]{2,1,0:T(8,128)(2,1)}, u32[]{:S(2)}, u32[]{:S(2)}) %collective-permute-start.35) | collective-permute-done | bytes 1867808 | tf_op jit(solution)/shard_map/cores/ppermute | solution.py:70
  150.3 3.4 %shard_map.281 = (bf16[304,768]{1,0:T(8,128)(2,1)}, bf16[304,768]{1,0:T(8,128)(2,1)}, bf16[304,768]{1,0:T(8,128)(2,1)}) custom-call(s32[9]{0:T(128)} %pad_add_fusion.spots_ref, bf16[4,304,768]{2,1,0:T(8,128)(2,1)} %get-tuple-element.120.keep_hbm.refs_3_, bf16[4,304,768]{2,1,0:T(8,128)(2,1)} %collective-permute-done.35.come_hbm.refs_4_), custom_call_target="tpu_custom_call" | custom-call | tf_op jit(solution)/shard_map/pallas_call | solution.py:350
  157.2 11.8 %shard_map.282 = (f32[512,768]{1,0:T(8,128)}, bf16[512,768]{1,0:T(8,128)(2,1)}) custom-call(s32[9]{0:T(128)} %pad_add_fusion.spots_ref, bf16[512,768]{1,0:T(8,128)(2,1)} %get-tuple-element.107.g_ref, f32[512,1]{1,0:T(8,128)} %get-tuple-element.108.rstd_ref, f32[4,768]{1,0:T(4,128)} %pad_maximum_fusion.2.norms_ref, ...), custom_call_target="tpu_custom_call" | custom-call | flops 4831838208 | bytes 12582912 | tf_op jit(solution)/shard_map/pallas_call | solution.py:839
  169.0 9.2 %shard_map.283 = (bf16[256,768]{1,0:T(8,128)(2,1)}, bf16[256,768]{1,0:T(8,128)(2,1)}) custom-call(s32[9]{0:T(128)} %pad_add_fusion.spots_ref, bf16[512,768]{1,0:T(8,128)(2,1)} %get-tuple-element.112.refs_0_, f32[512,768]{1,0:T(8,128)} %get-tuple-element.111.refs_1_.refs_0_, bf16[6,96,768]{2,1,0:T(8,128)(2,1)} %copy-done.1, bf16[6,96,768]{2,1,0:T(8,128)(2,1)} %copy-done.6, ...), custom_call_target="tpu_custom_call" | custom-call | flops 2214592512 | bytes 8650752 | tf_op jit(solution)/shard_map/pallas_call | solution.py:947
  179.0 3.7 %shard_map.284 = (f32[80,768]{1,0:T(8,128)}, bf16[80,768]{1,0:T(8,128)(2,1)}, bf16[80,768]{1,0:T(8,128)(2,1)}, bf16[80,768]{1,0:T(8,128)(2,1)}) custom-call(s32[9]{0:T(128)} %pad_add_fusion.spots_ref, bf16[304,768]{1,0:T(8,128)(2,1)} %collective-permute-done.36.refs_0_, bf16[304,768]{1,0:T(8,128)(2,1)} %collective-permute-done.37.refs_1_, ...), custom_call_target="tpu_custom_call" | custom-call | tf_op jit(solution)/shard_map/pallas_call | solution.py:363
  185.1 2.1 %collective-permute-start.41 = (bf16[80,768]{1,0:T(8,128)(2,1)}, bf16[80,768]{1,0:T(8,128)(2,1)S(1)}, u32[]{:S(2)}, u32[]{:S(2)}) collective-permute-start(bf16[80,768]{1,0:T(8,128)(2,1)} %get-tuple-element.126), channel_id=1, source_target_pairs={{0,3},{1,0},{2,1},{3,2},{4,7},{5,4},{6,5},{7,6},{8,11},{9,8},{10,9... | collective-permute-start | bytes 368648 | tf_op jit(solution)/shard_map/stack2/ppermute | solution.py:74
  187.2 8.3 %shard_map.285 = bf16[512,768]{1,0:T(8,128)(2,1)} custom-call(s32[9]{0:T(128)} %pad_add_fusion.spots_ref, f32[512,768]{1,0:T(8,128)} %get-tuple-element.111.refs_1_.refs_0_, bf16[256,768]{1,0:T(8,128)(2,1)} %get-tuple-element.122.refs_1_, bf16[256,768]{1,0:T(8,128)(2,1)} %get-tuple-element.123.refs_2_, bf16[6,96,768]{2,1,0:T(8,128)(2,1)} %copy-done.1, ...), custom_call_target="tpu_custom_call" | custom-call | flops 1610612736 | bytes 6684672 | tf_op jit(solution)/shard_map/pallas_call | solution.py:964
  (164 shorter events, 46.1 us)
Async XLA Ops:
  4.5 17.5 %collective-permute-start.1 = (bf16[96,768]{1,0:T(8,128)(2,1)}, bf16[96,768]{1,0:T(8,128)(2,1)S(1)}, u32[]{:S(2)}, u32[]{:S(2)}) collective-permute-start(bf16[96,768]{1,0:T(8,128)(2,1)} %slice_select_fusion), channel_id=1, source_target_pairs={{0,2},{1,3},{2,0},{3,1},{4,6},{5,7},{6,4},{7,5},{8,10},{9,11},{10,... | collective-permute-start | bytes 442376 | tf_op jit(solution)/shard_map/planes0/across/ppermute | solution.py:74
  8.5 13.5 %collective-permute-start = (bf16[192,768]{1,0:T(8,128)(2,1)}, bf16[192,768]{1,0:T(8,128)(2,1)}, u32[]{:S(2)}, u32[]{:S(2)}) collective-permute-start(bf16[192,768]{1,0:T(8,128)(2,1)} %select_select_fusion), channel_id=1, source_target_pairs={{0,3},{1,0},{2,1},{3,2},{4,5},{5,6},{6,7},{7,4},{8,11},{9,8},{10,9... | collective-permute-start | bytes 884744 | tf_op jit(solution)/shard_map/planes0/beside/ppermute | solution.py:79
  10.3 11.7 %collective-permute-start.2 = (bf16[80,768]{1,0:T(8,128)(2,1)S(1)}, bf16[80,768]{1,0:T(8,128)(2,1)S(1)}, u32[]{:S(2)}, u32[]{:S(2)}) collective-permute-start(bf16[80,768]{1,0:T(8,128)(2,1)S(1)} %pad_maximum_fusion.1.refs_4_), channel_id=1, source_target_pairs={{0,4},{4,0},{8,12},{12,8},{16,20},{20,16},{24,28},{28,24},{1,5},{5... | collective-permute-start | bytes 368648 | tf_op jit(solution)/shard_map/ppermute | solution.py:70
  26.0 18.1 %collective-permute-start.7 = (bf16[6,96,768]{2,1,0:T(8,128)(2,1)S(1)}, bf16[6,96,768]{2,1,0:T(8,128)(2,1)S(1)}, u32[]{:S(2)}, u32[]{:S(2)}) collective-permute-start(bf16[6,96,768]{2,1,0:T(8,128)(2,1)S(1)} %round0.1.refs_0_.refs_2_.refs_3_), channel_id=1, source_target_pairs={{0,8},{4,20},{8,0},{12,28},{16,24},{20,4},{24,16},{28,12},{1,9},{5... | collective-permute-start | bytes 2654216 | tf_op jit(solution)/shard_map/round0/near/ppermute | solution.py:70
  27.8 16.3 %collective-permute-start.5 = (bf16[192,768]{1,0:T(8,128)(2,1)S(1)}, bf16[192,768]{1,0:T(8,128)(2,1)S(1)}, u32[]{:S(2)}, u32[]{:S(2)}) collective-permute-start(bf16[192,768]{1,0:T(8,128)(2,1)S(1)} %copy-done.25), channel_id=1, source_target_pairs={{0,3},{1,0},{2,1},{3,2},{4,5},{5,6},{6,7},{7,4},{8,11},{9,8},{10,9... | collective-permute-start | bytes 884744 | tf_op jit(solution)/shard_map/round0/planes1/beside/ppermute | solution.py:79
  29.5 14.7 %collective-permute-start.6 = (bf16[96,768]{1,0:T(8,128)(2,1)S(1)}, bf16[96,768]{1,0:T(8,128)(2,1)S(1)}, u32[]{:S(2)}, u32[]{:S(2)}) collective-permute-start(bf16[96,768]{1,0:T(8,128)(2,1)S(1)} %copy-done.27), channel_id=1, source_target_pairs={{0,2},{1,3},{2,0},{3,1},{4,6},{5,7},{6,4},{7,5},{8,10},{9,11},{10,... | collective-permute-start | bytes 442376 | tf_op jit(solution)/shard_map/round0/planes1/across/ppermute | solution.py:74
  44.7 16.2 %collective-permute-start.14 = (bf16[6,96,768]{2,1,0:T(8,128)(2,1)S(1)}, bf16[6,96,768]{2,1,0:T(8,128)(2,1)S(1)}, u32[]{:S(2)}, u32[]{:S(2)}) collective-permute-start(bf16[6,96,768]{2,1,0:T(8,128)(2,1)S(1)} %collective-permute-done.7.refs_1_.refs_3_.refs_4_), channel_id=1, source_target_pairs={{0,4},{4,0},{8,12},{12,8},{16,20},{20,16},{24,28},{28,24},{1,5},{5... | collective-permute-start | bytes 2654216 | tf_op jit(solution)/shard_map/round1/swap/ppermute | solution.py:70
  46.6 17.9 %collective-permute-start.12 = (bf16[6,96,768]{2,1,0:T(8,128)(2,1)S(1)}, bf16[6,96,768]{2,1,0:T(8,128)(2,1)}, u32[]{:S(2)}, u32[]{:S(2)}) collective-permute-start(bf16[6,96,768]{2,1,0:T(8,128)(2,1)S(1)} %round1.1.refs_0_.refs_9_), channel_id=1, source_target_pairs={{0,8},{4,20},{8,0},{12,28},{16,24},{20,4},{24,16},{28,12},{1,9},{5... | collective-permute-start | bytes 2654216 | tf_op jit(solution)/shard_map/round1/near/ppermute | solution.py:70
  47.2 13.7 %collective-permute-start.13 = (bf16[3,96,768]{2,1,0:T(8,128)(2,1)S(1)}, bf16[3,96,768]{2,1,0:T(8,128)(2,1)S(1)}, u32[]{:S(2)}, u32[]{:S(2)}) collective-permute-start(bf16[3,96,768]{2,1,0:T(8,128)(2,1)S(1)} %slice.26), channel_id=1, source_target_pairs={{0,20},{4,8},{8,28},{12,0},{16,4},{20,24},{24,12},{28,16},{1,21},{... | collective-permute-start | bytes 1327112 | tf_op jit(solution)/shard_map/round1/far/ppermute | solution.py:70
  48.3 12.6 %collective-permute-start.8 = (bf16[160,768]{1,0:T(8,128)(2,1)S(1)}, bf16[160,768]{1,0:T(8,128)(2,1)S(1)}, u32[]{:S(2)}, u32[]{:S(2)}) collective-permute-start(bf16[160,768]{1,0:T(8,128)(2,1)S(1)} %pad_maximum_fusion), channel_id=1, source_target_pairs={{0,3},{1,0},{2,1},{3,2},{4,5},{5,6},{6,7},{7,4},{8,11},{9,8},{10,9... | collective-permute-start | bytes 737288 | tf_op jit(solution)/shard_map/round1/planes2/beside/ppermute | solution.py:79
  49.9 11.0 %collective-permute-start.9 = (bf16[80,768]{1,0:T(8,128)(2,1)S(1)}, bf16[80,768]{1,0:T(8,128)(2,1)S(1)}, u32[]{:S(2)}, u32[]{:S(2)}) collective-permute-start(bf16[80,768]{1,0:T(8,128)(2,1)S(1)} %pad_maximum_fusion.1.refs_4_), channel_id=1, source_target_pairs={{0,2},{1,3},{2,0},{3,1},{4,6},{5,7},{6,4},{7,5},{8,10},{9,11},{10,... | collective-permute-start | bytes 368648 | tf_op jit(solution)/shard_map/round1/planes2/across/ppermute | solution.py:74
  67.8 19.2 %collective-permute-start.20 = (bf16[8,80,768]{2,1,0:T(8,128)(2,1)}, bf16[8,80,768]{2,1,0:T(8,128)(2,1)}, u32[]{:S(2)}, u32[]{:S(2)}) collective-permute-start(bf16[8,80,768]{2,1,0:T(8,128)(2,1)} %round2.3.refs_2_), channel_id=1, source_target_pairs={{0,8},{4,20},{8,0},{12,28},{16,24},{20,4},{24,16},{28,12},{1,9},{5... | collective-permute-start | bytes 2949128 | tf_op jit(solution)/shard_map/round2/near/ppermute | solution.py:70
  68.3 18.3 %collective-permute-start.22 = (bf16[6,96,768]{2,1,0:T(8,128)(2,1)}, bf16[6,96,768]{2,1,0:T(8,128)(2,1)}, u32[]{:S(2)}, u32[]{:S(2)}) collective-permute-start(bf16[6,96,768]{2,1,0:T(8,128)(2,1)} %collective-permute-done.12.refs_1_.refs_10_), channel_id=1, source_target_pairs={{0,4},{4,0},{8,12},{12,8},{16,20},{20,16},{24,28},{28,24},{1,5},{5... | collective-permute-start | bytes 2654216 | tf_op jit(solution)/shard_map/round2/swap/ppermute | solution.py:70
  70.6 16.0 %collective-permute-start.21 = (bf16[3,96,768]{2,1,0:T(8,128)(2,1)}, bf16[3,96,768]{2,1,0:T(8,128)(2,1)}, u32[]{:S(2)}, u32[]{:S(2)}) collective-permute-start(bf16[3,96,768]{2,1,0:T(8,128)(2,1)} %slice.27), channel_id=1, source_target_pairs={{0,20},{4,8},{8,28},{12,0},{16,4},{20,24},{24,12},{28,16},{1,21},{... | collective-permute-start | bytes 1327112 | tf_op jit(solution)/shard_map/round2/far/ppermute | solution.py:70
  71.9 14.8 %collective-permute-start.16 = (bf16[192,768]{1,0:T(8,128)(2,1)}, bf16[192,768]{1,0:T(8,128)(2,1)S(1)}, u32[]{:S(2)}, u32[]{:S(2)}) collective-permute-start(bf16[192,768]{1,0:T(8,128)(2,1)} %get-tuple-element.90), channel_id=1, source_target_pairs={{0,3},{1,0},{2,1},{3,2},{4,5},{5,6},{6,7},{7,4},{8,11},{9,8},{10,9... | collective-permute-start | bytes 884744 | tf_op jit(solution)/shard_map/round2/planes3/beside/ppermute | solution.py:79
  73.2 13.4 %collective-permute-start.17 = (bf16[96,768]{1,0:T(8,128)(2,1)S(1)}, bf16[96,768]{1,0:T(8,128)(2,1)S(1)}, u32[]{:S(2)}, u32[]{:S(2)}) collective-permute-start(bf16[96,768]{1,0:T(8,128)(2,1)S(1)} %copy-done.26), channel_id=1, source_target_pairs={{0,2},{1,3},{2,0},{3,1},{4,6},{5,7},{6,4},{7,5},{8,10},{9,11},{10,... | collective-permute-start | bytes 442376 | tf_op jit(solution)/shard_map/round2/planes3/across/ppermute | solution.py:74
  87.0 16.3 %collective-permute-start.25 = (bf16[8,80,768]{2,1,0:T(8,128)(2,1)}, bf16[8,80,768]{2,1,0:T(8,128)(2,1)}, u32[]{:S(2)}, u32[]{:S(2)}) collective-permute-start(bf16[8,80,768]{2,1,0:T(8,128)(2,1)} %collective-permute-done.20.refs_3_), channel_id=1, source_target_pairs={{0,4},{4,0},{8,12},{12,8},{16,20},{20,16},{24,28},{28,24},{1,5},{5... | collective-permute-start | bytes 2949128 | tf_op jit(solution)/shard_map/round3/swap/ppermute | solution.py:70
  89.8 13.2 %collective-permute-start.24 = (bf16[4,80,768]{2,1,0:T(8,128)(2,1)}, bf16[4,80,768]{2,1,0:T(8,128)(2,1)S(1)}, u32[]{:S(2)}, u32[]{:S(2)}) collective-permute-start(bf16[4,80,768]{2,1,0:T(8,128)(2,1)} %slice.28), channel_id=1, source_target_pairs={{0,20},{4,8},{8,28},{12,0},{16,4},{20,24},{24,12},{28,16},{1,21},{... | collective-permute-start | bytes 1474568 | tf_op jit(solution)/shard_map/round3/far/ppermute | solution.py:70
  93.3 16.5 %collective-permute-start.30 = (bf16[3,96,768]{2,1,0:T(8,128)(2,1)}, bf16[3,96,768]{2,1,0:T(8,128)(2,1)}, u32[]{:S(2)}, u32[]{:S(2)}) collective-permute-start(bf16[3,96,768]{2,1,0:T(8,128)(2,1)} %get-tuple-element.100.refs_8_.refs_1_), channel_id=1, source_target_pairs={{0,8},{4,20},{8,0},{12,28},{16,24},{20,4},{24,16},{28,12},{1,9},{5... | collective-permute-start | bytes 1327112 | tf_op jit(solution)/shard_map/round3/near/ppermute | solution.py:70
  153.6 24.6 %collective-permute-start.38 = (bf16[304,768]{1,0:T(8,128)(2,1)}, bf16[304,768]{1,0:T(8,128)(2,1)S(1)}, u32[]{:S(2)}, u32[]{:S(2)}) collective-permute-start(bf16[304,768]{1,0:T(8,128)(2,1)} %get-tuple-element.106), channel_id=1, source_target_pairs={{0,24},{4,28},{8,16},{12,20},{16,8},{20,12},{24,0},{28,4},{1,25},{... | collective-permute-start | bytes 1400840 | tf_op jit(solution)/shard_map/far/ppermute | solution.py:70
  155.2 23.0 %collective-permute-start.36 = (bf16[304,768]{1,0:T(8,128)(2,1)}, bf16[304,768]{1,0:T(8,128)(2,1)}, u32[]{:S(2)}, u32[]{:S(2)}) collective-permute-start(bf16[304,768]{1,0:T(8,128)(2,1)} %get-tuple-element.118), channel_id=1, source_target_pairs={{0,8},{4,12},{8,0},{12,4},{16,24},{20,28},{24,16},{28,20},{1,9},{5... | collective-permute-start | bytes 1400840 | tf_op jit(solution)/shard_map/x/ppermute | solution.py:70
  156.3 21.9 %collective-permute-start.37 = (bf16[304,768]{1,0:T(8,128)(2,1)}, bf16[304,768]{1,0:T(8,128)(2,1)}, u32[]{:S(2)}, u32[]{:S(2)}) collective-permute-start(bf16[304,768]{1,0:T(8,128)(2,1)} %get-tuple-element.119), channel_id=1, source_target_pairs={{0,16},{4,20},{8,24},{12,28},{16,0},{20,4},{24,8},{28,12},{1,17},{... | collective-permute-start | bytes 1400840 | tf_op jit(solution)/shard_map/y/ppermute | solution.py:70
  182.7 12.9 %collective-permute-start.39 = (bf16[80,768]{1,0:T(8,128)(2,1)}, bf16[80,768]{1,0:T(8,128)(2,1)S(1)}, u32[]{:S(2)}, u32[]{:S(2)}) collective-permute-start(bf16[80,768]{1,0:T(8,128)(2,1)} %get-tuple-element.124), channel_id=1, source_target_pairs={{0,1},{1,2},{2,3},{3,0},{4,5},{5,6},{6,7},{7,4},{8,9},{9,10},{10,1... | collective-permute-start | bytes 368648 | tf_op jit(solution)/shard_map/stack0/ppermute | solution.py:74
  184.1 11.5 %collective-permute-start.40 = (bf16[80,768]{1,0:T(8,128)(2,1)}, bf16[80,768]{1,0:T(8,128)(2,1)S(1)}, u32[]{:S(2)}, u32[]{:S(2)}) collective-permute-start(bf16[80,768]{1,0:T(8,128)(2,1)} %get-tuple-element.125), channel_id=1, source_target_pairs={{0,2},{1,3},{2,0},{3,1},{4,6},{5,7},{6,4},{7,5},{8,10},{9,11},{10,... | collective-permute-start | bytes 368648 | tf_op jit(solution)/shard_map/stack1/ppermute | solution.py:74
  (48 other events, 381.2 us)

commit v3 on v2

--- a/solution.py
+++ b/solution.py
@@ -576,8 +576,13 @@
     bias_ref[...] = total[3 * rows :]
 
 
+def belongs(shape, unit_dim, adapter_dim, neck):
+    unit, adapter = (lax.broadcasted_iota(jnp.int32, shape, d) for d in (unit_dim, adapter_dim))
+    return jnp.where(jnp.logical_and(unit >= adapter * neck, unit < (adapter + 1) * neck), 1.0, 0.0).astype(BF)
+
+
 def joining_kernel(
-    spots_ref, member_ref, member_t_ref, avail_ref, norms_ref, act_hbm, xhat1_hbm, cot_hbm, *refs, halves, count
+    spots_ref, mask_ref, norms_ref, act_hbm, xhat1_hbm, cot_hbm, *refs, halves, count, adapters
 ):
     gain1, bias1, gain2, bias2 = (norms_ref[i : i + 1, :] for i in range(4))
     down_hbm, up_hbm, *refs = refs
@@ -590,11 +595,13 @@
     out_ref, g2_ref, bias_rows_ref, bias_ref = refs[31:35]
     rows, dim = out_ref.shape
     units = w_out_ref.shape[0] // 4
-    seqs = avail_ref.shape[0]
+    seqs = mask_ref.shape[0]
     per = rows // seqs
     everyone = [slice(i * per, (i + 1) * per) for i in range(seqs)]
     fscale = 1.0 / math.sqrt(dim)
-    member, member_t = member_ref[...], member_t_ref[...]
+    member = belongs((dim, 128), 0, 1, dim // adapters)
+    member_t = belongs((128, dim), 1, 0, dim // adapters)
+    lane = lax.broadcasted_iota(jnp.int32, (1, 128), 1)
     loads = []
 
     def issue(r):
@@ -656,7 +663,8 @@
         big_u = mm_t(u_ref[at, :].astype(BF), up)
         big_u_ref[at, :] = big_u
         fscores = (per_adapter(act2_ref[at, :].astype(F32) * big_u) + narrow(i, "dot")) * fscale
-        fscores = jnp.where(avail_ref[i] > 0, fscores, MASKED)
+        bit = lax.rem(lax.shift_right_logical(jnp.full_like(lane, mask_ref[i]), jnp.minimum(lane, adapters)), 2)
+        fscores = jnp.where(jnp.logical_and(bit == 1, lane < adapters), fscores, MASKED)
         fexp = jnp.exp(fscores - jnp.max(fscores, axis=-1, keepdims=True))
         narrow(i, "probs", fexp / jnp.sum(fexp, axis=-1, keepdims=True))
 
@@ -740,7 +748,7 @@
         store.wait()
 
 
-def joining(spots, halves, act, sources, adapt_down, up, join_sources, member, member_t, avail, xhat1, norms, cot):
+def joining(spots, halves, act, sources, adapt_down, up, join_sources, masks, adapters, xhat1, norms, cot):
     rows, dim = xhat1.shape
     if halves:
         grads = [jax.ShapeDtypeStruct((4, 3 * dim // 8 + 16, dim), BF)] * 2
@@ -750,13 +758,13 @@
     height, blocks = join_sources[-1].shape[-2:][0], 32
     stage_shape = join_sources[0].shape if len(join_sources) == 1 else (blocks, height, dim)
     return pl.pallas_call(
-        partial(joining_kernel, halves=halves, count=len(join_sources)),
+        partial(joining_kernel, halves=halves, count=len(join_sources), adapters=adapters),
         out_shape=[
             jax.ShapeDtypeStruct((rows, dim), BF),
             jax.ShapeDtypeStruct((rows, dim), F32),
             jax.ShapeDtypeStruct((rows, dim), BF),
         ] + grads,
-        in_specs=[SMEM] + [VMEM] * 4 + [ANY] * (len(sources) + len(join_sources) + 5),
+        in_specs=[SMEM] * 2 + [VMEM] + [ANY] * (len(sources) + len(join_sources) + 5),
         out_specs=[ANY, ANY, VMEM, ANY, ANY],
         scratch_shapes=[
             pltpu.VMEM(act.shape, BF),
@@ -781,7 +789,7 @@
         ],
         compiler_params=limit(60),
         cost_estimate=cost(2 * rows * dim * (15 * dim + act.shape[1]), 2 * dim * (8 * dim + 10 * rows), 2 * rows * dim),
-    )(spots, member, member_t, avail, norms, act, xhat1, cot, adapt_down, up, *join_sources, *sources)
+    )(spots, masks, norms, act, xhat1, cot, adapt_down, up, *join_sources, *sources)
 
 
 def ffn_back_kernel(spots_ref, g_ref, rstd_ref, norms_ref, slope_hbm, g2_hbm, xhat_hbm, *refs, count):
@@ -1001,14 +1009,9 @@
         return lax.dynamic_slice_in_dim(array, my_z * mine, mine, 0)
 
     x = my_slice(tokens).reshape(rows, dim)
-    shifts = jnp.arange(128, dtype=jnp.int32)
-    bits = jnp.right_shift(my_slice(adapter_mask)[:, None], jnp.minimum(shifts, adapters)[None, :]) % 2
-    avail = jnp.where(shifts[None, :] < adapters, bits, 0)[:, None, :]
+    masks = my_slice(adapter_mask)
     norms = jnp.stack([norm1_gain, norm1_bias, norm2_gain, norm2_bias])
     lens = my_slice(lengths)
-    owner = jnp.arange(adapters * neck, dtype=jnp.int32) // neck
-    member = (owner[:, None] == shifts[None, :]).astype(BF)
-    member_t = (shifts[:, None] == owner[None, :]).astype(BF)
     kept = {}
 
     def attend(sources):
@@ -1032,7 +1035,11 @@
         quarter = att_mats[3]
         for i in range(3):
             quarter = jnp.where(my_d // 2 == i, att_mats[i], quarter)
-        half = gather.half_of(quarter)
+        low = quarter.shape[0] // 2
+        choices = [part for mat in att_mats for part in (mat[:low], mat[low:])]
+        half = choices[7]
+        for i in range(7):
+            half = jnp.where(my_d == i, choices[i], half)
         rounds = [(half, tie(quarter, half))]
         shards_in, shards_out = tie(ffn_in, half), tie(ffn_out, half)
         in_quarter, in_half, out_quarter, out_half = cut(spots, [shards_in, shards_out])
@@ -1042,7 +1049,7 @@
         even = lax.rem(my_d, 2) == 0
         pair = jnp.concatenate([jnp.where(even, join_part, theirs), jnp.where(even, theirs, join_part)], axis=0)
         rounds.insert(2, (join_part, pair, join_part, theirs))
-        got = gather.all_rounds(rounds, [x, norms, lens, avail, member, member_t, spots], steps)
+        got = gather.all_rounds(rounds, [spots, x, norms, lens, masks], steps)
         att_sources, in_sources, out_sources = (got[i] + own[i] for i in (0, 1, 3))
         join_sources = got[2]
     else:
@@ -1053,11 +1060,11 @@
     up = adapt_up.reshape(adapters * neck, dim)
     cot = cotangent.reshape(rows, dim)
 
-    def rest(att, ffn, avail, cot):
+    def rest(att, ffn, masks, cot):
         q, k, v, probs, low1, xhat1, rstd1 = att
         act, slope = ffn
         layer_out, g2, g_ffn, *grads = joining(
-            spots, gather.paired, act, out_sources, adapt_down, up, join_sources, member, member_t, avail, xhat1, norms, cot
+            spots, gather.paired, act, out_sources, adapt_down, up, join_sources, masks, adapters, xhat1, norms, cot
         )
         done = {}
 
@@ -1074,7 +1081,7 @@
         return layer_out, grads, between, at_last
 
     if gather.paired:
-        layer_out, grads, between, at_last = rest(kept["att"], kept["ffn"], avail, cot)
+        layer_out, grads, between, at_last = rest(kept["att"], kept["ffn"], masks, cot)
         (d_q, d_k, d_v, d_bias), input_grad = reduce_grads(gather, grads, own_rows, between, at_last)
     else:
         outs = []
@@ -1082,7 +1089,7 @@
             at = slice(first * seq_len, (first + 2) * seq_len)
             att = attention_forward(spots, lens[first : first + 2], x[at], att_sources, norms, seq_len)
             ffn = ffn_forward(spots, att[4], in_sources, ffn_bias, ffn_in.shape[1])
-            outs.append(rest(att, ffn, avail[first : first + 2], cot[at]))
+            outs.append(rest(att, ffn, masks[first : first + 2], cot[at]))
         layer_out = jnp.concatenate([out[0] for out in outs])
         grads = [sum(out[1][i] for out in outs) for i in range(2)]
         (d_q, d_k, d_v, d_bias), input_grad = reduce_grads(

time: 201 us -> 199 us (0.990)
  other arithmetic: 9.57 us -> 6.05 us
  waiting for transfers between devices: 46 us -> 48.5 us
    unnamed x60 -> x56, local copies, waits for them, and re-layouts: 4.05 us -> 4 us
  transfers between devices with their start and end apart: 42 -> 42, of which waited for: 13 -> 15; matrix products, arithmetic and copies ran while one was open for 6% -> 5% of each run, Pallas kernels for 28% -> 28%
where the time goes in v3:
time: 199 us; the launch traced here: 195 us
  Pallas kernels  95.9 us (48%)
  waiting for transfers between devices  48.5 us (24%)
  starting transfers between devices  32.1 us (16%)
  local copies, waits for them, and re-layouts  11.2 us (6%)
  other arithmetic  6.05 us (3%)
    pallas_call x1, Pallas kernels, joining(): pl.pallas_call(partial(joining_kernel, halves=halves, count=len(join_sour...  30.3 us
    ppermute x7, waiting for transfers between devices, shift(): lax.ppermute(array, 'tensor', [(i, (i + by) % groups) for i in range(grou...  25.4 us
    ppermute x31, waiting for transfers between devices, send(): return lax.ppermute(array, 'dp', pairs)  21.4 us
    ppermute x31, starting transfers between devices, send(): return lax.ppermute(array, 'dp', pairs)  16.5 us
    pallas_call x1, Pallas kernels, attention_forward(): pl.pallas_call(attention_kernel, out_shape=[low, low, low, jax.ShapeDtype...  12.2 us
    pallas_call x1, Pallas kernels, ffn_backward(): pl.pallas_call(partial(ffn_back_kernel, count=(len(out_sources), len(in_s...  11.8 us
    ppermute x7, starting transfers between devices, shift(): lax.ppermute(array, 'tensor', [(i, (i + by) % groups) for i in range(grou...  9.94 us
    pallas_call x1, Pallas kernels, attention_backward_first(): pl.pallas_call(attention_back_first_kernel, out_shape=[half, half], in_sp...  9.17 us
  transfers between devices with their start and end apart: 42, of which 15 were waited for; matrix products, arithmetic and copies ran while one was open for 5% of the time, Pallas kernels for 28%

profile of v3, /device:TPU:0, one launch (start us, length us, event | category | flops | bytes accessed | tf_op | source)
XLA Modules:
  0.0 195.2 jit_solution(2497568884192549367)
XLA Ops:
  0.8 2.2 %fusion.5 = bf16[96,768]{1,0:T(8,128)(2,1)} fusion(bf16[192,768]{1,0:T(8,128)(2,1)} %bitcast.19, bf16[192,768]{1,0:T(8,128)(2,1)} %bitcast.23, bf16[192,768]{1,0:T(8,128)(2,1)} %bitcast.27, bf16[192,768]{1,0:T(8,128)(2,1)} %refs_11_.1, pred[]{:T(512)S(6)} %eq.44, pred[]{:T(512)S(6)} %eq.43, pred[]{:T(512)S(6)} %eq.42, pred[]{:T(512)S(6)} %eq.41, pred[]{:T(512)S(6)} %eq.40, ...), kind=kLoop, calls=%fused_computation.8 | loop fusion | flops 516096 | bytes 1327111 | tf_op jit(solution)/shard_map/jit(_where)/select_n | solution.py:1042
  3.0 4.0 %collective-permute-start.1 = (bf16[96,768]{1,0:T(8,128)(2,1)}, bf16[96,768]{1,0:T(8,128)(2,1)S(1)}, u32[]{:S(2)}, u32[]{:S(2)}) collective-permute-start(bf16[96,768]{1,0:T(8,128)(2,1)} %fusion.5), channel_id=1, source_target_pairs={{0,2},{1,3},{2,0},{3,1},{4,6},{5,7},{6,4},{7,5},{8,10},{9,11},{10,... | collective-permute-start | bytes 442376 | tf_op jit(solution)/shard_map/planes0/across/ppermute | solution.py:74
  7.0 1.9 select_select_fusion
  14.5 2.8 %shard_map.279 = (bf16[192,768]{1,0:T(8,128)(2,1)}, bf16[96,768]{1,0:T(8,128)(2,1)}, bf16[192,768]{1,0:T(8,128)(2,1)}, bf16[96,768]{1,0:T(8,128)(2,1)}) custom-call(s32[9]{0:T(128)} %pad_add_fusion.spots_ref, bf16[768,768]{1,0:T(8,128)(2,1)} %refs_14_.1, bf16[768,768]{1,0:T(8,128)(2,1)} %refs_8_.3), custom_call_target="tpu_custom_call" | custom-call | tf_op jit(solution)/shard_map/pallas_call | solution.py:195
  19.0 1.6 collective-permute-done.refs_0_
  28.3 14.1 %collective-permute-done.6.refs_1_ = bf16[96,768]{1,0:T(8,128)(2,1)S(1)} collective-permute-done((bf16[96,768]{1,0:T(8,128)(2,1)S(1)}, bf16[96,768]{1,0:T(8,128)(2,1)S(1)}, u32[]{:S(2)}, u32[]{:S(2)}) %collective-permute-start.6) | collective-permute-done | bytes 147488 | tf_op jit(solution)/shard_map/round0/planes1/across/ppermute | solution.py:74
  46.5 1.8 collective-permute-start.8
  48.3 11.0 %collective-permute-done.9.refs_1_ = bf16[80,768]{1,0:T(8,128)(2,1)S(1)} collective-permute-done((bf16[80,768]{1,0:T(8,128)(2,1)S(1)}, bf16[80,768]{1,0:T(8,128)(2,1)S(1)}, u32[]{:S(2)}, u32[]{:S(2)}) %collective-permute-start.9) | collective-permute-done | bytes 122912 | tf_op jit(solution)/shard_map/round1/planes2/across/ppermute | solution.py:74
  59.4 3.5 %collective-permute-done.12.refs_1_.refs_10_ = bf16[6,96,768]{2,1,0:T(8,128)(2,1)} collective-permute-done((bf16[6,96,768]{2,1,0:T(8,128)(2,1)S(1)}, bf16[6,96,768]{2,1,0:T(8,128)(2,1)}, u32[]{:S(2)}, u32[]{:S(2)}) %collective-permute-start.12) | collective-permute-done | bytes 884768 | tf_op jit(solution)/shard_map/round1/near/ppermute | solution.py:70
  64.5 1.6 round2.3.refs_2_
  67.2 1.8 slice.51
  72.4 12.2 %round2.2 = (bf16[512,768]{1,0:T(8,128)(2,1)}, bf16[512,768]{1,0:T(8,128)(2,1)}, bf16[512,768]{1,0:T(8,128)(2,1)}, bf16[24,256,256]{2,1,0:T(8,128)(2,1)}, bf16[5...) custom-call(s32[9]{0:T(128)} %pad_add_fusion.spots_ref, s32[2]{0:T(128)} %dynamic_slice.13.len_ref, ...), custom_call_target="tpu_custom_call" | custom-call | flops 2818572288 | bytes 11010048 | tf_op jit(solution)/shard_map/round2/pallas_call | solution.py:439
  92.3 8.6 %round3.2 = (bf16[512,3072]{1,0:T(8,128)(2,1)}, bf16[512,3072]{1,0:T(8,128)(2,1)}) custom-call(s32[9]{0:T(128)} %pad_add_fusion.spots_ref, bf16[512,768]{1,0:T(8,128)(2,1)} %get-tuple-element.87.x_ref, f32[4,1,768]{2,1,0:T(1,128)} %bitcast.35, bf16[6,96,768]{2,1,0:T(8,128)(2,1)} %copy-done.2, bf16[6,96,768]{2,1,0:T(8,128)(2,1)} %collective-permute-done.12.refs_1_.refs_10_, ...), custom_call_target="tpu_custom_call" | custom-call | flops 2415919104 | bytes 11010048 | tf_op jit(solution)/shard_map/round3/pallas_call | solution.py:483
  102.1 4.6 %collective-permute-done.30.refs_10_.refs_3_ = bf16[3,96,768]{2,1,0:T(8,128)(2,1)} collective-permute-done((bf16[3,96,768]{2,1,0:T(8,128)(2,1)}, bf16[3,96,768]{2,1,0:T(8,128)(2,1)}, u32[]{:S(2)}, u32[]{:S(2)}) %collective-permute-start.30) | collective-permute-done | bytes 442400 | tf_op jit(solution)/shard_map/round3/near/ppermute | solution.py:70
  107.1 3.0 %collective-permute-done.31.refs_11_.refs_4_ = bf16[3,96,768]{2,1,0:T(8,128)(2,1)S(1)} collective-permute-done((bf16[3,96,768]{2,1,0:T(8,128)(2,1)}, bf16[3,96,768]{2,1,0:T(8,128)(2,1)S(1)}, u32[]{:S(2)}, u32[]{:S(2)}) %collective-permute-start.31) | collective-permute-done | bytes 442400 | tf_op jit(solution)/shard_map/round3/far/ppermute | solution.py:70
  110.3 1.6 collective-permute-done.34.refs_14_.refs_7_
  112.7 30.3 %shard_map.280 = (bf16[512,768]{1,0:T(8,128)(2,1)}, f32[512,768]{1,0:T(8,128)}, bf16[512,768]{1,0:T(8,128)(2,1)}, bf16[4,304,768]{2,1,0:T(8,128)(2,1)}, bf16[4,304,768]{2,1,0:T(8,128)(2,1)}) custom-call(s32[9]{0:T(128)} %pad_add_fusion.spots_ref, s32[2]{0:T(128)} %dynamic_slice.12.mask_ref, f32[4,768]{1,0:T(4,128)} %pad_maximum_fusion.2.norms_ref, ...), custom_call_target="tpu_custom_call" | custom-call | flops 11475615744 | bytes 17301504 | tf_op jit(solution)/shard_map/pallas_call | solution.py:760
  143.3 4.0 %collective-permute-done.35.come_hbm.refs_4_ = bf16[4,304,768]{2,1,0:T(8,128)(2,1)} collective-permute-done((bf16[4,304,768]{2,1,0:T(8,128)(2,1)}, bf16[4,304,768]{2,1,0:T(8,128)(2,1)}, u32[]{:S(2)}, u32[]{:S(2)}) %collective-permute-start.35) | collective-permute-done | bytes 1867808 | tf_op jit(solution)/shard_map/cores/ppermute | solution.py:70
  147.3 3.4 %shard_map.281 = (bf16[304,768]{1,0:T(8,128)(2,1)}, bf16[304,768]{1,0:T(8,128)(2,1)}, bf16[304,768]{1,0:T(8,128)(2,1)}) custom-call(s32[9]{0:T(128)} %pad_add_fusion.spots_ref, bf16[4,304,768]{2,1,0:T(8,128)(2,1)} %get-tuple-element.120.keep_hbm.refs_3_, bf16[4,304,768]{2,1,0:T(8,128)(2,1)} %collective-permute-done.35.come_hbm.refs_4_), custom_call_target="tpu_custom_call" | custom-call | tf_op jit(solution)/shard_map/pallas_call | solution.py:350
  154.3 11.8 %shard_map.282 = (f32[512,768]{1,0:T(8,128)}, bf16[512,768]{1,0:T(8,128)(2,1)}) custom-call(s32[9]{0:T(128)} %pad_add_fusion.spots_ref, bf16[512,768]{1,0:T(8,128)(2,1)} %get-tuple-element.107.g_ref, f32[512,1]{1,0:T(8,128)} %get-tuple-element.108.rstd_ref, f32[4,768]{1,0:T(4,128)} %pad_maximum_fusion.2.norms_ref, ...), custom_call_target="tpu_custom_call" | custom-call | flops 4831838208 | bytes 12582912 | tf_op jit(solution)/shard_map/pallas_call | solution.py:847
  166.1 9.2 %shard_map.283 = (bf16[256,768]{1,0:T(8,128)(2,1)}, bf16[256,768]{1,0:T(8,128)(2,1)}) custom-call(s32[9]{0:T(128)} %pad_add_fusion.spots_ref, bf16[512,768]{1,0:T(8,128)(2,1)} %get-tuple-element.112.refs_0_, f32[512,768]{1,0:T(8,128)} %get-tuple-element.111.refs_1_.refs_0_, bf16[6,96,768]{2,1,0:T(8,128)(2,1)} %copy-done.1, bf16[6,96,768]{2,1,0:T(8,128)(2,1)} %copy-done.6, ...), custom_call_target="tpu_custom_call" | custom-call | flops 2214592512 | bytes 8650752 | tf_op jit(solution)/shard_map/pallas_call | solution.py:955
  176.9 3.8 %shard_map.284 = (f32[80,768]{1,0:T(8,128)}, bf16[80,768]{1,0:T(8,128)(2,1)}, bf16[80,768]{1,0:T(8,128)(2,1)}, bf16[80,768]{1,0:T(8,128)(2,1)}) custom-call(s32[9]{0:T(128)} %pad_add_fusion.spots_ref, bf16[304,768]{1,0:T(8,128)(2,1)} %copy-done.11, bf16[304,768]{1,0:T(8,128)(2,1)} %collective-permute-done.37.refs_1_, bf16[304,768]{1,0:T(8,128)(2,1)} %copy-done.10, ...), custom_call_target="tpu_custom_call" | custom-call | tf_op jit(solution)/shard_map/pallas_call | solution.py:363
  182.9 2.4 %collective-permute-start.41 = (bf16[80,768]{1,0:T(8,128)(2,1)}, bf16[80,768]{1,0:T(8,128)(2,1)S(1)}, u32[]{:S(2)}, u32[]{:S(2)}) collective-permute-start(bf16[80,768]{1,0:T(8,128)(2,1)} %get-tuple-element.126), channel_id=1, source_target_pairs={{0,3},{1,0},{2,1},{3,2},{4,7},{5,4},{6,5},{7,6},{8,11},{9,8},{10,9... | collective-permute-start | bytes 368648 | tf_op jit(solution)/shard_map/stack2/ppermute | solution.py:74
  185.2 8.3 %shard_map.285 = bf16[512,768]{1,0:T(8,128)(2,1)} custom-call(s32[9]{0:T(128)} %pad_add_fusion.spots_ref, f32[512,768]{1,0:T(8,128)} %get-tuple-element.111.refs_1_.refs_0_, bf16[256,768]{1,0:T(8,128)(2,1)} %get-tuple-element.122.refs_1_, bf16[256,768]{1,0:T(8,128)(2,1)} %get-tuple-element.123.refs_2_, bf16[6,96,768]{2,1,0:T(8,128)(2,1)} %copy-done.1, ...), custom_call_target="tpu_custom_call" | custom-call | flops 1610612736 | bytes 6684672 | tf_op jit(solution)/shard_map/pallas_call | solution.py:972
  (154 shorter events, 44.1 us)
Async XLA Ops:
  3.0 16.0 %collective-permute-start.1 = (bf16[96,768]{1,0:T(8,128)(2,1)}, bf16[96,768]{1,0:T(8,128)(2,1)S(1)}, u32[]{:S(2)}, u32[]{:S(2)}) collective-permute-start(bf16[96,768]{1,0:T(8,128)(2,1)} %fusion.5), channel_id=1, source_target_pairs={{0,2},{1,3},{2,0},{3,1},{4,6},{5,7},{6,4},{7,5},{8,10},{9,11},{10,... | collective-permute-start | bytes 442376 | tf_op jit(solution)/shard_map/planes0/across/ppermute | solution.py:74
  8.9 11.7 %collective-permute-start = (bf16[192,768]{1,0:T(8,128)(2,1)}, bf16[192,768]{1,0:T(8,128)(2,1)}, u32[]{:S(2)}, u32[]{:S(2)}) collective-permute-start(bf16[192,768]{1,0:T(8,128)(2,1)} %select_select_fusion), channel_id=1, source_target_pairs={{0,3},{1,0},{2,1},{3,2},{4,5},{5,6},{6,7},{7,4},{8,11},{9,8},{10,9... | collective-permute-start | bytes 884744 | tf_op jit(solution)/shard_map/planes0/beside/ppermute | solution.py:79
  24.6 17.8 %collective-permute-start.7 = (bf16[6,96,768]{2,1,0:T(8,128)(2,1)S(1)}, bf16[6,96,768]{2,1,0:T(8,128)(2,1)S(1)}, u32[]{:S(2)}, u32[]{:S(2)}) collective-permute-start(bf16[6,96,768]{2,1,0:T(8,128)(2,1)S(1)} %round0.1.refs_0_.refs_2_.refs_3_), channel_id=1, source_target_pairs={{0,8},{4,20},{8,0},{12,28},{16,24},{20,4},{24,16},{28,12},{1,9},{5... | collective-permute-start | bytes 2654216 | tf_op jit(solution)/shard_map/round0/near/ppermute | solution.py:70
  26.2 16.2 %collective-permute-start.5 = (bf16[192,768]{1,0:T(8,128)(2,1)S(1)}, bf16[192,768]{1,0:T(8,128)(2,1)S(1)}, u32[]{:S(2)}, u32[]{:S(2)}) collective-permute-start(bf16[192,768]{1,0:T(8,128)(2,1)S(1)} %copy-done.24), channel_id=1, source_target_pairs={{0,3},{1,0},{2,1},{3,2},{4,5},{5,6},{6,7},{7,4},{8,11},{9,8},{10,9... | collective-permute-start | bytes 884744 | tf_op jit(solution)/shard_map/round0/planes1/beside/ppermute | solution.py:79
  27.1 15.3 %collective-permute-start.6 = (bf16[96,768]{1,0:T(8,128)(2,1)S(1)}, bf16[96,768]{1,0:T(8,128)(2,1)S(1)}, u32[]{:S(2)}, u32[]{:S(2)}) collective-permute-start(bf16[96,768]{1,0:T(8,128)(2,1)S(1)} %copy-done.25), channel_id=1, source_target_pairs={{0,2},{1,3},{2,0},{3,1},{4,6},{5,7},{6,4},{7,5},{8,10},{9,11},{10,... | collective-permute-start | bytes 442376 | tf_op jit(solution)/shard_map/round0/planes1/across/ppermute | solution.py:74
  43.0 16.4 %collective-permute-start.14 = (bf16[6,96,768]{2,1,0:T(8,128)(2,1)S(1)}, bf16[6,96,768]{2,1,0:T(8,128)(2,1)S(1)}, u32[]{:S(2)}, u32[]{:S(2)}) collective-permute-start(bf16[6,96,768]{2,1,0:T(8,128)(2,1)S(1)} %collective-permute-done.7.refs_1_.refs_3_.refs_4_), channel_id=1, source_target_pairs={{0,4},{4,0},{8,12},{12,8},{16,20},{20,16},{24,28},{28,24},{1,5},{5... | collective-permute-start | bytes 2654216 | tf_op jit(solution)/shard_map/round1/swap/ppermute | solution.py:70
  44.9 18.0 %collective-permute-start.12 = (bf16[6,96,768]{2,1,0:T(8,128)(2,1)S(1)}, bf16[6,96,768]{2,1,0:T(8,128)(2,1)}, u32[]{:S(2)}, u32[]{:S(2)}) collective-permute-start(bf16[6,96,768]{2,1,0:T(8,128)(2,1)S(1)} %round1.1.refs_0_.refs_9_), channel_id=1, source_target_pairs={{0,8},{4,20},{8,0},{12,28},{16,24},{20,4},{24,16},{28,12},{1,9},{5... | collective-permute-start | bytes 2654216 | tf_op jit(solution)/shard_map/round1/near/ppermute | solution.py:70
  45.6 13.8 %collective-permute-start.13 = (bf16[3,96,768]{2,1,0:T(8,128)(2,1)S(1)}, bf16[3,96,768]{2,1,0:T(8,128)(2,1)S(1)}, u32[]{:S(2)}, u32[]{:S(2)}) collective-permute-start(bf16[3,96,768]{2,1,0:T(8,128)(2,1)S(1)} %slice.50), channel_id=1, source_target_pairs={{0,20},{4,8},{8,28},{12,0},{16,4},{20,24},{24,12},{28,16},{1,21},{... | collective-permute-start | bytes 1327112 | tf_op jit(solution)/shard_map/round1/far/ppermute | solution.py:70
  46.5 12.8 %collective-permute-start.8 = (bf16[160,768]{1,0:T(8,128)(2,1)S(1)}, bf16[160,768]{1,0:T(8,128)(2,1)S(1)}, u32[]{:S(2)}, u32[]{:S(2)}) collective-permute-start(bf16[160,768]{1,0:T(8,128)(2,1)S(1)} %pad_maximum_fusion), channel_id=1, source_target_pairs={{0,3},{1,0},{2,1},{3,2},{4,5},{5,6},{6,7},{7,4},{8,11},{9,8},{10,9... | collective-permute-start | bytes 737288 | tf_op jit(solution)/shard_map/round1/planes2/beside/ppermute | solution.py:79
  48.3 11.0 %collective-permute-start.9 = (bf16[80,768]{1,0:T(8,128)(2,1)S(1)}, bf16[80,768]{1,0:T(8,128)(2,1)S(1)}, u32[]{:S(2)}, u32[]{:S(2)}) collective-permute-start(bf16[80,768]{1,0:T(8,128)(2,1)S(1)} %pad_maximum_fusion.1.refs_4_), channel_id=1, source_target_pairs={{0,2},{1,3},{2,0},{3,1},{4,6},{5,7},{6,4},{7,5},{8,10},{9,11},{10,... | collective-permute-start | bytes 368648 | tf_op jit(solution)/shard_map/round1/planes2/across/ppermute | solution.py:74
  66.1 19.2 %collective-permute-start.20 = (bf16[8,80,768]{2,1,0:T(8,128)(2,1)}, bf16[8,80,768]{2,1,0:T(8,128)(2,1)}, u32[]{:S(2)}, u32[]{:S(2)}) collective-permute-start(bf16[8,80,768]{2,1,0:T(8,128)(2,1)} %round2.3.refs_2_), channel_id=1, source_target_pairs={{0,8},{4,20},{8,0},{12,28},{16,24},{20,4},{24,16},{28,12},{1,9},{5... | collective-permute-start | bytes 2949128 | tf_op jit(solution)/shard_map/round2/near/ppermute | solution.py:70
  66.7 18.2 %collective-permute-start.22 = (bf16[6,96,768]{2,1,0:T(8,128)(2,1)}, bf16[6,96,768]{2,1,0:T(8,128)(2,1)}, u32[]{:S(2)}, u32[]{:S(2)}) collective-permute-start(bf16[6,96,768]{2,1,0:T(8,128)(2,1)} %collective-permute-done.12.refs_1_.refs_10_), channel_id=1, source_target_pairs={{0,4},{4,0},{8,12},{12,8},{16,20},{20,16},{24,28},{28,24},{1,5},{5... | collective-permute-start | bytes 2654216 | tf_op jit(solution)/shard_map/round2/swap/ppermute | solution.py:70
  69.0 15.9 %collective-permute-start.21 = (bf16[3,96,768]{2,1,0:T(8,128)(2,1)}, bf16[3,96,768]{2,1,0:T(8,128)(2,1)}, u32[]{:S(2)}, u32[]{:S(2)}) collective-permute-start(bf16[3,96,768]{2,1,0:T(8,128)(2,1)} %slice.51), channel_id=1, source_target_pairs={{0,20},{4,8},{8,28},{12,0},{16,4},{20,24},{24,12},{28,16},{1,21},{... | collective-permute-start | bytes 1327112 | tf_op jit(solution)/shard_map/round2/far/ppermute | solution.py:70
  70.1 14.9 %collective-permute-start.16 = (bf16[192,768]{1,0:T(8,128)(2,1)}, bf16[192,768]{1,0:T(8,128)(2,1)S(1)}, u32[]{:S(2)}, u32[]{:S(2)}) collective-permute-start(bf16[192,768]{1,0:T(8,128)(2,1)} %get-tuple-element.90), channel_id=1, source_target_pairs={{0,3},{1,0},{2,1},{3,2},{4,5},{5,6},{6,7},{7,4},{8,11},{9,8},{10,9... | collective-permute-start | bytes 884744 | tf_op jit(solution)/shard_map/round2/planes3/beside/ppermute | solution.py:79
  71.6 13.3 %collective-permute-start.17 = (bf16[96,768]{1,0:T(8,128)(2,1)}, bf16[96,768]{1,0:T(8,128)(2,1)S(1)}, u32[]{:S(2)}, u32[]{:S(2)}) collective-permute-start(bf16[96,768]{1,0:T(8,128)(2,1)} %get-tuple-element.91), channel_id=1, source_target_pairs={{0,2},{1,3},{2,0},{3,1},{4,6},{5,7},{6,4},{7,5},{8,10},{9,11},{10,... | collective-permute-start | bytes 442376 | tf_op jit(solution)/shard_map/round2/planes3/across/ppermute | solution.py:74
  85.3 15.7 %collective-permute-start.25 = (bf16[8,80,768]{2,1,0:T(8,128)(2,1)}, bf16[8,80,768]{2,1,0:T(8,128)(2,1)}, u32[]{:S(2)}, u32[]{:S(2)}) collective-permute-start(bf16[8,80,768]{2,1,0:T(8,128)(2,1)} %collective-permute-done.20.refs_3_), channel_id=1, source_target_pairs={{0,4},{4,0},{8,12},{12,8},{16,20},{20,16},{24,28},{28,24},{1,5},{5... | collective-permute-start | bytes 2949128 | tf_op jit(solution)/shard_map/round3/swap/ppermute | solution.py:70
  87.4 13.6 %collective-permute-start.24 = (bf16[4,80,768]{2,1,0:T(8,128)(2,1)S(1)}, bf16[4,80,768]{2,1,0:T(8,128)(2,1)}, u32[]{:S(2)}, u32[]{:S(2)}) collective-permute-start(bf16[4,80,768]{2,1,0:T(8,128)(2,1)S(1)} %slice.52), channel_id=1, source_target_pairs={{0,20},{4,8},{8,28},{12,0},{16,4},{20,24},{24,12},{28,16},{1,21},{... | collective-permute-start | bytes 1474568 | tf_op jit(solution)/shard_map/round3/far/ppermute | solution.py:70
  91.2 15.4 %collective-permute-start.30 = (bf16[3,96,768]{2,1,0:T(8,128)(2,1)}, bf16[3,96,768]{2,1,0:T(8,128)(2,1)}, u32[]{:S(2)}, u32[]{:S(2)}) collective-permute-start(bf16[3,96,768]{2,1,0:T(8,128)(2,1)} %get-tuple-element.100.refs_8_.refs_1_), channel_id=1, source_target_pairs={{0,8},{4,20},{8,0},{12,28},{16,24},{20,4},{24,16},{28,12},{1,9},{5... | collective-permute-start | bytes 1327112 | tf_op jit(solution)/shard_map/round3/near/ppermute | solution.py:70
  150.7 24.6 %collective-permute-start.38 = (bf16[304,768]{1,0:T(8,128)(2,1)}, bf16[304,768]{1,0:T(8,128)(2,1)S(1)}, u32[]{:S(2)}, u32[]{:S(2)}) collective-permute-start(bf16[304,768]{1,0:T(8,128)(2,1)} %get-tuple-element.106), channel_id=1, source_target_pairs={{0,24},{4,28},{8,16},{12,20},{16,8},{20,12},{24,0},{28,4},{1,25},{... | collective-permute-start | bytes 1400840 | tf_op jit(solution)/shard_map/far/ppermute | solution.py:70
  152.2 23.1 %collective-permute-start.36 = (bf16[304,768]{1,0:T(8,128)(2,1)}, bf16[304,768]{1,0:T(8,128)(2,1)S(1)}, u32[]{:S(2)}, u32[]{:S(2)}) collective-permute-start(bf16[304,768]{1,0:T(8,128)(2,1)} %get-tuple-element.118), channel_id=1, source_target_pairs={{0,8},{4,12},{8,0},{12,4},{16,24},{20,28},{24,16},{28,20},{1,9},{5... | collective-permute-start | bytes 1400840 | tf_op jit(solution)/shard_map/x/ppermute | solution.py:70
  153.2 22.1 %collective-permute-start.37 = (bf16[304,768]{1,0:T(8,128)(2,1)}, bf16[304,768]{1,0:T(8,128)(2,1)}, u32[]{:S(2)}, u32[]{:S(2)}) collective-permute-start(bf16[304,768]{1,0:T(8,128)(2,1)} %get-tuple-element.119), channel_id=1, source_target_pairs={{0,16},{4,20},{8,24},{12,28},{16,0},{20,4},{24,8},{28,12},{1,17},{... | collective-permute-start | bytes 1400840 | tf_op jit(solution)/shard_map/y/ppermute | solution.py:70
  180.6 13.0 %collective-permute-start.39 = (bf16[80,768]{1,0:T(8,128)(2,1)}, bf16[80,768]{1,0:T(8,128)(2,1)S(1)}, u32[]{:S(2)}, u32[]{:S(2)}) collective-permute-start(bf16[80,768]{1,0:T(8,128)(2,1)} %get-tuple-element.124), channel_id=1, source_target_pairs={{0,1},{1,2},{2,3},{3,0},{4,5},{5,6},{6,7},{7,4},{8,9},{9,10},{10,1... | collective-permute-start | bytes 368648 | tf_op jit(solution)/shard_map/stack0/ppermute | solution.py:74
  181.8 11.8 %collective-permute-start.40 = (bf16[80,768]{1,0:T(8,128)(2,1)}, bf16[80,768]{1,0:T(8,128)(2,1)S(1)}, u32[]{:S(2)}, u32[]{:S(2)}) collective-permute-start(bf16[80,768]{1,0:T(8,128)(2,1)} %get-tuple-element.125), channel_id=1, source_target_pairs={{0,2},{1,3},{2,0},{3,1},{4,6},{5,7},{6,4},{7,5},{8,10},{9,11},{10,... | collective-permute-start | bytes 368648 | tf_op jit(solution)/shard_map/stack1/ppermute | solution.py:74
  182.9 10.8 %collective-permute-start.41 = (bf16[80,768]{1,0:T(8,128)(2,1)}, bf16[80,768]{1,0:T(8,128)(2,1)S(1)}, u32[]{:S(2)}, u32[]{:S(2)}) collective-permute-start(bf16[80,768]{1,0:T(8,128)(2,1)} %get-tuple-element.126), channel_id=1, source_target_pairs={{0,3},{1,0},{2,1},{3,2},{4,7},{5,4},{6,5},{7,6},{8,11},{9,8},{10,9... | collective-permute-start | bytes 368648 | tf_op jit(solution)/shard_map/stack2/ppermute | solution.py:74
  (46 other events, 330.3 us)

commit v4 on v3

--- a/solution.py
+++ b/solution.py
@@ -617,8 +617,9 @@
 
     issue(0)
     issue(1)
+    issue(2)
     for r in range(4):
-        issue(r + 2)
+        issue(r + 3)
         loads[r].wait()
         arrive(w_out_ref, out_sems, r)
         if r % 2 == 1:

time: 199 us -> 199 us (level)
  no operation moved by 1% of the time
where the time goes in v4:
time: 199 us; the launch traced here: 195 us
  Pallas kernels  95.6 us (48%)
  waiting for transfers between devices  48.5 us (24%)
  starting transfers between devices  32.1 us (16%)
  local copies, waits for them, and re-layouts  11.2 us (6%)
  other arithmetic  6.05 us (3%)
    pallas_call x1, Pallas kernels, joining(): pl.pallas_call(partial(joining_kernel, halves=halves, count=len(join_sour...  30 us
    ppermute x7, waiting for transfers between devices, shift(): lax.ppermute(array, 'tensor', [(i, (i + by) % groups) for i in range(grou...  25.4 us
    ppermute x31, waiting for transfers between devices, send(): return lax.ppermute(array, 'dp', pairs)  21.4 us
    ppermute x31, starting transfers between devices, send(): return lax.ppermute(array, 'dp', pairs)  16.5 us
    pallas_call x1, Pallas kernels, attention_forward(): pl.pallas_call(attention_kernel, out_shape=[low, low, low, jax.ShapeDtype...  12.2 us
    pallas_call x1, Pallas kernels, ffn_backward(): pl.pallas_call(partial(ffn_back_kernel, count=(len(out_sources), len(in_s...  11.8 us
    ppermute x7, starting transfers between devices, shift(): lax.ppermute(array, 'tensor', [(i, (i + by) % groups) for i in range(grou...  9.93 us
    pallas_call x1, Pallas kernels, attention_backward_first(): pl.pallas_call(attention_back_first_kernel, out_shape=[half, half], in_sp...  9.17 us
  transfers between devices with their start and end apart: 42, of which 15 were waited for; matrix products, arithmetic and copies ran while one was open for 5% of the time, Pallas kernels for 28%

profile of v4, /device:TPU:0, one launch (start us, length us, event | category | flops | bytes accessed | tf_op | source)
XLA Modules:
  0.0 194.8 jit_solution(3903425510128891367)
XLA Ops:
  0.8 2.2 %fusion.5 = bf16[96,768]{1,0:T(8,128)(2,1)} fusion(bf16[192,768]{1,0:T(8,128)(2,1)} %bitcast.19, bf16[192,768]{1,0:T(8,128)(2,1)} %bitcast.23, bf16[192,768]{1,0:T(8,128)(2,1)} %bitcast.27, bf16[192,768]{1,0:T(8,128)(2,1)} %refs_11_.1, pred[]{:T(512)S(6)} %eq.44, pred[]{:T(512)S(6)} %eq.43, pred[]{:T(512)S(6)} %eq.42, pred[]{:T(512)S(6)} %eq.41, pred[]{:T(512)S(6)} %eq.40, ...), kind=kLoop, calls=%fused_computation.8 | loop fusion | flops 516096 | bytes 1327111 | tf_op jit(solution)/shard_map/jit(_where)/select_n | solution.py:1043
  3.0 4.0 %collective-permute-start.1 = (bf16[96,768]{1,0:T(8,128)(2,1)}, bf16[96,768]{1,0:T(8,128)(2,1)S(1)}, u32[]{:S(2)}, u32[]{:S(2)}) collective-permute-start(bf16[96,768]{1,0:T(8,128)(2,1)} %fusion.5), channel_id=1, source_target_pairs={{0,2},{1,3},{2,0},{3,1},{4,6},{5,7},{6,4},{7,5},{8,10},{9,11},{10,... | collective-permute-start | bytes 442376 | tf_op jit(solution)/shard_map/planes0/across/ppermute | solution.py:74
  7.0 1.9 select_select_fusion
  14.5 2.8 %shard_map.279 = (bf16[192,768]{1,0:T(8,128)(2,1)}, bf16[96,768]{1,0:T(8,128)(2,1)}, bf16[192,768]{1,0:T(8,128)(2,1)}, bf16[96,768]{1,0:T(8,128)(2,1)}) custom-call(s32[9]{0:T(128)} %pad_add_fusion.spots_ref, bf16[768,768]{1,0:T(8,128)(2,1)} %refs_14_.1, bf16[768,768]{1,0:T(8,128)(2,1)} %refs_8_.3), custom_call_target="tpu_custom_call" | custom-call | tf_op jit(solution)/shard_map/pallas_call | solution.py:195
  19.0 1.6 collective-permute-done.refs_0_
  28.3 14.1 %collective-permute-done.6.refs_1_ = bf16[96,768]{1,0:T(8,128)(2,1)S(1)} collective-permute-done((bf16[96,768]{1,0:T(8,128)(2,1)S(1)}, bf16[96,768]{1,0:T(8,128)(2,1)S(1)}, u32[]{:S(2)}, u32[]{:S(2)}) %collective-permute-start.6) | collective-permute-done | bytes 147488 | tf_op jit(solution)/shard_map/round0/planes1/across/ppermute | solution.py:74
  46.5 1.8 collective-permute-start.8
  48.3 11.0 %collective-permute-done.9.refs_1_ = bf16[80,768]{1,0:T(8,128)(2,1)S(1)} collective-permute-done((bf16[80,768]{1,0:T(8,128)(2,1)S(1)}, bf16[80,768]{1,0:T(8,128)(2,1)S(1)}, u32[]{:S(2)}, u32[]{:S(2)}) %collective-permute-start.9) | collective-permute-done | bytes 122912 | tf_op jit(solution)/shard_map/round1/planes2/across/ppermute | solution.py:74
  59.4 3.5 %collective-permute-done.12.refs_1_.refs_10_ = bf16[6,96,768]{2,1,0:T(8,128)(2,1)} collective-permute-done((bf16[6,96,768]{2,1,0:T(8,128)(2,1)S(1)}, bf16[6,96,768]{2,1,0:T(8,128)(2,1)}, u32[]{:S(2)}, u32[]{:S(2)}) %collective-permute-start.12) | collective-permute-done | bytes 884768 | tf_op jit(solution)/shard_map/round1/near/ppermute | solution.py:70
  64.5 1.6 round2.3.refs_2_
  67.2 1.8 slice.51
  72.4 12.2 %round2.2 = (bf16[512,768]{1,0:T(8,128)(2,1)}, bf16[512,768]{1,0:T(8,128)(2,1)}, bf16[512,768]{1,0:T(8,128)(2,1)}, bf16[24,256,256]{2,1,0:T(8,128)(2,1)}, bf16[5...) custom-call(s32[9]{0:T(128)} %pad_add_fusion.spots_ref, s32[2]{0:T(128)} %dynamic_slice.13.len_ref, ...), custom_call_target="tpu_custom_call" | custom-call | flops 2818572288 | bytes 11010048 | tf_op jit(solution)/shard_map/round2/pallas_call | solution.py:439
  92.3 8.6 %round3.2 = (bf16[512,3072]{1,0:T(8,128)(2,1)}, bf16[512,3072]{1,0:T(8,128)(2,1)}) custom-call(s32[9]{0:T(128)} %pad_add_fusion.spots_ref, bf16[512,768]{1,0:T(8,128)(2,1)} %get-tuple-element.87.x_ref, f32[4,1,768]{2,1,0:T(1,128)} %bitcast.35, bf16[6,96,768]{2,1,0:T(8,128)(2,1)} %copy-done.2, bf16[6,96,768]{2,1,0:T(8,128)(2,1)} %collective-permute-done.12.refs_1_.refs_10_, ...), custom_call_target="tpu_custom_call" | custom-call | flops 2415919104 | bytes 11010048 | tf_op jit(solution)/shard_map/round3/pallas_call | solution.py:483
  102.1 4.6 %collective-permute-done.30.refs_10_.refs_3_ = bf16[3,96,768]{2,1,0:T(8,128)(2,1)} collective-permute-done((bf16[3,96,768]{2,1,0:T(8,128)(2,1)}, bf16[3,96,768]{2,1,0:T(8,128)(2,1)}, u32[]{:S(2)}, u32[]{:S(2)}) %collective-permute-start.30) | collective-permute-done | bytes 442400 | tf_op jit(solution)/shard_map/round3/near/ppermute | solution.py:70
  107.1 3.0 %collective-permute-done.31.refs_11_.refs_4_ = bf16[3,96,768]{2,1,0:T(8,128)(2,1)S(1)} collective-permute-done((bf16[3,96,768]{2,1,0:T(8,128)(2,1)}, bf16[3,96,768]{2,1,0:T(8,128)(2,1)S(1)}, u32[]{:S(2)}, u32[]{:S(2)}) %collective-permute-start.31) | collective-permute-done | bytes 442400 | tf_op jit(solution)/shard_map/round3/far/ppermute | solution.py:70
  110.3 1.6 collective-permute-done.34.refs_14_.refs_7_
  112.7 30.0 %shard_map.280 = (bf16[512,768]{1,0:T(8,128)(2,1)}, f32[512,768]{1,0:T(8,128)}, bf16[512,768]{1,0:T(8,128)(2,1)}, bf16[4,304,768]{2,1,0:T(8,128)(2,1)}, bf16[4,304,768]{2,1,0:T(8,128)(2,1)}) custom-call(s32[9]{0:T(128)} %pad_add_fusion.spots_ref, s32[2]{0:T(128)} %dynamic_slice.12.mask_ref, f32[4,768]{1,0:T(4,128)} %pad_maximum_fusion.2.norms_ref, ...), custom_call_target="tpu_custom_call" | custom-call | flops 11475615744 | bytes 17301504 | tf_op jit(solution)/shard_map/pallas_call | solution.py:761
  142.9 4.0 %collective-permute-done.35.come_hbm.refs_4_ = bf16[4,304,768]{2,1,0:T(8,128)(2,1)} collective-permute-done((bf16[4,304,768]{2,1,0:T(8,128)(2,1)}, bf16[4,304,768]{2,1,0:T(8,128)(2,1)}, u32[]{:S(2)}, u32[]{:S(2)}) %collective-permute-start.35) | collective-permute-done | bytes 1867808 | tf_op jit(solution)/shard_map/cores/ppermute | solution.py:70
  147.0 3.4 %shard_map.281 = (bf16[304,768]{1,0:T(8,128)(2,1)}, bf16[304,768]{1,0:T(8,128)(2,1)}, bf16[304,768]{1,0:T(8,128)(2,1)}) custom-call(s32[9]{0:T(128)} %pad_add_fusion.spots_ref, bf16[4,304,768]{2,1,0:T(8,128)(2,1)} %get-tuple-element.120.keep_hbm.refs_3_, bf16[4,304,768]{2,1,0:T(8,128)(2,1)} %collective-permute-done.35.come_hbm.refs_4_), custom_call_target="tpu_custom_call" | custom-call | tf_op jit(solution)/shard_map/pallas_call | solution.py:350
  153.9 11.8 %shard_map.282 = (f32[512,768]{1,0:T(8,128)}, bf16[512,768]{1,0:T(8,128)(2,1)}) custom-call(s32[9]{0:T(128)} %pad_add_fusion.spots_ref, bf16[512,768]{1,0:T(8,128)(2,1)} %get-tuple-element.107.g_ref, f32[512,1]{1,0:T(8,128)} %get-tuple-element.108.rstd_ref, f32[4,768]{1,0:T(4,128)} %pad_maximum_fusion.2.norms_ref, ...), custom_call_target="tpu_custom_call" | custom-call | flops 4831838208 | bytes 12582912 | tf_op jit(solution)/shard_map/pallas_call | solution.py:848
  165.8 9.2 %shard_map.283 = (bf16[256,768]{1,0:T(8,128)(2,1)}, bf16[256,768]{1,0:T(8,128)(2,1)}) custom-call(s32[9]{0:T(128)} %pad_add_fusion.spots_ref, bf16[512,768]{1,0:T(8,128)(2,1)} %get-tuple-element.112.refs_0_, f32[512,768]{1,0:T(8,128)} %get-tuple-element.111.refs_1_.refs_0_, bf16[6,96,768]{2,1,0:T(8,128)(2,1)} %copy-done.1, bf16[6,96,768]{2,1,0:T(8,128)(2,1)} %copy-done.6, ...), custom_call_target="tpu_custom_call" | custom-call | flops 2214592512 | bytes 8650752 | tf_op jit(solution)/shard_map/pallas_call | solution.py:956
  176.5 3.8 %shard_map.284 = (f32[80,768]{1,0:T(8,128)}, bf16[80,768]{1,0:T(8,128)(2,1)}, bf16[80,768]{1,0:T(8,128)(2,1)}, bf16[80,768]{1,0:T(8,128)(2,1)}) custom-call(s32[9]{0:T(128)} %pad_add_fusion.spots_ref, bf16[304,768]{1,0:T(8,128)(2,1)} %copy-done.11, bf16[304,768]{1,0:T(8,128)(2,1)} %collective-permute-done.37.refs_1_, bf16[304,768]{1,0:T(8,128)(2,1)} %copy-done.10, ...), custom_call_target="tpu_custom_call" | custom-call | tf_op jit(solution)/shard_map/pallas_call | solution.py:363
  182.5 2.4 %collective-permute-start.41 = (bf16[80,768]{1,0:T(8,128)(2,1)}, bf16[80,768]{1,0:T(8,128)(2,1)S(1)}, u32[]{:S(2)}, u32[]{:S(2)}) collective-permute-start(bf16[80,768]{1,0:T(8,128)(2,1)} %get-tuple-element.126), channel_id=1, source_target_pairs={{0,3},{1,0},{2,1},{3,2},{4,7},{5,4},{6,5},{7,6},{8,11},{9,8},{10,9... | collective-permute-start | bytes 368648 | tf_op jit(solution)/shard_map/stack2/ppermute | solution.py:74
  184.9 8.3 %shard_map.285 = bf16[512,768]{1,0:T(8,128)(2,1)} custom-call(s32[9]{0:T(128)} %pad_add_fusion.spots_ref, f32[512,768]{1,0:T(8,128)} %get-tuple-element.111.refs_1_.refs_0_, bf16[256,768]{1,0:T(8,128)(2,1)} %get-tuple-element.122.refs_1_, bf16[256,768]{1,0:T(8,128)(2,1)} %get-tuple-element.123.refs_2_, bf16[6,96,768]{2,1,0:T(8,128)(2,1)} %copy-done.1, ...), custom_call_target="tpu_custom_call" | custom-call | flops 1610612736 | bytes 6684672 | tf_op jit(solution)/shard_map/pallas_call | solution.py:973
  (154 shorter events, 44.1 us)
Async XLA Ops:
  3.0 16.0 %collective-permute-start.1 = (bf16[96,768]{1,0:T(8,128)(2,1)}, bf16[96,768]{1,0:T(8,128)(2,1)S(1)}, u32[]{:S(2)}, u32[]{:S(2)}) collective-permute-start(bf16[96,768]{1,0:T(8,128)(2,1)} %fusion.5), channel_id=1, source_target_pairs={{0,2},{1,3},{2,0},{3,1},{4,6},{5,7},{6,4},{7,5},{8,10},{9,11},{10,... | collective-permute-start | bytes 442376 | tf_op jit(solution)/shard_map/planes0/across/ppermute | solution.py:74
  8.9 11.7 %collective-permute-start = (bf16[192,768]{1,0:T(8,128)(2,1)}, bf16[192,768]{1,0:T(8,128)(2,1)}, u32[]{:S(2)}, u32[]{:S(2)}) collective-permute-start(bf16[192,768]{1,0:T(8,128)(2,1)} %select_select_fusion), channel_id=1, source_target_pairs={{0,3},{1,0},{2,1},{3,2},{4,5},{5,6},{6,7},{7,4},{8,11},{9,8},{10,9... | collective-permute-start | bytes 884744 | tf_op jit(solution)/shard_map/planes0/beside/ppermute | solution.py:79
  24.6 17.8 %collective-permute-start.7 = (bf16[6,96,768]{2,1,0:T(8,128)(2,1)S(1)}, bf16[6,96,768]{2,1,0:T(8,128)(2,1)S(1)}, u32[]{:S(2)}, u32[]{:S(2)}) collective-permute-start(bf16[6,96,768]{2,1,0:T(8,128)(2,1)S(1)} %round0.1.refs_0_.refs_2_.refs_3_), channel_id=1, source_target_pairs={{0,8},{4,20},{8,0},{12,28},{16,24},{20,4},{24,16},{28,12},{1,9},{5... | collective-permute-start | bytes 2654216 | tf_op jit(solution)/shard_map/round0/near/ppermute | solution.py:70
  26.2 16.2 %collective-permute-start.5 = (bf16[192,768]{1,0:T(8,128)(2,1)S(1)}, bf16[192,768]{1,0:T(8,128)(2,1)S(1)}, u32[]{:S(2)}, u32[]{:S(2)}) collective-permute-start(bf16[192,768]{1,0:T(8,128)(2,1)S(1)} %copy-done.24), channel_id=1, source_target_pairs={{0,3},{1,0},{2,1},{3,2},{4,5},{5,6},{6,7},{7,4},{8,11},{9,8},{10,9... | collective-permute-start | bytes 884744 | tf_op jit(solution)/shard_map/round0/planes1/beside/ppermute | solution.py:79
  27.1 15.3 %collective-permute-start.6 = (bf16[96,768]{1,0:T(8,128)(2,1)S(1)}, bf16[96,768]{1,0:T(8,128)(2,1)S(1)}, u32[]{:S(2)}, u32[]{:S(2)}) collective-permute-start(bf16[96,768]{1,0:T(8,128)(2,1)S(1)} %copy-done.25), channel_id=1, source_target_pairs={{0,2},{1,3},{2,0},{3,1},{4,6},{5,7},{6,4},{7,5},{8,10},{9,11},{10,... | collective-permute-start | bytes 442376 | tf_op jit(solution)/shard_map/round0/planes1/across/ppermute | solution.py:74
  43.0 16.4 %collective-permute-start.14 = (bf16[6,96,768]{2,1,0:T(8,128)(2,1)S(1)}, bf16[6,96,768]{2,1,0:T(8,128)(2,1)S(1)}, u32[]{:S(2)}, u32[]{:S(2)}) collective-permute-start(bf16[6,96,768]{2,1,0:T(8,128)(2,1)S(1)} %collective-permute-done.7.refs_1_.refs_3_.refs_4_), channel_id=1, source_target_pairs={{0,4},{4,0},{8,12},{12,8},{16,20},{20,16},{24,28},{28,24},{1,5},{5... | collective-permute-start | bytes 2654216 | tf_op jit(solution)/shard_map/round1/swap/ppermute | solution.py:70
  44.9 18.0 %collective-permute-start.12 = (bf16[6,96,768]{2,1,0:T(8,128)(2,1)S(1)}, bf16[6,96,768]{2,1,0:T(8,128)(2,1)}, u32[]{:S(2)}, u32[]{:S(2)}) collective-permute-start(bf16[6,96,768]{2,1,0:T(8,128)(2,1)S(1)} %round1.1.refs_0_.refs_9_), channel_id=1, source_target_pairs={{0,8},{4,20},{8,0},{12,28},{16,24},{20,4},{24,16},{28,12},{1,9},{5... | collective-permute-start | bytes 2654216 | tf_op jit(solution)/shard_map/round1/near/ppermute | solution.py:70
  45.6 13.8 %collective-permute-start.13 = (bf16[3,96,768]{2,1,0:T(8,128)(2,1)S(1)}, bf16[3,96,768]{2,1,0:T(8,128)(2,1)S(1)}, u32[]{:S(2)}, u32[]{:S(2)}) collective-permute-start(bf16[3,96,768]{2,1,0:T(8,128)(2,1)S(1)} %slice.50), channel_id=1, source_target_pairs={{0,20},{4,8},{8,28},{12,0},{16,4},{20,24},{24,12},{28,16},{1,21},{... | collective-permute-start | bytes 1327112 | tf_op jit(solution)/shard_map/round1/far/ppermute | solution.py:70
  46.5 12.8 %collective-permute-start.8 = (bf16[160,768]{1,0:T(8,128)(2,1)S(1)}, bf16[160,768]{1,0:T(8,128)(2,1)S(1)}, u32[]{:S(2)}, u32[]{:S(2)}) collective-permute-start(bf16[160,768]{1,0:T(8,128)(2,1)S(1)} %pad_maximum_fusion), channel_id=1, source_target_pairs={{0,3},{1,0},{2,1},{3,2},{4,5},{5,6},{6,7},{7,4},{8,11},{9,8},{10,9... | collective-permute-start | bytes 737288 | tf_op jit(solution)/shard_map/round1/planes2/beside/ppermute | solution.py:79
  48.3 11.0 %collective-permute-start.9 = (bf16[80,768]{1,0:T(8,128)(2,1)S(1)}, bf16[80,768]{1,0:T(8,128)(2,1)S(1)}, u32[]{:S(2)}, u32[]{:S(2)}) collective-permute-start(bf16[80,768]{1,0:T(8,128)(2,1)S(1)} %pad_maximum_fusion.1.refs_4_), channel_id=1, source_target_pairs={{0,2},{1,3},{2,0},{3,1},{4,6},{5,7},{6,4},{7,5},{8,10},{9,11},{10,... | collective-permute-start | bytes 368648 | tf_op jit(solution)/shard_map/round1/planes2/across/ppermute | solution.py:74
  66.1 19.2 %collective-permute-start.20 = (bf16[8,80,768]{2,1,0:T(8,128)(2,1)}, bf16[8,80,768]{2,1,0:T(8,128)(2,1)}, u32[]{:S(2)}, u32[]{:S(2)}) collective-permute-start(bf16[8,80,768]{2,1,0:T(8,128)(2,1)} %round2.3.refs_2_), channel_id=1, source_target_pairs={{0,8},{4,20},{8,0},{12,28},{16,24},{20,4},{24,16},{28,12},{1,9},{5... | collective-permute-start | bytes 2949128 | tf_op jit(solution)/shard_map/round2/near/ppermute | solution.py:70
  66.7 18.2 %collective-permute-start.22 = (bf16[6,96,768]{2,1,0:T(8,128)(2,1)}, bf16[6,96,768]{2,1,0:T(8,128)(2,1)}, u32[]{:S(2)}, u32[]{:S(2)}) collective-permute-start(bf16[6,96,768]{2,1,0:T(8,128)(2,1)} %collective-permute-done.12.refs_1_.refs_10_), channel_id=1, source_target_pairs={{0,4},{4,0},{8,12},{12,8},{16,20},{20,16},{24,28},{28,24},{1,5},{5... | collective-permute-start | bytes 2654216 | tf_op jit(solution)/shard_map/round2/swap/ppermute | solution.py:70
  69.0 15.9 %collective-permute-start.21 = (bf16[3,96,768]{2,1,0:T(8,128)(2,1)}, bf16[3,96,768]{2,1,0:T(8,128)(2,1)}, u32[]{:S(2)}, u32[]{:S(2)}) collective-permute-start(bf16[3,96,768]{2,1,0:T(8,128)(2,1)} %slice.51), channel_id=1, source_target_pairs={{0,20},{4,8},{8,28},{12,0},{16,4},{20,24},{24,12},{28,16},{1,21},{... | collective-permute-start | bytes 1327112 | tf_op jit(solution)/shard_map/round2/far/ppermute | solution.py:70
  70.1 14.9 %collective-permute-start.16 = (bf16[192,768]{1,0:T(8,128)(2,1)}, bf16[192,768]{1,0:T(8,128)(2,1)S(1)}, u32[]{:S(2)}, u32[]{:S(2)}) collective-permute-start(bf16[192,768]{1,0:T(8,128)(2,1)} %get-tuple-element.90), channel_id=1, source_target_pairs={{0,3},{1,0},{2,1},{3,2},{4,5},{5,6},{6,7},{7,4},{8,11},{9,8},{10,9... | collective-permute-start | bytes 884744 | tf_op jit(solution)/shard_map/round2/planes3/beside/ppermute | solution.py:79
  71.6 13.3 %collective-permute-start.17 = (bf16[96,768]{1,0:T(8,128)(2,1)}, bf16[96,768]{1,0:T(8,128)(2,1)S(1)}, u32[]{:S(2)}, u32[]{:S(2)}) collective-permute-start(bf16[96,768]{1,0:T(8,128)(2,1)} %get-tuple-element.91), channel_id=1, source_target_pairs={{0,2},{1,3},{2,0},{3,1},{4,6},{5,7},{6,4},{7,5},{8,10},{9,11},{10,... | collective-permute-start | bytes 442376 | tf_op jit(solution)/shard_map/round2/planes3/across/ppermute | solution.py:74
  85.3 15.7 %collective-permute-start.25 = (bf16[8,80,768]{2,1,0:T(8,128)(2,1)}, bf16[8,80,768]{2,1,0:T(8,128)(2,1)}, u32[]{:S(2)}, u32[]{:S(2)}) collective-permute-start(bf16[8,80,768]{2,1,0:T(8,128)(2,1)} %collective-permute-done.20.refs_3_), channel_id=1, source_target_pairs={{0,4},{4,0},{8,12},{12,8},{16,20},{20,16},{24,28},{28,24},{1,5},{5... | collective-permute-start | bytes 2949128 | tf_op jit(solution)/shard_map/round3/swap/ppermute | solution.py:70
  87.4 13.6 %collective-permute-start.24 = (bf16[4,80,768]{2,1,0:T(8,128)(2,1)S(1)}, bf16[4,80,768]{2,1,0:T(8,128)(2,1)}, u32[]{:S(2)}, u32[]{:S(2)}) collective-permute-start(bf16[4,80,768]{2,1,0:T(8,128)(2,1)S(1)} %slice.52), channel_id=1, source_target_pairs={{0,20},{4,8},{8,28},{12,0},{16,4},{20,24},{24,12},{28,16},{1,21},{... | collective-permute-start | bytes 1474568 | tf_op jit(solution)/shard_map/round3/far/ppermute | solution.py:70
  91.2 15.4 %collective-permute-start.30 = (bf16[3,96,768]{2,1,0:T(8,128)(2,1)}, bf16[3,96,768]{2,1,0:T(8,128)(2,1)}, u32[]{:S(2)}, u32[]{:S(2)}) collective-permute-start(bf16[3,96,768]{2,1,0:T(8,128)(2,1)} %get-tuple-element.100.refs_8_.refs_1_), channel_id=1, source_target_pairs={{0,8},{4,20},{8,0},{12,28},{16,24},{20,4},{24,16},{28,12},{1,9},{5... | collective-permute-start | bytes 1327112 | tf_op jit(solution)/shard_map/round3/near/ppermute | solution.py:70
  150.3 24.6 %collective-permute-start.38 = (bf16[304,768]{1,0:T(8,128)(2,1)}, bf16[304,768]{1,0:T(8,128)(2,1)S(1)}, u32[]{:S(2)}, u32[]{:S(2)}) collective-permute-start(bf16[304,768]{1,0:T(8,128)(2,1)} %get-tuple-element.106), channel_id=1, source_target_pairs={{0,24},{4,28},{8,16},{12,20},{16,8},{20,12},{24,0},{28,4},{1,25},{... | collective-permute-start | bytes 1400840 | tf_op jit(solution)/shard_map/far/ppermute | solution.py:70
  151.8 23.1 %collective-permute-start.36 = (bf16[304,768]{1,0:T(8,128)(2,1)}, bf16[304,768]{1,0:T(8,128)(2,1)S(1)}, u32[]{:S(2)}, u32[]{:S(2)}) collective-permute-start(bf16[304,768]{1,0:T(8,128)(2,1)} %get-tuple-element.118), channel_id=1, source_target_pairs={{0,8},{4,12},{8,0},{12,4},{16,24},{20,28},{24,16},{28,20},{1,9},{5... | collective-permute-start | bytes 1400840 | tf_op jit(solution)/shard_map/x/ppermute | solution.py:70
  152.9 22.1 %collective-permute-start.37 = (bf16[304,768]{1,0:T(8,128)(2,1)}, bf16[304,768]{1,0:T(8,128)(2,1)}, u32[]{:S(2)}, u32[]{:S(2)}) collective-permute-start(bf16[304,768]{1,0:T(8,128)(2,1)} %get-tuple-element.119), channel_id=1, source_target_pairs={{0,16},{4,20},{8,24},{12,28},{16,0},{20,4},{24,8},{28,12},{1,17},{... | collective-permute-start | bytes 1400840 | tf_op jit(solution)/shard_map/y/ppermute | solution.py:70
  180.3 13.0 %collective-permute-start.39 = (bf16[80,768]{1,0:T(8,128)(2,1)}, bf16[80,768]{1,0:T(8,128)(2,1)S(1)}, u32[]{:S(2)}, u32[]{:S(2)}) collective-permute-start(bf16[80,768]{1,0:T(8,128)(2,1)} %get-tuple-element.124), channel_id=1, source_target_pairs={{0,1},{1,2},{2,3},{3,0},{4,5},{5,6},{6,7},{7,4},{8,9},{9,10},{10,1... | collective-permute-start | bytes 368648 | tf_op jit(solution)/shard_map/stack0/ppermute | solution.py:74
  181.5 11.7 %collective-permute-start.40 = (bf16[80,768]{1,0:T(8,128)(2,1)}, bf16[80,768]{1,0:T(8,128)(2,1)S(1)}, u32[]{:S(2)}, u32[]{:S(2)}) collective-permute-start(bf16[80,768]{1,0:T(8,128)(2,1)} %get-tuple-element.125), channel_id=1, source_target_pairs={{0,2},{1,3},{2,0},{3,1},{4,6},{5,7},{6,4},{7,5},{8,10},{9,11},{10,... | collective-permute-start | bytes 368648 | tf_op jit(solution)/shard_map/stack1/ppermute | solution.py:74
  182.5 10.8 %collective-permute-start.41 = (bf16[80,768]{1,0:T(8,128)(2,1)}, bf16[80,768]{1,0:T(8,128)(2,1)S(1)}, u32[]{:S(2)}, u32[]{:S(2)}) collective-permute-start(bf16[80,768]{1,0:T(8,128)(2,1)} %get-tuple-element.126), channel_id=1, source_target_pairs={{0,3},{1,0},{2,1},{3,2},{4,7},{5,4},{6,5},{7,6},{8,11},{9,8},{10,9... | collective-permute-start | bytes 368648 | tf_op jit(solution)/shard_map/stack2/ppermute | solution.py:74
  (46 other events, 330.3 us)
